TPU v7x, 32 devices: a whole 2x2x4 slice. The times are simulated.
32 devices in a mesh: member: 2 (over core), slab: 16 (over z, y, x).
Axes of the slice: x: 2, y: 2, z: 4, core: 2. Of those that a mesh axis runs over, the one named last changes fastest.
Arguments:
- base_field: bfloat16 [32, 512, 2, 512], P(None, 'slab'), may hold values from -6 to 6
- forcing: bfloat16 [512, 2, 512], P('slab'), may hold values from -6 to 6
- load: float32 [32], replicated, may hold values from 0.25 to 1.75
- amplitudes: float32 [16], replicated, may hold values from 0.25 to 2
- amp_index: int32 [2], P('member'), may hold values from 0 to 15
- mode_count: int32 [2], P('member'), may hold values from 32 to 64, as said below
- point_weight: bfloat16 [32, 32], replicated, may hold values from -1 to 1
- point_bias: float32 [32], replicated, may hold values from -3 to 3
- spectral_weight: bfloat16 [64, 64, 2, 32, 32], P('slab'), may hold values from -6 to 6
Outputs:
- dependence: bfloat16 [32, 512, 2, 512], P('member', 'slab')
Inputs may be any that keep to these rules, and one draw needn't show every extreme that they name: `mode_count`: each member keeps the second-dimension modes below its count; some member keeps all 64.
All inputs are finite; a program needn't handle non-finite values.
Results may differ from a plain program's by a relative error of at most 0.015.
Values may be sent and summed in bfloat16 or wider, within the bound.
No kernel may reach another device: no remote copies, remote signals or barrier semaphores. Data moves between devices by JAX's collectives and lax.ppermute only.
A program may use at most 64 MiB of HBM per device.

v0:
```python
import math

import jax
import jax.numpy as jnp
from jax import lax
from jax.sharding import PartitionSpec as P

TWO_PI = 2.0 * math.pi


def phases(frequency, positions, length):
    product = frequency[:, None] * positions[None, :] % length
    angles = product.astype(jnp.float32) * (TWO_PI / length)
    return (jnp.cos(angles), jnp.sin(angles))


def forward_x(pencil, cos_table, sin_table):
    row_total = pencil.shape[0]
    modes = cos_table.shape[0]
    with_cos = jnp.einsum(
        "kxf,mx->kmf", pencil, cos_table, preferred_element_type=jnp.float32
    ).reshape(row_total, modes, 2, -1)
    with_sin = jnp.einsum(
        "kxf,mx->kmf", pencil, sin_table, preferred_element_type=jnp.float32
    ).reshape(row_total, modes, 2, -1)
    real_part = with_cos[:, :, 0] + with_sin[:, :, 1]
    imag_part = with_cos[:, :, 1] - with_sin[:, :, 0]
    return jnp.stack([real_part, imag_part], axis=2).reshape(row_total, modes, -1)


def inverse_x(spectra, cos_table, sin_table):
    row_total = spectra.shape[0]
    points = cos_table.shape[1]
    with_cos = jnp.einsum(
        "kmf,mx->kxf", spectra, cos_table, preferred_element_type=jnp.float32
    ).reshape(row_total, points, 2, -1)
    with_sin = jnp.einsum(
        "kmf,mx->kxf", spectra, sin_table, preferred_element_type=jnp.float32
    ).reshape(row_total, points, 2, -1)
    real_part = with_cos[:, :, 0] - with_sin[:, :, 1]
    imag_part = with_cos[:, :, 1] + with_sin[:, :, 0]
    return jnp.stack([real_part, imag_part], axis=2).reshape(row_total, points, -1)


def mixing(weights, values):
    return jnp.einsum("kmoi,kmiz->kmoz", weights, values, preferred_element_type=jnp.float32)


def local(
    base_field,
    forcing,
    load,
    amplitudes,
    amp_index,
    mode_count,
    point_weight,
    point_bias,
    spectral_weight,
):
    channels, slab_rows, plane_count, length_y = base_field.shape
    slab_count = lax.axis_size("slab")
    local_modes = spectral_weight.shape[0]
    modes_y = local_modes * slab_count
    modes_x = spectral_weight.shape[1]
    length_x = slab_rows * slab_count
    packed_width = 2 * channels * plane_count
    slab_index = lax.axis_index("slab")
    level_ids = jnp.arange(amplitudes.shape[0], dtype=jnp.int32)
    amplitude = jnp.sum(jnp.where(level_ids == amp_index[0], amplitudes, 0.0))
    driven = base_field.astype(jnp.float32) + amplitude * load[:, None, None, None] * forcing[
        None
    ].astype(jnp.float32)
    field_now = (2.0 * jnp.tanh(0.5 * driven)).astype(jnp.bfloat16)
    y_cos, y_sin = phases(
        jnp.arange(modes_y, dtype=jnp.int32), jnp.arange(length_y, dtype=jnp.int32), length_y
    )
    y_real = jnp.einsum(
        "cxzy,ky->kxcz", field_now, y_cos.astype(jnp.bfloat16), preferred_element_type=jnp.float32
    )
    y_imag = -jnp.einsum(
        "cxzy,ky->kxcz", field_now, y_sin.astype(jnp.bfloat16), preferred_element_type=jnp.float32
    )
    packed = (
        jnp.stack([y_real, y_imag], axis=2)
        .astype(jnp.bfloat16)
        .reshape(modes_y, slab_rows, packed_width)
    )
    frequency_x = jnp.concatenate(
        [
            jnp.arange(modes_x // 2, dtype=jnp.int32),
            jnp.arange(length_x - modes_x // 2, length_x, dtype=jnp.int32),
        ]
    )
    full_cos, full_sin = phases(frequency_x, jnp.arange(length_x, dtype=jnp.int32), length_x)
    full_cos = full_cos.astype(jnp.bfloat16)
    full_sin = full_sin.astype(jnp.bfloat16)
    pencil = lax.all_to_all(packed, "slab", split_axis=0, concat_axis=1, tiled=True)
    spectrum = forward_x(pencil, full_cos, full_sin)
    spectrum = spectrum.astype(jnp.bfloat16).reshape(local_modes, modes_x, 2, channels, plane_count)
    weight_real = spectral_weight[:, :, 0]
    weight_imag = spectral_weight[:, :, 1]
    spec_real = spectrum[:, :, 0]
    spec_imag = spectrum[:, :, 1]
    mix_real = mixing(weight_real, spec_real) - mixing(weight_imag, spec_imag)
    mix_imag = mixing(weight_real, spec_imag) + mixing(weight_imag, spec_real)
    global_modes = slab_index * local_modes + jnp.arange(local_modes, dtype=jnp.int32)
    keep = (global_modes < mode_count[0]).astype(jnp.float32)[:, None, None, None, None]
    mixed = (
        (jnp.stack([mix_real, mix_imag], axis=2) * keep)
        .astype(jnp.bfloat16)
        .reshape(local_modes, modes_x, packed_width)
    )
    back = inverse_x(mixed, full_cos, full_sin).astype(jnp.bfloat16)
    returned = lax.all_to_all(back, "slab", split_axis=1, concat_axis=0, tiled=True)
    returned = returned.reshape(modes_y, slab_rows, 2, channels, plane_count)
    weights_y = jnp.where(jnp.arange(modes_y) == 0, 1.0, 2.0).astype(jnp.float32) / (
        length_x * length_y
    )
    back_cos = (weights_y[:, None] * y_cos).astype(jnp.bfloat16)
    back_sin = (weights_y[:, None] * y_sin).astype(jnp.bfloat16)
    spectral = jnp.einsum(
        "kxcz,ky->cxzy", returned[:, :, 0], back_cos, preferred_element_type=jnp.float32
    )
    spectral = spectral - jnp.einsum(
        "kxcz,ky->cxzy", returned[:, :, 1], back_sin, preferred_element_type=jnp.float32
    )
    pointwise = (
        jnp.einsum("oc,cxzy->oxzy", point_weight, field_now, preferred_element_type=jnp.float32)
        + point_bias[:, None, None, None]
    )
    layer = jax.nn.gelu(pointwise + spectral, approximate=True).astype(jnp.bfloat16)
    layer = lax.optimization_barrier(layer).astype(jnp.float32)
    total = lax.psum_scatter(
        layer.astype(jnp.bfloat16), "member", scatter_dimension=0, tiled=True
    ).astype(jnp.float32)
    return (total / lax.axis_size("member")).astype(jnp.bfloat16)


def solution(mesh):
    in_specs = (
        P(None, "slab", None, None),
        P("slab", None, None),
        P(),
        P(),
        P("member"),
        P("member"),
        P(),
        P(),
        P("slab", None, None, None, None),
    )
    out_specs = P("member", "slab", None, None)
    return jax.shard_map(local, mesh=mesh, in_specs=in_specs, out_specs=out_specs, check_vma=False)
```

profile of v0, /device:TPU:0, one launch (start us, length us, event | category | flops | bytes accessed | tf_op | source)
XLA Modules:
  0.0 110.3 jit_solution(3655331555602271941)
XLA Ops:
  6.5 0.0 copy-start
  7.2 0.9 convert_element_type.77
  8.1 1.3 %fusion.96 = f32[]{:T(128)} fusion(f32[16]{0:T(128)} %param.12, s32[]{:T(128)} %bitcast.120), kind=kLoop, calls=%fused_computation.96 | loop fusion | flops 47 | bytes 72 | tf_op jit(solution)/shard_map/reduce_sum | solution.py:69
  9.4 1.3 %broadcast_multiply_fusion = f32[32]{0:T(128)S(1)} fusion(f32[32]{0:T(128)} %param.11, f32[]{:T(128)} %fusion.96), kind=kLoop, calls=%fused_computation.100 | loop fusion | flops 32 | bytes 260 | tf_op jit(solution)/shard_map/mul | solution.py:70
  10.7 4.3 %multiply_convert_fusion = bf16[32,32,2,512]{3,0,2,1:T(8,128)(2,1)S(1)} fusion(bf16[32,32,2,512]{3,2,1,0:T(2,128)(2,1)} %param.9, f32[32,2,512]{2,1,0:T(2,128)S(1)} %convert_element_type.77, f32[32]{0:T(128)S(1)} %broadcast_multiply_fusion), kind=kLoop, calls=%fused_computation.10 | loop fusion | flops 6291456 | bytes 4325504 | tf_op jit(solution)/shard_map/convert_element_type | solution.py:73
  15.0 0.0 copy-start.2
  15.0 2.9 %fusion.32 = bf16[64,32,1,32,2]{0,1,4,3,2:T(8,128)(2,1)S(1)} fusion(bf16[32,32,2,512]{3,0,2,1:T(8,128)(2,1)S(1)} %multiply_convert_fusion), kind=kOutput, calls=%fused_computation.28 | convolution fusion | flops 134971392 | bytes 2359296 | tf_op jit(solution)/shard_map/cxzy,ky->kxcz/dot_general | solution.py:80
  17.9 2.9 %fusion.29 = bf16[64,32,1,32,2]{0,1,4,3,2:T(8,128)(2,1)S(1)} fusion(bf16[32,32,2,512]{3,0,2,1:T(8,128)(2,1)S(1)} %multiply_convert_fusion), kind=kOutput, calls=%fused_computation.27 | convolution fusion | flops 134840320 | bytes 2359296 | tf_op jit(solution)/shard_map/cxzy,ky->kxcz/dot_general | solution.py:77
  20.8 0.0 copy-done.2
  20.8 0.2 pad_maximum_fusion
  21.1 2.3 %copy.84 = bf16[64,32,128]{2,1,0:T(8,128)(2,1)} copy(bf16[64,32,128]{0,1,2:T(8,128)(2,1)S(1)} %bitcast.125) | data formatting | bytes 1048576 | tf_op jit(solution)/shard_map/convert_element_type | solution.py:85
  23.4 8.4 %all-to-all-start = ((bf16[64,32,128]{2,1,0:T(8,128)(2,1)}), bf16[64,32,128]{2,1,0:T(8,128)(2,1)}, u32[]{:S(2)}, u32[]{:S(2)}) async-start(bf16[64,32,128]{2,1,0:T(8,128)(2,1)} %copy.84), calls=%async_computation | async-start | bytes 1048576 | tf_op jit(solution)/shard_map/all_to_all | solution.py:97
  32.4 2.0 %fusion.131 = (bf16[4,64,1,32,32]{1,4,3,2,0:T(8,128)(2,1)S(1)}, bf16[4,64,1,32,32]{1,4,3,2,0:T(8,128)(2,1)S(1)}) fusion(bf16[4,64,2,32,32]{1,4,3,2,0:T(8,128)(2,1)} %param.17), kind=kLoop, calls=%fused_computation.134 | loop fusion | bytes 2097152 | tf_op jit(solution)/shard_map/slice | solution.py:100
  34.5 3.8 %copy.110 = bf16[4,64,1,32,32]{4,3,1,0,2:T(8,128)(2,1)} copy(bf16[4,64,1,32,32]{1,4,3,2,0:T(8,128)(2,1)S(1)} %get-tuple-element.9) | data formatting | bytes 1048576
  38.2 3.0 %copy.112 = bf16[4,64,1,32,32]{4,3,1,0,2:T(8,128)(2,1)S(1)} copy(bf16[4,64,1,32,32]{1,4,3,2,0:T(8,128)(2,1)S(1)} %get-tuple-element.10) | data formatting | bytes 1048576
  41.3 0.1 pad_add_fusion
  41.4 5.6 %all-to-all-done = bf16[64,32,128]{2,1,0:T(8,128)(2,1)} async-done(((bf16[64,32,128]{2,1,0:T(8,128)(2,1)}), bf16[64,32,128]{2,1,0:T(8,128)(2,1)}, u32[]{:S(2)}, u32[]{:S(2)}) %all-to-all-start) | async-done | bytes 524320 | tf_op jit(solution)/shard_map/all_to_all | solution.py:97
  47.0 1.1 copy.85
  48.0 0.7 convolution_bitcast_fusion
  48.7 0.7 convolution_bitcast_fusion.1
  49.4 0.1 copy.107
  49.5 0.1 copy.108
  49.8 0.1 fusion.132
  49.9 0.1 copy.111
  50.0 0.1 copy.109
  50.1 0.0 copy-start.1
  50.1 1.2 %fusion.8 = f32[4,64,2,32]{3,2,1,0:T(2,128)S(1)} fusion(bf16[4,64,1,32,32]{4,3,1,0,2:T(8,128)(2,1)S(1)} %copy.112, bf16[4,64,1,32,2]{3,4,1,0,2:T(2,128)(2,1)S(1)} %copy.109), kind=kOutput, calls=%fused_computation.11 | convolution fusion | flops 1048576 | bytes 622592 | tf_op jit(solution)/shard_map/kmoi,kmiz->kmoz/dot_general | solution.py:46
  51.3 1.2 %fusion.10 = f32[4,64,2,32]{3,2,1,0:T(2,128)S(1)} fusion(bf16[4,64,1,32,32]{4,3,1,0,2:T(8,128)(2,1)S(1)} %copy.112, bf16[4,64,1,32,2]{3,4,1,0,2:T(2,128)(2,1)S(1)} %copy.111), kind=kOutput, calls=%fused_computation.13 | convolution fusion | flops 1048576 | bytes 622592 | tf_op jit(solution)/shard_map/kmoi,kmiz->kmoz/dot_general | solution.py:46
  52.5 0.0 copy-done.1
  52.5 1.2 %fusion.44 = f32[4,64,1,32,2]{3,4,1,0,2:T(2,128)S(1)} fusion(f32[4,64,2,32]{3,2,1,0:T(2,128)S(1)} %fusion.8, bf16[4,64,1,32,32]{4,3,1,0,2:T(8,128)(2,1)S(1)} %copy-done.1, bf16[4,64,1,32,2]{3,4,1,0,2:T(2,128)(2,1)S(1)} %copy.111), kind=kOutput, calls=%fused_computation.32 | convolution fusion | flops 1064960 | bytes 688128 | tf_op jit(solution)/shard_map/kmoi,kmiz->kmoz/dot_general | solution.py:46
  53.7 1.2 %fusion.38 = f32[4,64,1,32,2]{3,4,1,0,2:T(2,128)S(1)} fusion(f32[4,64,2,32]{3,2,1,0:T(2,128)S(1)} %fusion.10, bf16[4,64,1,32,32]{4,3,1,0,2:T(8,128)(2,1)S(1)} %copy-done.1, bf16[4,64,1,32,2]{3,4,1,0,2:T(2,128)(2,1)S(1)} %copy.109), kind=kOutput, calls=%fused_computation.30 | convolution fusion | flops 1064960 | bytes 688128 | tf_op jit(solution)/shard_map/kmoi,kmiz->kmoz/dot_general | solution.py:46
  54.9 0.3 pad_maximum_fusion.1
  55.2 0.2 copy.94
  55.4 0.1 copy.95
  55.5 0.8 fusion.87
  56.4 0.8 fusion.90
  57.2 0.3 fusion.48
  57.5 0.1 pad_maximum_fusion.2
  57.5 1.1 copy.96
  58.6 3.9 %all-to-all-start.1 = ((bf16[4,512,128]{2,0,1:T(4,128)(2,1)}), bf16[4,512,128]{2,0,1:T(4,128)(2,1)S(1)}, u32[]{:S(2)}, u32[]{:S(2)}) async-start(bf16[4,512,128]{2,0,1:T(4,128)(2,1)} %copy.96), calls=%async_computation.1 | async-start | bytes 1048576 | tf_op jit(solution)/shard_map/all_to_all | solution.py:114
  62.5 0.3 reduce-scatter.2.cloned.1.call-start
  62.8 14.1 %all-to-all-done.1 = bf16[4,512,128]{2,0,1:T(4,128)(2,1)S(1)} async-done(((bf16[4,512,128]{2,0,1:T(4,128)(2,1)}), bf16[4,512,128]{2,0,1:T(4,128)(2,1)S(1)}, u32[]{:S(2)}, u32[]{:S(2)}) %all-to-all-start.1) | async-done | bytes 524320 | tf_op jit(solution)/shard_map/all_to_all | solution.py:114
  76.9 0.1 copy.97
  77.0 1.0 copy.98
  78.0 2.9 %fusion.130 = (bf16[64,32,1,32,2]{1,4,3,2,0:T(2,128)(2,1)}, bf16[64,32,1,32,2]{1,4,3,2,0:T(2,128)(2,1)S(1)}) fusion(bf16[64,32,2,32,2]{1,4,3,2,0:T(2,128)(2,1)S(1)} %bitcast.122), kind=kLoop, calls=%fused_computation.133 | loop fusion | bytes 1048576 | tf_op jit(solution)/shard_map/slice | solution.py:125
  80.9 3.0 %copy.114 = bf16[64,32,1,32,2]{0,3,4,1,2:T(8,128)(2,1)S(1)} copy(bf16[64,32,1,32,2]{1,4,3,2,0:T(2,128)(2,1)} %get-tuple-element.5) | data formatting | bytes 524288
  83.9 1.5 %copy.113 = bf16[64,32,1,32,2]{0,3,4,1,2:T(8,128)(2,1)S(1)} copy(bf16[64,32,1,32,2]{1,4,3,2,0:T(2,128)(2,1)S(1)} %get-tuple-element.6) | data formatting | bytes 524288
  85.4 1.2 %fusion.51 = f32[512,32,32,2]{0,2,3,1:T(8,128)S(1)} fusion(bf16[64,32,1,32,2]{0,3,4,1,2:T(8,128)(2,1)S(1)} %copy.113, f32[64]{0:T(128)S(1)} %fusion.97), kind=kOutput, calls=%fused_computation.44 | convolution fusion | flops 134742016 | bytes 4456704 | tf_op jit(solution)/shard_map/kxcz,ky->cxzy/dot_general | solution.py:121
  86.5 0.0 copy-start.3
  86.5 0.0 copy-start.4
  86.5 1.2 %fusion.49 = f32[512,32,32,2]{0,2,3,1:T(8,128)S(1)} fusion(bf16[64,32,1,32,2]{0,3,4,1,2:T(8,128)(2,1)S(1)} %copy.114, f32[64]{0:T(128)S(1)} %fusion.97), kind=kOutput, calls=%fused_computation.42 | convolution fusion | flops 134742016 | bytes 4456704 | tf_op jit(solution)/shard_map/kxcz,ky->cxzy/dot_general | solution.py:124
  87.7 0.0 copy-done
  87.7 0.4 copy-done.3
  88.1 0.0 copy-done.4
  88.1 3.7 %fusion.7 = bf16[32,32,2,512]{3,0,2,1:T(8,128)(2,1)} fusion(f32[512,32,32,2]{0,2,3,1:T(8,128)S(1)} %fusion.51, f32[512,32,32,2]{0,2,3,1:T(8,128)S(1)} %fusion.49, bf16[32,32,2,512]{3,0,2,1:T(8,128)(2,1)S(1)} %copy-done.3, f32[32]{0:T(128)S(1)} %copy-done.4, bf16[32,32]{1,0:T(8,128)(2,1)S(1)} %copy-done), kind=kOutput, calls=%fused_computation.8 | convolution fusion | flops 79691776 | bytes 12585088 | tf_op jit(solution)/shard_map/oc,cxzy->oxzy/dot_general | solution.py:128
  91.9 0.0 reduce-scatter.2.cloned.1.call-update
  91.9 8.0 %reduce-scatter.2.cloned.1.call-done = bf16[16,32,2,512]{3,0,2,1:T(8,128)(2,1)} async-done(((bf16[32,32,2,512]{3,0,2,1:T(8,128)(2,1)}), bf16[16,32,2,512]{3,0,2,1:T(8,128)(2,1)}) %reduce-scatter.2.cloned.1.call-update) | async-done | bytes 1048592 | tf_op jit(solution)/shard_map/reduce_scatter | solution.py:133
  99.9 1.5 %multiply_convert_fusion.1 = bf16[16,32,2,512]{3,0,2,1:T(8,128)(2,1)S(1)} fusion(bf16[16,32,2,512]{3,0,2,1:T(8,128)(2,1)} %reduce-scatter.2.cloned.1.call-done), kind=kLoop, calls=%fused_computation.19 | loop fusion | flops 1572864 | bytes 2097152 | tf_op jit(solution)/shard_map/convert_element_type | solution.py:136
  101.4 2.1 %copy.101 = bf16[16,32,2,512]{3,2,1,0:T(2,128)(2,1)} copy(bf16[16,32,2,512]{3,0,2,1:T(8,128)(2,1)S(1)} %multiply_convert_fusion.1) | data formatting | bytes 2097152 | tf_op jit(solution)/shard_map/convert_element_type | solution.py:136
  (6 shorter events, 0.1 us)
Async XLA Ops:
  6.5 81.2 %copy-start = (bf16[32,32]{1,0:T(8,128)(2,1)S(1)}, bf16[32,32]{1,0:T(8,128)(2,1)}, u32[]{:S(2)}) copy-start(bf16[32,32]{1,0:T(8,128)(2,1)} %param.15) | copy-start | bytes 6148
  15.0 5.8 %copy-start.2 = (bf16[32,32,2,512]{3,0,2,1:T(8,128)(2,1)}, bf16[32,32,2,512]{3,0,2,1:T(8,128)(2,1)S(1)}, u32[]{:S(2)}) copy-start(bf16[32,32,2,512]{3,0,2,1:T(8,128)(2,1)S(1)} %multiply_convert_fusion) | copy-start | bytes 6291460
  23.4 23.6 %all-to-all-start = ((bf16[64,32,128]{2,1,0:T(8,128)(2,1)}), bf16[64,32,128]{2,1,0:T(8,128)(2,1)}, u32[]{:S(2)}, u32[]{:S(2)}) async-start(bf16[64,32,128]{2,1,0:T(8,128)(2,1)} %copy.84), calls=%async_computation | async-start | bytes 1048576 | tf_op jit(solution)/shard_map/all_to_all | solution.py:97
  50.1 2.4 %copy-start.1 = (bf16[4,64,1,32,32]{4,3,1,0,2:T(8,128)(2,1)S(1)}, bf16[4,64,1,32,32]{4,3,1,0,2:T(8,128)(2,1)}, u32[]{:S(2)}) copy-start(bf16[4,64,1,32,32]{4,3,1,0,2:T(8,128)(2,1)} %copy.110) | copy-start | bytes 1572868
  58.6 18.3 %all-to-all-start.1 = ((bf16[4,512,128]{2,0,1:T(4,128)(2,1)}), bf16[4,512,128]{2,0,1:T(4,128)(2,1)S(1)}, u32[]{:S(2)}, u32[]{:S(2)}) async-start(bf16[4,512,128]{2,0,1:T(4,128)(2,1)} %copy.96), calls=%async_computation.1 | async-start | bytes 1048576 | tf_op jit(solution)/shard_map/all_to_all | solution.py:114
  62.5 37.4 %reduce-scatter.2.cloned.1.call-start = ((), (), s32[]{:S(2)}) async-start(), calls=%async_computation.3 | async-start | bytes 3145728 | tf_op jit(solution)/shard_map/reduce_scatter | solution.py:133
  86.5 1.6 %copy-start.3 = (bf16[32,32,2,512]{3,0,2,1:T(8,128)(2,1)S(1)}, bf16[32,32,2,512]{3,0,2,1:T(8,128)(2,1)}, u32[]{:S(2)}) copy-start(bf16[32,32,2,512]{3,0,2,1:T(8,128)(2,1)} %copy-done.2) | copy-start | bytes 6291460
  86.5 1.6 %copy-start.4 = (f32[32]{0:T(128)S(1)}, f32[32]{0:T(128)}, u32[]{:S(2)}) copy-start(f32[32]{0:T(128)} %param.16) | copy-start | bytes 388
Sparse Core Ops, SparseCore 0:
  92.0 7.8 reduce-scatter.1
where the time goes:
time: 111 us; the launch traced here: 110 us
  waiting for transfers between devices  27.7 us (25%)
  local copies, waits for them, and re-layouts  25.1 us (23%)
  matrix products  19.6 us (18%)
  between operations  15 us (14%)
  starting transfers between devices  12.5 us (11%)
  other arithmetic  10.3 us (9%)
    all_to_all x1, waiting for transfers between devices, local(): lax.all_to_all(back, 'slab', split_axis=1, concat_axis=0, tiled=True)  14.1 us
    unnamed x16, local copies, waits for them, and re-layouts  11.9 us
    all_to_all x1, starting transfers between devices, local(): lax.all_to_all(packed, 'slab', split_axis=0, concat_axis=1, tiled=True)  8.38 us
    reduce_scatter x1, waiting for transfers between devices, local(): lax.psum_scatter(layer.astype(jnp.bfloat16), 'member', scatter_dimension=...  7.98 us
    all_to_all x1, waiting for transfers between devices, local(): lax.all_to_all(packed, 'slab', split_axis=0, concat_axis=1, tiled=True)  5.56 us
    dot_general x4, matrix products, mixing(): jnp.einsum('kmoi,kmiz->kmoz', weights, values, preferred_element_type=jnp...  4.77 us
    convert_element_type x1, other arithmetic, local(): field_now = (2.0 * jnp.tanh(0.5 * driven)).astype(jnp.bfloat16)  4.29 us
    all_to_all x1, starting transfers between devices, local(): lax.all_to_all(back, 'slab', split_axis=1, concat_axis=0, tiled=True)  3.89 us
  transfers between devices with their start and end apart: 3, of which 3 were waited for; matrix products, arithmetic and copies ran while one was open for 8% of the time, Pallas kernels for 0%

commit v1 on v0

--- a/solution.py
+++ b/solution.py
@@ -2,10 +2,405 @@
 
 import jax
 import jax.numpy as jnp
+import numpy as np
 from jax import lax
+from jax.experimental import pallas as pl
+from jax.experimental.pallas import tpu as pltpu
 from jax.sharding import PartitionSpec as P
 
 TWO_PI = 2.0 * math.pi
+LANES = 128
+SUBLANES = 8
+SMEM = pltpu.SMEM
+F32 = jnp.float32
+BF16 = jnp.bfloat16
+
+
+def host_phases(frequency, positions, length):
+    product = frequency[:, None] * positions[None, :] % length
+    angles = product.astype(np.float32) * np.float32(TWO_PI / length)
+    return np.cos(angles), np.sin(angles)
+
+
+def first_frequencies(modes_x, length_x):
+    return np.concatenate([np.arange(modes_x // 2), np.arange(length_x - modes_x // 2, length_x)])
+
+
+def as_bf16(table):
+    return jnp.asarray(table.astype(BF16))
+
+
+def forward_y_table(modes_y, length_y):
+    cos, sin = host_phases(np.arange(modes_y), np.arange(length_y), length_y)
+    return as_bf16(np.concatenate([cos, -sin], axis=0))
+
+
+def inverse_y_table(modes_y, length_y, length_x, slabs):
+    cos, sin = host_phases(np.arange(modes_y), np.arange(length_y), length_y)
+    scale = np.where(np.arange(modes_y) == 0, 1.0, 2.0).astype(np.float32)
+    scale = (scale / np.float32(length_x * length_y))[:, None]
+    parts = np.stack([scale * cos, -(scale * sin)], axis=0)
+    parts = parts.reshape(2, slabs, modes_y // slabs, length_y).transpose(1, 0, 2, 3)
+    return as_bf16(parts.reshape(2 * modes_y, length_y))
+
+
+def forward_x_table(modes_x, length_x, slabs, planes):
+    cos, sin = host_phases(first_frequencies(modes_x, length_x), np.arange(length_x), length_x)
+    whole = np.array([[cos, -sin], [sin, cos]])
+    whole = whole.reshape(2, 2, modes_x, slabs, length_x // slabs)
+    table = np.einsum("abqsx,zw->sazxwbq", whole, np.eye(planes, dtype=np.float32))
+    return as_bf16(table.reshape(2 * planes * length_x, planes * 2 * modes_x))
+
+
+def inverse_x_table(modes_x, length_x, slabs, planes):
+    cos, sin = host_phases(first_frequencies(modes_x, length_x), np.arange(length_x), length_x)
+    whole = np.array([cos, -sin]).reshape(2, modes_x, slabs, length_x // slabs)
+    table = np.einsum("aqsx,zw->zaqswx", whole, np.eye(planes, dtype=np.float32))
+    return as_bf16(table.reshape(planes * 2 * modes_x, planes * length_x))
+
+
+def low_half(shape):
+    return lax.broadcasted_iota(jnp.int32, shape, len(shape) - 1) < shape[-1] // 2
+
+
+def half_turn(values):
+    return pltpu.roll(values, values.shape[-1] // 2, values.ndim - 1)
+
+
+def pair_halves(first, second):
+    low = low_half(first.shape)
+    return (
+        jnp.where(low, first, half_turn(second)),
+        jnp.where(low, half_turn(first), second),
+    )
+
+
+def driven_field(base, forcing, strength):
+    return 2.0 * jnp.tanh(0.5 * (base.astype(F32) + strength * forcing))
+
+
+def y_modes_kernel(
+    index_ref, amplitude_ref, load_ref, base_ref, forcing_ref, table_ref, out_ref, cells, rows, modes
+):
+    group = pl.program_id(0)
+    width, cell_rows, _ = base_ref.shape
+    planes, y_blocks, slab_rows = Y_LAYOUT(cell_rows, table_ref.shape[1])
+    channels = load_ref.shape[0]
+    modes_y = table_ref.shape[0] // 2
+    amplitude = amplitude_ref[index_ref[0]]
+    forcing = forcing_ref[...].astype(F32)
+    span = planes * slab_rows
+    for c in range(width):
+        cells[c] = driven_field(base_ref[c], forcing, amplitude * load_ref[group * width + c])
+        for z in range(planes):
+            for j in range(y_blocks):
+                picked = cells[c, pl.ds(j * planes + z, slab_rows, stride=planes * y_blocks), :]
+                rows[
+                    pl.ds(c * span + z * slab_rows, slab_rows), pl.ds(j * LANES, LANES)
+                ] = picked.astype(BF16)
+    result = lax.dot_general(
+        table_ref[...], rows[...], (((1,), (1,)), ((), ())), preferred_element_type=F32
+    )
+    for t in range(width // 2):
+        tile = slice(t * LANES, (t + 1) * LANES)
+        pair = pair_halves(result[:modes_y, tile], result[modes_y:, tile])
+        for n in range(2):
+            modes[pl.ds(group * width + 2 * t + n, modes_y, stride=channels), :] = pair[n]
+
+    @pl.when(group == pl.num_programs(0) - 1)
+    def _():
+        block_rows = out_ref.shape[1]
+        for d in range(out_ref.shape[0]):
+            out_ref[d] = modes[pl.ds(d * block_rows, block_rows), :].astype(BF16)
+
+
+def Y_LAYOUT(cell_rows, length_y):
+    y_blocks = length_y // LANES
+    planes = SUBLANES // y_blocks
+    return planes, y_blocks, cell_rows // SUBLANES
+
+
+def y_modes(amp_index, amplitudes, load, cells, forcing, slabs, modes_y, length_y):
+    channels, cell_rows, _ = cells.shape
+    width = 4
+    block_rows = modes_y // slabs * channels
+    table = forward_y_table(modes_y, length_y)
+    planes, y_blocks, slab_rows = Y_LAYOUT(cell_rows, length_y)
+    smem = pl.BlockSpec(memory_space=SMEM)
+    return pl.pallas_call(
+        y_modes_kernel,
+        grid=(channels // width,),
+        in_specs=[
+            smem,
+            smem,
+            smem,
+            pl.BlockSpec((width, cell_rows, LANES), lambda g: (g, 0, 0)),
+            pl.BlockSpec((cell_rows, LANES), lambda g: (0, 0)),
+            pl.BlockSpec(table.shape, lambda g: (0, 0)),
+        ],
+        out_specs=pl.BlockSpec((slabs, block_rows, LANES), lambda g: (0, 0, 0)),
+        out_shape=jax.ShapeDtypeStruct((slabs, block_rows, LANES), BF16),
+        scratch_shapes=[
+            pltpu.VMEM((width, cell_rows, LANES), F32),
+            pltpu.VMEM((width * planes * slab_rows, length_y), BF16),
+            pltpu.VMEM((modes_y * channels, LANES), F32),
+        ],
+        compiler_params=pltpu.CompilerParams(vmem_limit_bytes=32 * 1024 * 1024),
+        cost_estimate=pl.CostEstimate(
+            flops=4 * modes_y * cells.size, bytes_accessed=4 * cells.size, transcendentals=cells.size
+        ),
+        name="y_modes",
+    )(amp_index, amplitudes, load, cells, forcing, table)
+
+
+def mix_kernel(
+    limit_ref, pencil_ref, forward_ref, straight_ref, crossed_ref, inverse_ref, out_ref, spectrum, turned, mixed
+):
+    slabs, block_rows, _ = pencil_ref.shape
+    local_modes, channels, _, width = straight_ref.shape
+    planes = forward_ref.shape[1] // width
+    groups = channels // SUBLANES
+    pencil = jnp.concatenate([pencil_ref[s] for s in range(slabs)], axis=1)
+    result = jnp.dot(pencil, forward_ref[...], preferred_element_type=F32)
+    for z in range(planes):
+        part = result[:, z * width : (z + 1) * width]
+        spectrum[z] = part
+        turned[z] = half_turn(part)
+    low = low_half((SUBLANES, width))
+    block = SUBLANES * 2 * local_modes
+    for k in range(local_modes):
+        keep = jnp.where(limit_ref[0] > k, 1.0, 0.0).astype(F32)
+        sums = [[jnp.zeros((SUBLANES, width), F32) for _ in range(groups)] for _ in range(planes)]
+        for i in range(channels):
+            row = pl.ds(k * channels + i, 1)
+            plain = [jnp.broadcast_to(spectrum[z, row, :], (SUBLANES, width)) for z in range(planes)]
+            other = [jnp.broadcast_to(turned[z, row, :], (SUBLANES, width)) for z in range(planes)]
+            for g in range(groups):
+                straight = straight_ref[k, i, pl.ds(g * SUBLANES, SUBLANES), :]
+                crossed = crossed_ref[k, i, pl.ds(g * SUBLANES, SUBLANES), :]
+                for z in range(planes):
+                    sums[z][g] = sums[z][g] + (straight * plain[z] + crossed * other[z])
+        for z in range(planes):
+            for g in range(groups):
+                kept = sums[z][g] * keep
+                swapped = half_turn(kept)
+                start = g * block + k
+                mixed[z, pl.ds(start, SUBLANES, stride=2 * local_modes), :] = kept
+                mixed[z, pl.ds(start + local_modes, SUBLANES, stride=2 * local_modes), :] = jnp.where(
+                    low, swapped, -swapped
+                )
+    left = jnp.concatenate([mixed[z].astype(BF16) for z in range(planes)], axis=1)
+    back = jnp.dot(left, inverse_ref[...], preferred_element_type=F32)
+    members = out_ref.shape[0] // slabs
+    for h in range(members):
+        for t in range(slabs // 2):
+            tile = slice(t * LANES, (t + 1) * LANES)
+            start = 2 * h * block
+            pair = pair_halves(back[start : start + block, tile], back[start + block : start + 2 * block, tile])
+            for n in range(2):
+                out_ref[h * slabs + 2 * t + n] = pair[n].astype(BF16)
+
+
+def mix(limit, pencil, straight, crossed, length_x, planes, members):
+    slabs, block_rows, _ = pencil.shape
+    local_modes, channels, _, width = straight.shape
+    modes_x = width // 2
+    forward = forward_x_table(modes_x, length_x, slabs, planes)
+    inverse = inverse_x_table(modes_x, length_x, slabs, planes)
+    vmem = pl.BlockSpec(memory_space=pltpu.VMEM)
+    block = SUBLANES * 2 * local_modes
+    return pl.pallas_call(
+        mix_kernel,
+        in_specs=[pl.BlockSpec(memory_space=SMEM)] + [vmem] * 5,
+        out_specs=vmem,
+        out_shape=jax.ShapeDtypeStruct((members * slabs, block, LANES), BF16),
+        scratch_shapes=[
+            pltpu.VMEM((planes, block_rows, width), F32),
+            pltpu.VMEM((planes, block_rows, width), F32),
+            pltpu.VMEM((planes, channels // SUBLANES * block, width), F32),
+        ],
+        compiler_params=pltpu.CompilerParams(vmem_limit_bytes=40 * 1024 * 1024),
+        cost_estimate=pl.CostEstimate(
+            flops=2 * block_rows * forward.size, bytes_accessed=8 * straight.size, transcendentals=0
+        ),
+        name="mix",
+    )(limit, pencil, forward, straight, crossed, inverse)
+
+
+def pointwise_kernel(
+    place_ref, index_ref, amplitude_ref, load_ref, bias_ref, base_ref, forcing_ref, weight_ref, out_ref
+):
+    channels, depth, _ = base_ref.shape
+    members = index_ref.shape[0]
+    me = place_ref[0]
+    forcing = forcing_ref[...].astype(F32)
+    fields = []
+    for m in range(members):
+        amplitude = amplitude_ref[index_ref[lax.rem(me - m + members, members)]]
+        parts = [
+            driven_field(base_ref[c], forcing, amplitude * load_ref[c]).astype(BF16) for c in range(channels)
+        ]
+        fields.append(jnp.concatenate(parts, axis=0))
+    result = jnp.dot(weight_ref[...], jnp.concatenate(fields, axis=1), preferred_element_type=F32)
+    _, outer, inner, _, _ = out_ref.shape
+    for a in range(outer):
+        for b in range(inner):
+            o = a * inner + b
+            bias = bias_ref[me * outer * inner + o]
+            for m in range(members):
+                out_ref[m, a, b] = result[o * depth : (o + 1) * depth, m * LANES : (m + 1) * LANES] + bias
+
+
+def pointwise(place, indices, amplitudes, load, bias, cells, forcing, weight):
+    channels, cell_rows, _ = cells.shape
+    members = indices.shape[0]
+    depth = 2 * SUBLANES
+    inner = SUBLANES
+    outer = channels // members // inner
+    spread = (weight[:, None, :, None] * jnp.eye(depth, dtype=BF16)[None, :, None, :]).reshape(
+        weight.shape[0] * depth, channels * depth
+    )
+    smem = pl.BlockSpec(memory_space=SMEM)
+    return pl.pallas_call(
+        pointwise_kernel,
+        grid=(cell_rows // depth,),
+        in_specs=[smem] * 5
+        + [
+            pl.BlockSpec((channels, depth, LANES), lambda r: (0, r, 0)),
+            pl.BlockSpec((depth, LANES), lambda r: (r, 0)),
+            pl.BlockSpec(spread.shape, lambda r: (0, 0)),
+        ],
+        out_specs=pl.BlockSpec((members, outer, inner, depth, LANES), lambda r: (0, 0, 0, r, 0)),
+        out_shape=jax.ShapeDtypeStruct((members, outer, inner, cell_rows, LANES), F32),
+        compiler_params=pltpu.CompilerParams(vmem_limit_bytes=32 * 1024 * 1024),
+        cost_estimate=pl.CostEstimate(
+            flops=4 * spread.size * members * cell_rows // depth * LANES,
+            bytes_accessed=8 * cells.size,
+            transcendentals=members * cells.size,
+        ),
+        name="pointwise",
+    )(place, indices, amplitudes, load, bias, cells, forcing, spread)
+
+
+def layer_kernel(back_ref, table_ref, point_ref, out_ref, columns, spectral):
+    step = pl.program_id(0)
+    members, outer, _, cell_rows, _ = point_ref.shape
+    sources, block_rows, _ = back_ref.shape
+    slabs = sources // members
+    inner = columns.shape[0]
+    depth = block_rows // inner
+    planes, y_blocks, slab_rows = Y_LAYOUT(cell_rows, table_ref.shape[1])
+
+    @pl.when(step == 0)
+    def _():
+        for m in range(members):
+            for s in range(slabs):
+                block = back_ref[m * slabs + s].astype(F32)
+                for b in range(inner):
+                    columns[b, m, pl.ds(s * depth, depth), :] = block[b * depth : (b + 1) * depth]
+
+    for m in range(members):
+        left = columns[step, m].astype(BF16)
+        values = lax.dot_general(
+            left, table_ref[...], (((0,), (0,)), ((), ())), preferred_element_type=F32
+        )
+        for a in range(outer):
+            for z in range(planes):
+                start = (a * planes + z) * slab_rows
+                for j in range(y_blocks):
+                    spectral[m, a, pl.ds(j * planes + z, slab_rows, stride=planes * y_blocks), :] = values[
+                        start : start + slab_rows, j * LANES : (j + 1) * LANES
+                    ]
+    for a in range(outer):
+        total = None
+        for m in range(members):
+            value = jax.nn.gelu(point_ref[m, a, 0] + spectral[m, a], approximate=True)
+            total = value if total is None else total + value
+        out_ref[a, 0] = (total * (1.0 / members)).astype(BF16)
+
+
+def layer(back, points, length_x, length_y, modes_y):
+    members, outer, inner, cell_rows, _ = points.shape
+    slabs = back.shape[0] // members
+    table = inverse_y_table(modes_y, length_y, length_x, slabs)
+    return pl.pallas_call(
+        layer_kernel,
+        grid=(inner,),
+        in_specs=[
+            pl.BlockSpec(back.shape, lambda b: (0, 0, 0)),
+            pl.BlockSpec(table.shape, lambda b: (0, 0)),
+            pl.BlockSpec((members, outer, 1, cell_rows, LANES), lambda b: (0, 0, b, 0, 0)),
+        ],
+        out_specs=pl.BlockSpec((outer, 1, cell_rows, LANES), lambda b: (0, b, 0, 0)),
+        out_shape=jax.ShapeDtypeStruct((outer, inner, cell_rows, LANES), BF16),
+        scratch_shapes=[
+            pltpu.VMEM((inner, members, 2 * modes_y, LANES), F32),
+            pltpu.VMEM((members, outer, cell_rows, LANES), F32),
+        ],
+        compiler_params=pltpu.CompilerParams(vmem_limit_bytes=32 * 1024 * 1024),
+        cost_estimate=pl.CostEstimate(
+            flops=4 * modes_y * points.size, bytes_accessed=5 * points.size, transcendentals=points.size
+        ),
+        name="layer",
+    )(back, table, points)
+
+
+def fast_local(
+    base_field,
+    forcing,
+    load,
+    amplitudes,
+    amp_index,
+    mode_count,
+    point_weight,
+    point_bias,
+    spectral_weight,
+):
+    channels, slab_rows, planes, length_y = base_field.shape
+    slabs, members = lax.axis_size("slab"), lax.axis_size("member")
+    local_modes, modes_x = spectral_weight.shape[:2]
+    modes_y = local_modes * slabs
+    length_x = slab_rows * slabs
+    y_blocks = length_y // LANES
+    cells = base_field.reshape(channels, slab_rows, planes, y_blocks, LANES).transpose(0, 1, 3, 2, 4)
+    cells = cells.reshape(channels, slab_rows * SUBLANES, LANES)
+    force = forcing.reshape(slab_rows, planes, y_blocks, LANES).transpose(0, 2, 1, 3)
+    force = force.reshape(slab_rows * SUBLANES, LANES)
+    me = lax.axis_index("member")
+    indices = jnp.concatenate(
+        [amp_index]
+        + [
+            lax.ppermute(amp_index, "member", [(s, (s + r) % members) for s in range(members)])
+            for r in range(1, members)
+        ]
+    )
+    out_channels = channels // members
+    packed = y_modes(amp_index, amplitudes, load, cells, force, slabs, modes_y, length_y)
+    pencil = lax.all_to_all(packed, "slab", split_axis=0, concat_axis=0, tiled=True)
+    weights = spectral_weight.transpose(0, 2, 4, 3, 1).astype(F32)
+    straight = jnp.concatenate([weights[:, 0], weights[:, 0]], axis=-1)
+    crossed = jnp.concatenate([-weights[:, 1], weights[:, 1]], axis=-1)
+    limit = mode_count - lax.axis_index("slab") * local_modes
+    back = mix(limit, pencil, straight, crossed, length_x, planes, members)
+    back = lax.all_to_all(back, ("member", "slab"), split_axis=0, concat_axis=0, tiled=True)
+    weight = lax.dynamic_slice_in_dim(point_weight, me * out_channels, out_channels, 0)
+    points = pointwise(me.reshape(1), indices, amplitudes, load, point_bias, cells, force, weight)
+    result = layer(back, points, length_x, length_y, modes_y)
+    result = result.reshape(out_channels, slab_rows, y_blocks, planes, LANES).transpose(0, 1, 3, 2, 4)
+    return result.reshape(out_channels, slab_rows, planes, length_y)
+
+
+def tiles_fit(base_shape, weight_shape, slabs, members):
+    channels, slab_rows, planes, length_y = base_shape
+    local_modes, modes_x = weight_shape[:2]
+    return (
+        2 * planes * slab_rows == LANES
+        and 2 * modes_x == LANES
+        and planes * length_y == SUBLANES * LANES
+        and 2 * local_modes == SUBLANES
+        and 2 * SUBLANES * members == channels
+        and slabs % 2 == 0
+    )
 
 
 def phases(frequency, positions, length):
@@ -46,7 +441,7 @@
     return jnp.einsum("kmoi,kmiz->kmoz", weights, values, preferred_element_type=jnp.float32)
 
 
-def local(
+def general_local(
     base_field,
     forcing,
     load,
@@ -136,6 +531,23 @@
     return (total / lax.axis_size("member")).astype(jnp.bfloat16)
 
 
+def local(base_field, forcing, load, amplitudes, amp_index, mode_count, point_weight, point_bias, spectral_weight):
+    fits = tiles_fit(
+        base_field.shape, spectral_weight.shape, lax.axis_size("slab"), lax.axis_size("member")
+    )
+    return (fast_local if fits else general_local)(
+        base_field,
+        forcing,
+        load,
+        amplitudes,
+        amp_index,
+        mode_count,
+        point_weight,
+        point_bias,
+        spectral_weight,
+    )
+
+
 def solution(mesh):
     in_specs = (
         P(None, "slab", None, None),

time: 111 us -> 67.3 us (0.61)
  waiting for transfers between devices: 27.7 us -> 7 us
  Pallas kernels: 0 us -> 19.9 us
  matrix products: 19.6 us -> 0 us
  between operations: 15 us -> 1.5 us
  local copies, waits for them, and re-layouts: 25.1 us -> 17.4 us
    pallas_call x0 -> x4, Pallas kernels: none -> 19.9 us  [the longest x1 6.68 us: pointwise(): pl.pallas_call(pointwise_kernel, grid=(cell_rows // depth,), in_specs=[sm...]
    dot_general x13 -> x0, matrix products: 19.6 us -> none  [the longest x4 4.77 us: mixing(): jnp.einsum('kmoi,kmiz->kmoz', weights, values, preferred_element_type=jnp...]
    all_to_all x2, waiting for transfers between devices: 19.7 us -> 7 us  [the longest x1 6.02 us: fast_local(): lax.all_to_all(packed, 'slab', split_axis=0, concat_axis=0, tiled=True)]
    reduce_scatter x1 -> x0, waiting for transfers between devices: 7.98 us -> none  [local(): lax.psum_scatter(layer.astype(jnp.bfloat16), 'member', scatter_dimension=...]
    convert_element_type x3 -> x0, local copies, waits for them, and re-layouts: 5.45 us -> none  [the longest x1 2.34 us: local(): packed = jnp.stack([y_real, y_imag], axis=2).astype(jnp.bfloat16).reshape...]
    slice x3 -> x0, local copies, waits for them, and re-layouts: 4.98 us -> none  [the longest x1 2.87 us: local(): returned[:, :, 1]]
    mul x0 -> x1, local copies, waits for them, and re-layouts: none -> 4.51 us  [pointwise(): weight[:, None, :, None] * jnp.eye(depth, dtype=BF16)[None, :, None, :]]
    convert_element_type x4 -> x2, other arithmetic: 6.67 us -> 2.7 us  [the longest x1 2.69 us: fast_local(): weights = spectral_weight.transpose(0, 2, 4, 3, 1).astype(F32)]
  transfers between devices with their start and end apart: 3 -> 3, of which waited for: 3 -> 2; matrix products, arithmetic and copies ran while one was open for 8% -> 22% of each run, Pallas kernels for 0% -> 10%
where the time goes in v1:
time: 67.3 us; the launch traced here: 66.7 us
  Pallas kernels  19.9 us (30%)
  local copies, waits for them, and re-layouts  17.4 us (26%)
  starting transfers between devices  11.5 us (17%)
  other arithmetic  9.4 us (14%)
  waiting for transfers between devices  7 us (10%)
  between operations  1.5 us (2%)
    unnamed x38, local copies, waits for them, and re-layouts  12.5 us
    all_to_all x1, starting transfers between devices, fast_local(): lax.all_to_all(packed, 'slab', split_axis=0, concat_axis=0, tiled=True)  8.31 us
    pallas_call x1, Pallas kernels, pointwise(): pl.pallas_call(pointwise_kernel, grid=(cell_rows // depth,), in_specs=[sm...  6.68 us
    all_to_all x1, waiting for transfers between devices, fast_local(): lax.all_to_all(packed, 'slab', split_axis=0, concat_axis=0, tiled=True)  6.02 us
    pallas_call x1, Pallas kernels, y_modes(): pl.pallas_call(y_modes_kernel, grid=(channels // width,), in_specs=[smem,...  5.54 us
    pallas_call x1, Pallas kernels, layer(): pl.pallas_call(layer_kernel, grid=(inner,), in_specs=[pl.BlockSpec(back.s...  5.03 us
    mul x1, local copies, waits for them, and re-layouts, pointwise(): weight[:, None, :, None] * jnp.eye(depth, dtype=BF16)[None, :, None, :]  4.51 us
    all_to_all x1, starting transfers between devices, fast_local(): lax.all_to_all(back, ('member', 'slab'), split_axis=0, concat_axis=0, til...  2.88 us
  transfers between devices with their start and end apart: 3, of which 2 were waited for; matrix products, arithmetic and copies ran while one was open for 22% of the time, Pallas kernels for 10%

profile of v1, /device:TPU:0, one launch (start us, length us, event | category | flops | bytes accessed | tf_op | source)
XLA Modules:
  0.0 66.7 jit_solution(6254531181683181115)
XLA Ops:
  0.0 0.0 copy-start
  0.7 0.0 copy-start.4
  0.7 1.6 %copy-done.4 = bf16[32,32,2,512]{3,2,1,0:T(2,128)(2,1)S(1)} copy-done((bf16[32,32,2,512]{3,2,1,0:T(2,128)(2,1)S(1)}, bf16[32,32,2,512]{3,2,1,0:T(2,128)(2,1)}, u32[]{:S(2)}) %copy-start.4) | copy-done | bytes 2097176
  2.3 0.0 copy-start.9
  2.3 0.9 %copy-done.9 = bf16[128,512]{1,0:T(8,128)(2,1)S(1)} copy-done((bf16[128,512]{1,0:T(8,128)(2,1)S(1)}, bf16[128,512]{1,0:T(8,128)(2,1)}, u32[]{:S(2)}) %copy-start.9) | copy-done | bytes 131096
  3.2 0.0 copy-start.10
  3.2 0.8 %copy-done.10 = bf16[32,2,512]{2,1,0:T(2,128)(2,1)S(1)} copy-done((bf16[32,2,512]{2,1,0:T(2,128)(2,1)S(1)}, bf16[32,2,512]{2,1,0:T(2,128)(2,1)}, u32[]{:S(2)}) %copy-start.10) | copy-done | bytes 65560
  4.0 0.0 copy-start.12
  4.0 0.7 copy-done.12
  4.7 0.0 copy-start.14
  4.7 0.7 copy-done.14
  5.3 0.0 copy-start.18
  5.3 5.5 %y_modes.1 = bf16[16,128,128]{2,1,0:T(8,128)(2,1)} custom-call(s32[1]{0:T(128)S(6)} %copy.23.index_ref, f32[16]{0:T(128)S(1)} %copy-done.12, f32[32]{0:T(128)S(1)} %copy-done.14, bf16[32,256,128]{2,1,0:T(8,128)(2,1)S(1)} %bitcast.27, bf16[256,128]{1,0:T(8,128)(2,1)S(1)} %bitcast.29, bf16[128,512]{1,0:T(8,128)(2,1)S(1)} %copy-done.9), custom_call_target="tpu_custom_call" | custom-call | flops 268435456 | bytes 4194304 | tf_op jit(solution)/shard_map/y_modes/pallas_call | solution.py:130
  10.9 8.3 %all-to-all-start = ((bf16[16,128,128]{2,1,0:T(8,128)(2,1)}), bf16[16,128,128]{2,1,0:T(8,128)(2,1)S(1)}, u32[]{:S(2)}, u32[]{:S(2)}) async-start(bf16[16,128,128]{2,1,0:T(8,128)(2,1)} %y_modes.1), calls=%async_computation | async-start | bytes 1048576 | tf_op jit(solution)/shard_map/all_to_all | solution.py:379
  19.2 0.0 copy-done.18
  19.2 2.7 %convert_bitcast_fusion = f32[4,2,32,32,64]{4,3,2,0,1:T(8,128)} fusion(bf16[4,64,2,32,32]{1,4,3,2,0:T(8,128)(2,1)S(1)} %copy-done.18), kind=kLoop, calls=%fused_computation | loop fusion | flops 524288 | bytes 3145728 | tf_op jit(solution)/shard_map/convert_element_type | solution.py:380
  22.5 0.0 copy-start.17
  22.6 2.0 %fusion.1 = f32[4,32,32,64]{3,2,1,0:T(8,128)S(1)} fusion(f32[4,2,32,32,64]{4,3,2,0,1:T(8,128)} %convert_bitcast_fusion), kind=kLoop, calls=%fused_computation.10 | loop fusion | flops 262144 | bytes 2097152 | tf_op jit(solution)/shard_map/neg | solution.py:382
  24.5 0.8 %copy-done.17 = f32[4,2,32,32,64]{4,3,2,0,1:T(8,128)S(1)} copy-done((f32[4,2,32,32,64]{4,3,2,0,1:T(8,128)S(1)}, f32[4,2,32,32,64]{4,3,2,0,1:T(8,128)}, u32[]{:S(2)}) %copy-start.17) | copy-done | bytes 2097176
  25.4 0.4 slice_bitcast_fusion
  25.8 0.0 copy-start.7
  25.8 2.5 %pad_maximum_fusion = (f32[4,32,32,128]{3,2,1,0:T(8,128)S(1)}, f32[4,32,32,128]{3,2,1,0:T(8,128)}) fusion(f32[4,32,32,64]{3,2,1,0:T(8,128)S(1)} %get-tuple-element.6, f32[4,32,32,64]{3,2,1,0:T(8,128)S(1)} %get-tuple-element.5, f32[4,32,32,64]{3,2,1,0:T(8,128)S(1)} %fusion.1), kind=kLoop, calls=%fused_computation.3 | loop fusion | flops 1048576 | bytes 7340032 | tf_op jit(solution)/shard_map/concatenate | solution.py:381
  28.3 6.0 %all-to-all-done.pencil_ref = bf16[16,128,128]{2,1,0:T(8,128)(2,1)S(1)} async-done(((bf16[16,128,128]{2,1,0:T(8,128)(2,1)}), bf16[16,128,128]{2,1,0:T(8,128)(2,1)S(1)}, u32[]{:S(2)}, u32[]{:S(2)}) %all-to-all-start) | async-done | bytes 524320 | tf_op jit(solution)/shard_map/all_to_all | solution.py:379
  34.3 0.0 copy-done.7
  34.3 0.0 copy-start.1
  34.3 1.6 %copy-done.1 = f32[4,32,32,128]{3,2,1,0:T(8,128)S(1)} copy-done((f32[4,32,32,128]{3,2,1,0:T(8,128)S(1)}, f32[4,32,32,128]{3,2,1,0:T(8,128)}, u32[]{:S(2)}) %copy-start.1) | copy-done | bytes 2097176
  35.9 0.0 copy-start.6
  35.9 1.2 %copy-done.6 = bf16[2048,256]{1,0:T(8,128)(2,1)S(1)} copy-done((bf16[2048,256]{1,0:T(8,128)(2,1)S(1)}, bf16[2048,256]{1,0:T(8,128)(2,1)}, u32[]{:S(2)}) %copy-start.6) | copy-done | bytes 1048600
  37.1 2.6 %mix.1 = bf16[32,64,128]{2,1,0:T(8,128)(2,1)} custom-call(s32[1]{0:T(128)S(6)} %sub.7.limit_ref, bf16[16,128,128]{2,1,0:T(8,128)(2,1)S(1)} %all-to-all-done.pencil_ref, bf16[2048,256]{1,0:T(8,128)(2,1)S(1)} %copy-done.6, f32[4,32,32,128]{3,2,1,0:T(8,128)S(1)} %get-tuple-element.7.straight_ref, f32[4,32,32,128]{3,2,1,0:T(8,128)S(1)} %copy-done.1, ...), custom_call_target="tpu_custom_call" | custom-call | flops 134217728 | bytes 4194304 | tf_op jit(solution)/shard_map/mix/pallas_call | solution.py:212
  39.8 2.9 %all-to-all-start.1 = ((bf16[32,64,128]{2,1,0:T(8,128)(2,1)}), bf16[32,64,128]{2,1,0:T(8,128)(2,1)S(1)}, u32[]{:S(2)}, u32[]{:S(2)}) async-start(bf16[32,64,128]{2,1,0:T(8,128)(2,1)} %mix.1), calls=%async_computation.1 | async-start | bytes 1048576 | tf_op jit(solution)/shard_map/all_to_all | solution.py:385
  42.6 0.3 collective-permute-start
  43.0 0.0 copy-done
  43.0 0.0 copy-start.5
  43.0 0.0 copy-start.11
  43.0 0.0 copy-start.13
  43.0 0.0 copy-start.15
  43.0 0.0 copy-start.16
  43.0 1.5 %broadcast_multiply_fusion = bf16[16,16,32,16]{3,2,1,0:T(8,128)(2,1)} fusion(bf16[16,16]{1,0:T(8,128)(2,1)S(1)} %fusion, bf16[16,32]{1,0:T(8,128)(2,1)S(1)} %constant_dynamic-slice_fusion), kind=kLoop, calls=%fused_computation.5 | loop fusion | flops 131072 | bytes 263680 | tf_op jit(solution)/shard_map/mul | solution.py:260
  44.6 4.5 %mul.28.weight_ref = bf16[256,512]{1,0:T(8,128)(2,1)S(1)} reshape(bf16[16,16,32,16]{3,2,1,0:T(8,128)(2,1)} %broadcast_multiply_fusion) | data formatting | bytes 524288 | tf_op jit(solution)/shard_map/mul | solution.py:260
  49.1 0.0 collective-permute-done
  49.1 0.7 %pad_add_fusion.index_ref = s32[2]{0:T(128)S(1)} fusion(s32[1]{0:T(128)} %collective-permute-done, s32[1]{0:T(128)S(6)} %copy.23.index_ref), kind=kLoop, calls=%fused_computation.8 | loop fusion | flops 2 | bytes 16 | tf_op jit(solution)/shard_map/concatenate | solution.py:370
  49.8 0.0 copy-done.5
  49.8 0.0 copy-done.11
  49.8 0.0 copy-done.13
  49.8 0.0 copy-done.15
  49.8 0.0 copy-done.16
  49.8 0.0 copy-start.8
  49.9 6.7 %pointwise.1.point_ref = f32[2,2,8,256,128]{4,3,2,1,0:T(8,128)S(1)} custom-call(s32[1]{0:T(128)} %bitcast.10.place_ref, s32[2]{0:T(128)S(1)} %pad_add_fusion.index_ref, f32[16]{0:T(128)S(1)} %copy-done.13, f32[32]{0:T(128)S(1)} %copy-done.15, f32[32]{0:T(128)S(1)} %copy-done.16, bf16[32,256,128]{2,1,0:T(8,128)(2,1)S(1)} %bitcast.28, ...), custom_call_target="tpu_custom_call" | custom-call | flops 2147483648 | bytes 8388608 | tf_op jit(solution)/shard_map/pointwise/pallas_call | solution.py:264
  56.5 0.0 copy-start.2
  56.6 1.9 %copy-done.2 = f32[2,2,8,256,128]{4,3,2,1,0:T(8,128)} copy-done((f32[2,2,8,256,128]{4,3,2,1,0:T(8,128)}, f32[2,2,8,256,128]{4,3,2,1,0:T(8,128)S(1)}, u32[]{:S(2)}) %copy-start.2) | copy-done | bytes 4194328
  58.5 1.0 %all-to-all-done.1.back_ref = bf16[32,64,128]{2,1,0:T(8,128)(2,1)S(1)} async-done(((bf16[32,64,128]{2,1,0:T(8,128)(2,1)}), bf16[32,64,128]{2,1,0:T(8,128)(2,1)S(1)}, u32[]{:S(2)}, u32[]{:S(2)}) %all-to-all-start.1) | async-done | bytes 524320 | tf_op jit(solution)/shard_map/all_to_all | solution.py:385
  59.5 0.0 copy-done.8
  59.5 0.0 copy-start.3
  59.5 2.2 %copy-done.3 = f32[2,2,8,256,128]{4,3,2,1,0:T(8,128)S(1)} copy-done((f32[2,2,8,256,128]{4,3,2,1,0:T(8,128)S(1)}, f32[2,2,8,256,128]{4,3,2,1,0:T(8,128)}, u32[]{:S(2)}) %copy-start.3) | copy-done | bytes 4194328
  61.7 5.0 %layer.1 = bf16[2,8,256,128]{3,2,1,0:T(8,128)(2,1)} custom-call(bf16[32,64,128]{2,1,0:T(8,128)(2,1)S(1)} %all-to-all-done.1.back_ref, bf16[128,512]{1,0:T(8,128)(2,1)S(1)} %copy-done.8, f32[2,2,8,256,128]{4,3,2,1,0:T(8,128)S(1)} %copy-done.3), custom_call_target="tpu_custom_call" | custom-call | flops 268435456 | bytes 5242880 | tf_op jit(solution)/shard_map/layer/pallas_call | solution.py:326
  (2 shorter events, 0.0 us)
Async XLA Ops:
  0.0 43.0 %copy-start = (bf16[32,32]{1,0:T(8,128)(2,1)S(1)}, bf16[32,32]{1,0:T(8,128)(2,1)}, u32[]{:S(2)}) copy-start(bf16[32,32]{1,0:T(8,128)(2,1)} %param.19) | copy-start | bytes 6148
  0.7 1.6 %copy-start.4 = (bf16[32,32,2,512]{3,2,1,0:T(2,128)(2,1)S(1)}, bf16[32,32,2,512]{3,2,1,0:T(2,128)(2,1)}, u32[]{:S(2)}) copy-start(bf16[32,32,2,512]{3,2,1,0:T(2,128)(2,1)} %param.13) | copy-start | bytes 6291460
  2.3 0.9 %copy-start.9 = (bf16[128,512]{1,0:T(8,128)(2,1)S(1)}, bf16[128,512]{1,0:T(8,128)(2,1)}, u32[]{:S(2)}) copy-start(bf16[128,512]{1,0:T(8,128)(2,1)} %constant.25.clone.table_ref) | copy-start | bytes 393220
  3.2 0.8 %copy-start.10 = (bf16[32,2,512]{2,1,0:T(2,128)(2,1)S(1)}, bf16[32,2,512]{2,1,0:T(2,128)(2,1)}, u32[]{:S(2)}) copy-start(bf16[32,2,512]{2,1,0:T(2,128)(2,1)} %param.14) | copy-start | bytes 196612
  4.0 0.7 copy-start.12
  4.7 0.7 copy-start.14
  5.3 13.9 %copy-start.18 = (bf16[4,64,2,32,32]{1,4,3,2,0:T(8,128)(2,1)S(1)}, bf16[4,64,2,32,32]{1,4,3,2,0:T(8,128)(2,1)}, u32[]{:S(2)}) copy-start(bf16[4,64,2,32,32]{1,4,3,2,0:T(8,128)(2,1)} %param.21) | copy-start | bytes 3145732
  10.9 23.5 %all-to-all-start = ((bf16[16,128,128]{2,1,0:T(8,128)(2,1)}), bf16[16,128,128]{2,1,0:T(8,128)(2,1)S(1)}, u32[]{:S(2)}, u32[]{:S(2)}) async-start(bf16[16,128,128]{2,1,0:T(8,128)(2,1)} %y_modes.1), calls=%async_computation | async-start | bytes 1048576 | tf_op jit(solution)/shard_map/all_to_all | solution.py:379
  22.5 2.8 %copy-start.17 = (f32[4,2,32,32,64]{4,3,2,0,1:T(8,128)S(1)}, f32[4,2,32,32,64]{4,3,2,0,1:T(8,128)}, u32[]{:S(2)}) copy-start(f32[4,2,32,32,64]{4,3,2,0,1:T(8,128)} %convert_bitcast_fusion) | copy-start | bytes 6291460
  25.8 8.5 %copy-start.7 = (bf16[256,1024]{1,0:T(8,128)(2,1)S(1)}, bf16[256,1024]{1,0:T(8,128)(2,1)}, u32[]{:S(2)}) copy-start(bf16[256,1024]{1,0:T(8,128)(2,1)} %constant.27.clone.inverse_ref) | copy-start | bytes 1572868
  34.3 1.6 %copy-start.1 = (f32[4,32,32,128]{3,2,1,0:T(8,128)S(1)}, f32[4,32,32,128]{3,2,1,0:T(8,128)}, u32[]{:S(2)}) copy-start(f32[4,32,32,128]{3,2,1,0:T(8,128)} %get-tuple-element.8.crossed_ref) | copy-start | bytes 6291460
  35.9 1.2 %copy-start.6 = (bf16[2048,256]{1,0:T(8,128)(2,1)S(1)}, bf16[2048,256]{1,0:T(8,128)(2,1)}, u32[]{:S(2)}) copy-start(bf16[2048,256]{1,0:T(8,128)(2,1)} %constant.26.clone.forward_ref) | copy-start | bytes 3145732
  39.8 19.7 %all-to-all-start.1 = ((bf16[32,64,128]{2,1,0:T(8,128)(2,1)}), bf16[32,64,128]{2,1,0:T(8,128)(2,1)S(1)}, u32[]{:S(2)}, u32[]{:S(2)}) async-start(bf16[32,64,128]{2,1,0:T(8,128)(2,1)} %mix.1), calls=%async_computation.1 | async-start | bytes 1048576 | tf_op jit(solution)/shard_map/all_to_all | solution.py:385
  42.6 6.5 %collective-permute-start = (s32[1]{0:T(128)}, s32[1]{0:T(128)}, u32[]{:S(2)}, u32[]{:S(2)}) collective-permute-start(s32[1]{0:T(128)} %param.17), channel_id=1, source_target_pairs={{0,16},{16,0},{1,17},{17,1},{2,18},{18,2},{3,19},{19,3},{4,20},{20... | collective-permute-start | bytes 20 | tf_op jit(solution)/shard_map/ppermute | solution.py:373
  43.0 6.8 %copy-start.5 = (bf16[32,32,2,512]{3,2,1,0:T(2,128)(2,1)S(1)}, bf16[32,32,2,512]{3,2,1,0:T(2,128)(2,1)}, u32[]{:S(2)}) copy-start(bf16[32,32,2,512]{3,2,1,0:T(2,128)(2,1)} %param.13) | copy-start | bytes 6291460
  43.0 6.8 %copy-start.11 = (bf16[32,2,512]{2,1,0:T(2,128)(2,1)S(1)}, bf16[32,2,512]{2,1,0:T(2,128)(2,1)}, u32[]{:S(2)}) copy-start(bf16[32,2,512]{2,1,0:T(2,128)(2,1)} %param.14) | copy-start | bytes 196612
  43.0 6.8 %copy-start.13 = (f32[16]{0:T(128)S(1)}, f32[16]{0:T(128)}, u32[]{:S(2)}) copy-start(f32[16]{0:T(128)} %amplitude_ref.3) | copy-start | bytes 196
  43.0 6.8 %copy-start.15 = (f32[32]{0:T(128)S(1)}, f32[32]{0:T(128)}, u32[]{:S(2)}) copy-start(f32[32]{0:T(128)} %load_ref.3) | copy-start | bytes 388
  43.0 6.8 %copy-start.16 = (f32[32]{0:T(128)S(1)}, f32[32]{0:T(128)}, u32[]{:S(2)}) copy-start(f32[32]{0:T(128)} %bias_ref.1) | copy-start | bytes 388
  49.8 9.6 %copy-start.8 = (bf16[128,512]{1,0:T(8,128)(2,1)S(1)}, bf16[128,512]{1,0:T(8,128)(2,1)}, u32[]{:S(2)}) copy-start(bf16[128,512]{1,0:T(8,128)(2,1)} %constant.28.clone.table_ref) | copy-start | bytes 393220
  56.5 1.9 %copy-start.2 = (f32[2,2,8,256,128]{4,3,2,1,0:T(8,128)}, f32[2,2,8,256,128]{4,3,2,1,0:T(8,128)S(1)}, u32[]{:S(2)}) copy-start(f32[2,2,8,256,128]{4,3,2,1,0:T(8,128)S(1)} %pointwise.1.point_ref) | copy-start | bytes 12582916
  59.5 2.2 %copy-start.3 = (f32[2,2,8,256,128]{4,3,2,1,0:T(8,128)S(1)}, f32[2,2,8,256,128]{4,3,2,1,0:T(8,128)}, u32[]{:S(2)}) copy-start(f32[2,2,8,256,128]{4,3,2,1,0:T(8,128)} %copy-done.2) | copy-start | bytes 12582916

commit v2 on v1

--- a/solution.py
+++ b/solution.py
@@ -32,7 +32,7 @@
 
 def forward_y_table(modes_y, length_y):
     cos, sin = host_phases(np.arange(modes_y), np.arange(length_y), length_y)
-    return as_bf16(np.concatenate([cos, -sin], axis=0))
+    return as_bf16(2.0 * np.concatenate([cos, -sin], axis=0).astype(BF16).astype(np.float32))
 
 
 def inverse_y_table(modes_y, length_y, length_x, slabs):
@@ -75,120 +75,234 @@
     )
 
 
-def driven_field(base, forcing, strength):
-    return 2.0 * jnp.tanh(0.5 * (base.astype(F32) + strength * forcing))
-
-
-def y_modes_kernel(
-    index_ref, amplitude_ref, load_ref, base_ref, forcing_ref, table_ref, out_ref, cells, rows, modes
-):
-    group = pl.program_id(0)
-    width, cell_rows, _ = base_ref.shape
-    planes, y_blocks, slab_rows = Y_LAYOUT(cell_rows, table_ref.shape[1])
-    channels = load_ref.shape[0]
-    modes_y = table_ref.shape[0] // 2
-    amplitude = amplitude_ref[index_ref[0]]
-    forcing = forcing_ref[...].astype(F32)
-    span = planes * slab_rows
-    for c in range(width):
-        cells[c] = driven_field(base_ref[c], forcing, amplitude * load_ref[group * width + c])
-        for z in range(planes):
-            for j in range(y_blocks):
-                picked = cells[c, pl.ds(j * planes + z, slab_rows, stride=planes * y_blocks), :]
-                rows[
-                    pl.ds(c * span + z * slab_rows, slab_rows), pl.ds(j * LANES, LANES)
-                ] = picked.astype(BF16)
-    result = lax.dot_general(
-        table_ref[...], rows[...], (((1,), (1,)), ((), ())), preferred_element_type=F32
-    )
-    for t in range(width // 2):
-        tile = slice(t * LANES, (t + 1) * LANES)
-        pair = pair_halves(result[:modes_y, tile], result[modes_y:, tile])
-        for n in range(2):
-            modes[pl.ds(group * width + 2 * t + n, modes_y, stride=channels), :] = pair[n]
-
-    @pl.when(group == pl.num_programs(0) - 1)
-    def _():
-        block_rows = out_ref.shape[1]
-        for d in range(out_ref.shape[0]):
-            out_ref[d] = modes[pl.ds(d * block_rows, block_rows), :].astype(BF16)
-
-
-def Y_LAYOUT(cell_rows, length_y):
+def half_field(base, forcing, strength):
+    return jnp.tanh(0.5 * (base.astype(F32) + strength * forcing))
+
+
+def cell_layout(cell_rows, length_y):
     y_blocks = length_y // LANES
     planes = SUBLANES // y_blocks
     return planes, y_blocks, cell_rows // SUBLANES
 
 
+def in_hbm(*arrays):
+    return [pltpu.with_memory_space_constraint(a, pltpu.HBM) for a in arrays]
+
+
+def y_modes_kernel(
+    index,
+    amplitude_hbm,
+    load_hbm,
+    cells_hbm,
+    forcing_hbm,
+    table_hbm,
+    out_hbm,
+    amplitudes,
+    load,
+    cells,
+    forcing,
+    forcing_wide,
+    table,
+    field,
+    rows,
+    modes,
+    packed,
+    arrived,
+    sent,
+):
+    channels, cell_rows, _ = cells.shape
+    width = field.shape[1]
+    groups = channels // width
+    planes, y_blocks, slab_rows = cell_layout(cell_rows, table.shape[1])
+    modes_y = table.shape[0] // 2
+    span = planes * slab_rows
+    halves, slabs, half_rows, _ = packed.shape
+    half_channels = channels // halves
+    small = [
+        pltpu.make_async_copy(source, target, arrived.at[n])
+        for n, (source, target) in enumerate(
+            [
+                (amplitude_hbm, amplitudes),
+                (load_hbm, load),
+                (forcing_hbm, forcing),
+                (table_hbm, table),
+            ]
+        )
+    ]
+    large = [
+        pltpu.make_async_copy(
+            cells_hbm.at[pl.ds(g * width, width)], cells.at[pl.ds(g * width, width)], arrived.at[len(small) + g]
+        )
+        for g in range(groups)
+    ]
+    for copy in small[:3] + large[:1] + small[3:] + large[1:]:
+        copy.start()
+    for copy in small[:3]:
+        copy.wait()
+    amplitude = amplitudes[index[0]]
+    forcing_wide[...] = forcing[...].astype(F32)
+    small[3].wait()
+    leaving = []
+    for step in range(groups + 1):
+        if step < groups:
+            large[step].wait()
+            for c in range(width):
+                channel = step * width + c
+                field[step % 2, c] = half_field(cells[channel], forcing_wide[...], amplitude * load[channel])
+                for z in range(planes):
+                    for j in range(y_blocks):
+                        picked = field[step % 2, c, pl.ds(j * planes + z, slab_rows, stride=planes * y_blocks), :]
+                        rows[
+                            step % 2, pl.ds(c * span + z * slab_rows, slab_rows), pl.ds(j * LANES, LANES)
+                        ] = picked.astype(BF16)
+        if step > 0:
+            g = step - 1
+            result = lax.dot_general(
+                table[...], rows[g % 2], (((1,), (1,)), ((), ())), preferred_element_type=F32
+            )
+            for t in range(width // 2):
+                tile = slice(t * LANES, (t + 1) * LANES)
+                pair = pair_halves(result[:modes_y, tile], result[modes_y:, tile])
+                for n in range(2):
+                    half, c = divmod(g * width + 2 * t + n, half_channels)
+                    modes[half, pl.ds(c, modes_y, stride=half_channels), :] = pair[n]
+            if step * width % half_channels == 0:
+                half = g * width // half_channels
+                for d in range(slabs):
+                    packed[half, d] = modes[half, pl.ds(d * half_rows, half_rows), :].astype(BF16)
+                copy = pltpu.make_async_copy(
+                    packed.at[half], out_hbm.at[:, pl.ds(half * half_rows, half_rows), :], sent.at[half]
+                )
+                copy.start()
+                leaving.append(copy)
+    for copy in leaving:
+        copy.wait()
+
+
 def y_modes(amp_index, amplitudes, load, cells, forcing, slabs, modes_y, length_y):
     channels, cell_rows, _ = cells.shape
-    width = 4
+    width, halves = 4, 2
     block_rows = modes_y // slabs * channels
     table = forward_y_table(modes_y, length_y)
-    planes, y_blocks, slab_rows = Y_LAYOUT(cell_rows, length_y)
-    smem = pl.BlockSpec(memory_space=SMEM)
+    planes, _, slab_rows = cell_layout(cell_rows, length_y)
+    operands = in_hbm(amplitudes, load, cells, forcing, table)
+    anywhere = pl.BlockSpec(memory_space=pl.ANY)
     return pl.pallas_call(
         y_modes_kernel,
-        grid=(channels // width,),
-        in_specs=[
-            smem,
-            smem,
-            smem,
-            pl.BlockSpec((width, cell_rows, LANES), lambda g: (g, 0, 0)),
-            pl.BlockSpec((cell_rows, LANES), lambda g: (0, 0)),
-            pl.BlockSpec(table.shape, lambda g: (0, 0)),
-        ],
-        out_specs=pl.BlockSpec((slabs, block_rows, LANES), lambda g: (0, 0, 0)),
+        in_specs=[pl.BlockSpec(memory_space=SMEM)] + [anywhere] * len(operands),
+        out_specs=anywhere,
         out_shape=jax.ShapeDtypeStruct((slabs, block_rows, LANES), BF16),
         scratch_shapes=[
-            pltpu.VMEM((width, cell_rows, LANES), F32),
-            pltpu.VMEM((width * planes * slab_rows, length_y), BF16),
-            pltpu.VMEM((modes_y * channels, LANES), F32),
+            SMEM(amplitudes.shape, F32),
+            SMEM(load.shape, F32),
+            pltpu.VMEM(cells.shape, BF16),
+            pltpu.VMEM(forcing.shape, BF16),
+            pltpu.VMEM(forcing.shape, F32),
+            pltpu.VMEM(table.shape, BF16),
+            pltpu.VMEM((2, width, cell_rows, LANES), F32),
+            pltpu.VMEM((2, width * planes * slab_rows, length_y), BF16),
+            pltpu.VMEM((halves, modes_y * channels // halves, LANES), F32),
+            pltpu.VMEM((halves, slabs, block_rows // halves, LANES), BF16),
+            pltpu.SemaphoreType.DMA((4 + channels // width,)),
+            pltpu.SemaphoreType.DMA((halves,)),
         ],
-        compiler_params=pltpu.CompilerParams(vmem_limit_bytes=32 * 1024 * 1024),
+        compiler_params=pltpu.CompilerParams(vmem_limit_bytes=12 * 1024 * 1024),
         cost_estimate=pl.CostEstimate(
             flops=4 * modes_y * cells.size, bytes_accessed=4 * cells.size, transcendentals=cells.size
         ),
         name="y_modes",
-    )(amp_index, amplitudes, load, cells, forcing, table)
-
-
-def mix_kernel(
-    limit_ref, pencil_ref, forward_ref, straight_ref, crossed_ref, inverse_ref, out_ref, spectrum, turned, mixed
-):
+    )(amp_index, *operands)
+
+
+def prepare_kernel(weight_ref, forward_ref, inverse_ref, weights, forward_out, inverse_out, wide):
+    forward_out[...] = forward_ref[...]
+    inverse_out[...] = inverse_ref[...]
+    local_modes, parts, channels, _, _ = weight_ref.shape
+    for k in range(local_modes // 2):
+        for r in range(parts):
+            for o in range(channels):
+                pair = [weight_ref[2 * k + n, r, o].astype(F32) for n in range(2)]
+                wide[k, r, pl.ds(o, channels, stride=channels), :] = jnp.concatenate(pair, axis=1)
+    weights[...] = wide[...].astype(BF16)
+
+
+def prepare(spectral_weight, length_x, slabs, planes):
+    local_modes, parts, channels, _, modes_x = spectral_weight.shape
+    forward = forward_x_table(modes_x, length_x, slabs, planes)
+    inverse = inverse_x_table(modes_x, length_x, slabs, planes)
+    wide = (local_modes // 2, parts, channels * channels, 2 * modes_x)
+    vmem = pl.BlockSpec(memory_space=pltpu.VMEM)
+    return pl.pallas_call(
+        prepare_kernel,
+        in_specs=[vmem] * 3,
+        out_specs=[vmem] * 3,
+        out_shape=[
+            pltpu.VMEM(wide, BF16),
+            pltpu.VMEM(forward.shape, BF16),
+            pltpu.VMEM(inverse.shape, BF16),
+        ],
+        scratch_shapes=[pltpu.VMEM(wide, F32)],
+        compiler_params=pltpu.CompilerParams(vmem_limit_bytes=16 * 1024 * 1024),
+        cost_estimate=pl.CostEstimate(
+            flops=4 * spectral_weight.size, bytes_accessed=10 * spectral_weight.size, transcendentals=0
+        ),
+        name="prepare",
+    )(*in_hbm(spectral_weight, forward, inverse))
+
+
+def mix_kernel(limit_ref, pencil_ref, forward_ref, weight_ref, inverse_ref, out_ref, spectrum, mixed):
     slabs, block_rows, _ = pencil_ref.shape
-    local_modes, channels, _, width = straight_ref.shape
+    pairs, _, rows, width = weight_ref.shape
+    local_modes = 2 * pairs
+    channels = block_rows // local_modes
     planes = forward_ref.shape[1] // width
     groups = channels // SUBLANES
+    half_channels = channels // 2
+    block = SUBLANES * 2 * local_modes
     pencil = jnp.concatenate([pencil_ref[s] for s in range(slabs)], axis=1)
     result = jnp.dot(pencil, forward_ref[...], preferred_element_type=F32)
     for z in range(planes):
-        part = result[:, z * width : (z + 1) * width]
-        spectrum[z] = part
-        turned[z] = half_turn(part)
+        for half in range(2):
+            for k in range(pairs):
+                start = (half * local_modes + 2 * k) * half_channels
+                both = [
+                    result[start + n * half_channels : start + (n + 1) * half_channels, z * width : (z + 1) * width]
+                    for n in range(2)
+                ]
+                parts = pair_halves(*both)
+                for r in range(2):
+                    spectrum[k, z, r, pl.ds(half * half_channels, half_channels), :] = parts[r]
     low = low_half((SUBLANES, width))
-    block = SUBLANES * 2 * local_modes
-    for k in range(local_modes):
-        keep = jnp.where(limit_ref[0] > k, 1.0, 0.0).astype(F32)
-        sums = [[jnp.zeros((SUBLANES, width), F32) for _ in range(groups)] for _ in range(planes)]
+    for k in range(pairs):
+        keep = [jnp.where(limit_ref[0] > 2 * k + n, 1.0, 0.0).astype(F32) for n in range(2)]
+        sums = [[[None, None] for _ in range(groups)] for _ in range(planes)]
         for i in range(channels):
-            row = pl.ds(k * channels + i, 1)
-            plain = [jnp.broadcast_to(spectrum[z, row, :], (SUBLANES, width)) for z in range(planes)]
-            other = [jnp.broadcast_to(turned[z, row, :], (SUBLANES, width)) for z in range(planes)]
+            values = [
+                [jnp.broadcast_to(spectrum[k, z, r, pl.ds(i, 1), :], (SUBLANES, width)) for r in range(2)]
+                for z in range(planes)
+            ]
+            weights = [weight_ref[k, r, pl.ds(i * channels, channels), :].astype(F32) for r in range(2)]
             for g in range(groups):
-                straight = straight_ref[k, i, pl.ds(g * SUBLANES, SUBLANES), :]
-                crossed = crossed_ref[k, i, pl.ds(g * SUBLANES, SUBLANES), :]
+                real, imag = (w[g * SUBLANES : (g + 1) * SUBLANES] for w in weights)
                 for z in range(planes):
-                    sums[z][g] = sums[z][g] + (straight * plain[z] + crossed * other[z])
+                    terms = (
+                        real * values[z][0] - imag * values[z][1],
+                        real * values[z][1] + imag * values[z][0],
+                    )
+                    for r in range(2):
+                        old = sums[z][g][r]
+                        sums[z][g][r] = terms[r] if old is None else old + terms[r]
         for z in range(planes):
             for g in range(groups):
-                kept = sums[z][g] * keep
-                swapped = half_turn(kept)
-                start = g * block + k
-                mixed[z, pl.ds(start, SUBLANES, stride=2 * local_modes), :] = kept
-                mixed[z, pl.ds(start + local_modes, SUBLANES, stride=2 * local_modes), :] = jnp.where(
-                    low, swapped, -swapped
-                )
+                modes = pair_halves(*sums[z][g])
+                for n in range(2):
+                    kept = modes[n] * keep[n]
+                    swapped = half_turn(kept)
+                    start = g * block + 2 * k + n
+                    mixed[z, pl.ds(start, SUBLANES, stride=2 * local_modes), :] = kept
+                    mixed[z, pl.ds(start + local_modes, SUBLANES, stride=2 * local_modes), :] = jnp.where(
+                        low, swapped, -swapped
+                    )
     left = jnp.concatenate([mixed[z].astype(BF16) for z in range(planes)], axis=1)
     back = jnp.dot(left, inverse_ref[...], preferred_element_type=F32)
     members = out_ref.shape[0] // slabs
@@ -198,146 +312,158 @@
             start = 2 * h * block
             pair = pair_halves(back[start : start + block, tile], back[start + block : start + 2 * block, tile])
             for n in range(2):
-                out_ref[h * slabs + 2 * t + n] = pair[n].astype(BF16)
-
-
-def mix(limit, pencil, straight, crossed, length_x, planes, members):
+                out_ref[(2 * t + n) * members + h] = pair[n].astype(BF16)
+
+
+def mix(limit, pencil, weights, forward, inverse, members):
     slabs, block_rows, _ = pencil.shape
-    local_modes, channels, _, width = straight.shape
-    modes_x = width // 2
-    forward = forward_x_table(modes_x, length_x, slabs, planes)
-    inverse = inverse_x_table(modes_x, length_x, slabs, planes)
+    pairs, _, _, width = weights.shape
+    channels = block_rows // (2 * pairs)
+    planes = forward.shape[1] // width
     vmem = pl.BlockSpec(memory_space=pltpu.VMEM)
-    block = SUBLANES * 2 * local_modes
+    block = SUBLANES * 4 * pairs
     return pl.pallas_call(
         mix_kernel,
-        in_specs=[pl.BlockSpec(memory_space=SMEM)] + [vmem] * 5,
+        in_specs=[pl.BlockSpec(memory_space=SMEM)] + [vmem] * 4,
         out_specs=vmem,
         out_shape=jax.ShapeDtypeStruct((members * slabs, block, LANES), BF16),
         scratch_shapes=[
-            pltpu.VMEM((planes, block_rows, width), F32),
-            pltpu.VMEM((planes, block_rows, width), F32),
+            pltpu.VMEM((pairs, planes, 2, channels, width), F32),
             pltpu.VMEM((planes, channels // SUBLANES * block, width), F32),
         ],
-        compiler_params=pltpu.CompilerParams(vmem_limit_bytes=40 * 1024 * 1024),
+        compiler_params=pltpu.CompilerParams(vmem_limit_bytes=12 * 1024 * 1024),
         cost_estimate=pl.CostEstimate(
-            flops=2 * block_rows * forward.size, bytes_accessed=8 * straight.size, transcendentals=0
+            flops=2 * block_rows * forward.size, bytes_accessed=8 * weights.size, transcendentals=0
         ),
         name="mix",
-    )(limit, pencil, forward, straight, crossed, inverse)
+    )(limit, pencil, forward, weights, inverse)
 
 
 def pointwise_kernel(
-    place_ref, index_ref, amplitude_ref, load_ref, bias_ref, base_ref, forcing_ref, weight_ref, out_ref
+    place_ref, index_ref, amplitude_ref, load_ref, bias_ref, weight_ref, base_ref, forcing_ref, out_ref, spread
 ):
     channels, depth, _ = base_ref.shape
     members = index_ref.shape[0]
+    out_channels = channels // members
     me = place_ref[0]
+
+    @pl.when(pl.program_id(0) == 0)
+    def _():
+        tall = (out_channels * depth, channels)
+        wide = (channels, channels * depth)
+        row_of = lax.broadcasted_iota(jnp.int32, tall, 0) // depth + me * out_channels
+        pick_rows = (row_of == lax.broadcasted_iota(jnp.int32, tall, 1)).astype(BF16)
+        column_of = lax.broadcasted_iota(jnp.int32, wide, 1) // depth
+        pick_columns = (column_of == lax.broadcasted_iota(jnp.int32, wide, 0)).astype(BF16)
+        picked = jnp.dot(pick_rows, weight_ref[...], preferred_element_type=F32).astype(BF16)
+        full = jnp.dot(picked, pick_columns, preferred_element_type=F32)
+        same = lax.broadcasted_iota(jnp.int32, full.shape, 0) % depth == (
+            lax.broadcasted_iota(jnp.int32, full.shape, 1) % depth
+        )
+        spread[...] = jnp.where(same, 2.0 * full, 0.0).astype(BF16)
+
     forcing = forcing_ref[...].astype(F32)
     fields = []
     for m in range(members):
         amplitude = amplitude_ref[index_ref[lax.rem(me - m + members, members)]]
-        parts = [
-            driven_field(base_ref[c], forcing, amplitude * load_ref[c]).astype(BF16) for c in range(channels)
-        ]
+        parts = [half_field(base_ref[c], forcing, amplitude * load_ref[c]).astype(BF16) for c in range(channels)]
         fields.append(jnp.concatenate(parts, axis=0))
-    result = jnp.dot(weight_ref[...], jnp.concatenate(fields, axis=1), preferred_element_type=F32)
+    result = jnp.dot(spread[...], jnp.concatenate(fields, axis=1), preferred_element_type=F32)
     _, outer, inner, _, _ = out_ref.shape
+    start = pl.program_id(0) * depth
     for a in range(outer):
         for b in range(inner):
             o = a * inner + b
-            bias = bias_ref[me * outer * inner + o]
+            bias = bias_ref[me * out_channels + o]
             for m in range(members):
-                out_ref[m, a, b] = result[o * depth : (o + 1) * depth, m * LANES : (m + 1) * LANES] + bias
-
-
-def pointwise(place, indices, amplitudes, load, bias, cells, forcing, weight):
+                cells = result[o * depth : (o + 1) * depth, m * LANES : (m + 1) * LANES] + bias
+                out_ref[m, a, b, pl.ds(pl.multiple_of(start, depth), depth), :] = cells.astype(BF16)
+
+
+def pointwise(place, indices, amplitudes, load, bias, weight, cells, forcing):
     channels, cell_rows, _ = cells.shape
     members = indices.shape[0]
     depth = 2 * SUBLANES
     inner = SUBLANES
     outer = channels // members // inner
-    spread = (weight[:, None, :, None] * jnp.eye(depth, dtype=BF16)[None, :, None, :]).reshape(
-        weight.shape[0] * depth, channels * depth
-    )
+    spread = (channels // members * depth, channels * depth)
     smem = pl.BlockSpec(memory_space=SMEM)
     return pl.pallas_call(
         pointwise_kernel,
         grid=(cell_rows // depth,),
         in_specs=[smem] * 5
         + [
+            pl.BlockSpec(weight.shape, lambda r: (0, 0)),
             pl.BlockSpec((channels, depth, LANES), lambda r: (0, r, 0)),
             pl.BlockSpec((depth, LANES), lambda r: (r, 0)),
-            pl.BlockSpec(spread.shape, lambda r: (0, 0)),
         ],
-        out_specs=pl.BlockSpec((members, outer, inner, depth, LANES), lambda r: (0, 0, 0, r, 0)),
-        out_shape=jax.ShapeDtypeStruct((members, outer, inner, cell_rows, LANES), F32),
-        compiler_params=pltpu.CompilerParams(vmem_limit_bytes=32 * 1024 * 1024),
+        out_specs=pl.BlockSpec(memory_space=pltpu.VMEM),
+        out_shape=pltpu.VMEM((members, outer, inner, cell_rows, LANES), BF16),
+        scratch_shapes=[pltpu.VMEM(spread, BF16)],
+        compiler_params=pltpu.CompilerParams(vmem_limit_bytes=12 * 1024 * 1024),
         cost_estimate=pl.CostEstimate(
-            flops=4 * spread.size * members * cell_rows // depth * LANES,
+            flops=4 * spread[0] * spread[1] * members * cell_rows // depth * LANES,
             bytes_accessed=8 * cells.size,
             transcendentals=members * cells.size,
         ),
         name="pointwise",
-    )(place, indices, amplitudes, load, bias, cells, forcing, spread)
-
-
-def layer_kernel(back_ref, table_ref, point_ref, out_ref, columns, spectral):
-    step = pl.program_id(0)
-    members, outer, _, cell_rows, _ = point_ref.shape
+    )(place, indices, amplitudes, load, bias, weight, *in_hbm(cells, forcing))
+
+
+def layer_kernel(back_ref, table_ref, points, out_hbm, columns, spectral, result, sent):
+    members, outer, inner, cell_rows, _ = points.shape
     sources, block_rows, _ = back_ref.shape
     slabs = sources // members
-    inner = columns.shape[0]
     depth = block_rows // inner
-    planes, y_blocks, slab_rows = Y_LAYOUT(cell_rows, table_ref.shape[1])
-
-    @pl.when(step == 0)
-    def _():
+    planes, y_blocks, slab_rows = cell_layout(cell_rows, table_ref.shape[1])
+    leaving = [pltpu.make_async_copy(result.at[:, b], out_hbm.at[:, b], sent.at[b]) for b in range(inner)]
+    for m in range(members):
+        for s in range(slabs):
+            block = back_ref[s * members + m].astype(F32)
+            for b in range(inner):
+                columns[b, m, pl.ds(s * depth, depth), :] = block[b * depth : (b + 1) * depth]
+    for b in range(inner):
+        turn = b % 2
         for m in range(members):
-            for s in range(slabs):
-                block = back_ref[m * slabs + s].astype(F32)
-                for b in range(inner):
-                    columns[b, m, pl.ds(s * depth, depth), :] = block[b * depth : (b + 1) * depth]
-
-    for m in range(members):
-        left = columns[step, m].astype(BF16)
-        values = lax.dot_general(
-            left, table_ref[...], (((0,), (0,)), ((), ())), preferred_element_type=F32
-        )
+            values = lax.dot_general(
+                columns[b, m].astype(BF16), table_ref[...], (((0,), (0,)), ((), ())), preferred_element_type=F32
+            )
+            for a in range(outer):
+                for z in range(planes):
+                    start = (a * planes + z) * slab_rows
+                    for j in range(y_blocks):
+                        spectral[
+                            turn, m, a, pl.ds(j * planes + z, slab_rows, stride=planes * y_blocks), :
+                        ] = values[start : start + slab_rows, j * LANES : (j + 1) * LANES]
         for a in range(outer):
-            for z in range(planes):
-                start = (a * planes + z) * slab_rows
-                for j in range(y_blocks):
-                    spectral[m, a, pl.ds(j * planes + z, slab_rows, stride=planes * y_blocks), :] = values[
-                        start : start + slab_rows, j * LANES : (j + 1) * LANES
-                    ]
-    for a in range(outer):
-        total = None
-        for m in range(members):
-            value = jax.nn.gelu(point_ref[m, a, 0] + spectral[m, a], approximate=True)
-            total = value if total is None else total + value
-        out_ref[a, 0] = (total * (1.0 / members)).astype(BF16)
+            total = None
+            for m in range(members):
+                value = jax.nn.gelu(points[m, a, b].astype(F32) + spectral[turn, m, a], approximate=True)
+                total = value if total is None else total + value
+            result[a, b] = (total * (1.0 / members)).astype(BF16)
+        leaving[b].start()
+    for copy in leaving:
+        copy.wait()
 
 
 def layer(back, points, length_x, length_y, modes_y):
     members, outer, inner, cell_rows, _ = points.shape
     slabs = back.shape[0] // members
     table = inverse_y_table(modes_y, length_y, length_x, slabs)
+    vmem = pl.BlockSpec(memory_space=pltpu.VMEM)
+    anywhere = pl.BlockSpec(memory_space=pl.ANY)
     return pl.pallas_call(
         layer_kernel,
-        grid=(inner,),
-        in_specs=[
-            pl.BlockSpec(back.shape, lambda b: (0, 0, 0)),
-            pl.BlockSpec(table.shape, lambda b: (0, 0)),
-            pl.BlockSpec((members, outer, 1, cell_rows, LANES), lambda b: (0, 0, b, 0, 0)),
-        ],
-        out_specs=pl.BlockSpec((outer, 1, cell_rows, LANES), lambda b: (0, b, 0, 0)),
-        out_shape=jax.ShapeDtypeStruct((outer, inner, cell_rows, LANES), BF16),
+        in_specs=[vmem, vmem, vmem],
+        out_specs=anywhere,
+        out_shape=pltpu.HBM((outer, inner, cell_rows, LANES), BF16),
         scratch_shapes=[
             pltpu.VMEM((inner, members, 2 * modes_y, LANES), F32),
-            pltpu.VMEM((members, outer, cell_rows, LANES), F32),
+            pltpu.VMEM((2, members, outer, cell_rows, LANES), F32),
+            pltpu.VMEM((outer, inner, cell_rows, LANES), BF16),
+            pltpu.SemaphoreType.DMA((inner,)),
         ],
-        compiler_params=pltpu.CompilerParams(vmem_limit_bytes=32 * 1024 * 1024),
+        compiler_params=pltpu.CompilerParams(vmem_limit_bytes=16 * 1024 * 1024),
         cost_estimate=pl.CostEstimate(
             flops=4 * modes_y * points.size, bytes_accessed=5 * points.size, transcendentals=points.size
         ),
@@ -377,14 +503,11 @@
     out_channels = channels // members
     packed = y_modes(amp_index, amplitudes, load, cells, force, slabs, modes_y, length_y)
     pencil = lax.all_to_all(packed, "slab", split_axis=0, concat_axis=0, tiled=True)
-    weights = spectral_weight.transpose(0, 2, 4, 3, 1).astype(F32)
-    straight = jnp.concatenate([weights[:, 0], weights[:, 0]], axis=-1)
-    crossed = jnp.concatenate([-weights[:, 1], weights[:, 1]], axis=-1)
+    weights, forward, inverse = prepare(spectral_weight.transpose(0, 2, 3, 4, 1), length_x, slabs, planes)
     limit = mode_count - lax.axis_index("slab") * local_modes
-    back = mix(limit, pencil, straight, crossed, length_x, planes, members)
-    back = lax.all_to_all(back, ("member", "slab"), split_axis=0, concat_axis=0, tiled=True)
-    weight = lax.dynamic_slice_in_dim(point_weight, me * out_channels, out_channels, 0)
-    points = pointwise(me.reshape(1), indices, amplitudes, load, point_bias, cells, force, weight)
+    back = mix(limit, pencil, weights, forward, inverse, members)
+    back = lax.all_to_all(back, ("slab", "member"), split_axis=0, concat_axis=0, tiled=True)
+    points = pointwise(me.reshape(1), indices, amplitudes, load, point_bias, point_weight, cells, force)
     result = layer(back, points, length_x, length_y, modes_y)
     result = result.reshape(out_channels, slab_rows, y_blocks, planes, LANES).transpose(0, 1, 3, 2, 4)
     return result.reshape(out_channels, slab_rows, planes, length_y)

time: 67.3 us -> 53.7 us (0.80)
  local copies, waits for them, and re-layouts: 17.4 us -> 0.02 us
  other arithmetic: 9.4 us -> 0.69 us
  waiting for transfers between devices: 7 us -> 13.9 us
  Pallas kernels: 19.9 us -> 25.7 us
    unnamed x38 -> x10, local copies, waits for them, and re-layouts: 12.5 us -> 0.02 us
    mul x1 -> x0, local copies, waits for them, and re-layouts: 4.51 us -> none  [pointwise(): weight[:, None, :, None] * jnp.eye(depth, dtype=BF16)[None, :, None, :]]
    all_to_all x1, waiting for transfers between devices: 6.02 us -> 10.2 us  [fast_local(): lax.all_to_all(packed, 'slab', split_axis=0, concat_axis=0, tiled=True)]
    pallas_call x1, Pallas kernels: 6.68 us -> 10.9 us  [pointwise(): pl.pallas_call(pointwise_kernel, grid=(cell_rows // depth,), in_specs=[sm...]
    convert_element_type x2 -> x0, other arithmetic: 2.7 us -> none  [the longest x1 2.69 us: fast_local(): weights = spectral_weight.transpose(0, 2, 4, 3, 1).astype(F32)]
    concatenate x1 -> x0, other arithmetic: 2.48 us -> none  [fast_local(): straight = jnp.concatenate([weights[:, 0], weights[:, 0]], axis=-1)]
    neg x1 -> x0, other arithmetic: 1.97 us -> none  [fast_local(): crossed = jnp.concatenate([-weights[:, 1], weights[:, 1]], axis=-1)]
    pallas_call x2 -> x3, Pallas kernels: 10.6 us -> 12.3 us  [the longest x1 5.12 us: y_modes(): pl.pallas_call(y_modes_kernel, in_specs=[pl.BlockSpec(memory_space=SMEM)]...]
  transfers between devices with their start and end apart: 3 -> 3, of which waited for: 2 -> 3; matrix products, arithmetic and copies ran while one was open for 22% -> 1% of each run, Pallas kernels for 10% -> 28%
where the time goes in v2:
time: 53.7 us; the launch traced here: 53.2 us
  Pallas kernels  25.7 us (48%)
  waiting for transfers between devices  13.9 us (26%)
  starting transfers between devices  11.5 us (21%)
  between operations  1.37 us (3%)
  other arithmetic  0.69 us (1%)
    pallas_call x1, Pallas kernels, pointwise(): pl.pallas_call(pointwise_kernel, grid=(cell_rows // depth,), in_specs=[sm...  10.9 us
    all_to_all x1, waiting for transfers between devices, fast_local(): lax.all_to_all(packed, 'slab', split_axis=0, concat_axis=0, tiled=True)  10.2 us
    all_to_all x1, starting transfers between devices, fast_local(): lax.all_to_all(packed, 'slab', split_axis=0, concat_axis=0, tiled=True)  8.32 us
    pallas_call x1, Pallas kernels, y_modes(): pl.pallas_call(y_modes_kernel, in_specs=[pl.BlockSpec(memory_space=SMEM)]...  5.12 us
    pallas_call x1, Pallas kernels, prepare(): pl.pallas_call(prepare_kernel, in_specs=[vmem] * 3, out_specs=[vmem] * 3,...  4.26 us
    pallas_call x1, Pallas kernels, layer(): pl.pallas_call(layer_kernel, in_specs=[vmem, vmem, vmem], out_specs=anywh...  2.95 us
    all_to_all x1, starting transfers between devices, fast_local(): lax.all_to_all(back, ('slab', 'member'), split_axis=0, concat_axis=0, til...  2.88 us
    all_to_all x1, waiting for transfers between devices, fast_local(): lax.all_to_all(back, ('slab', 'member'), split_axis=0, concat_axis=0, til...  2.66 us
  transfers between devices with their start and end apart: 3, of which 3 were waited for; matrix products, arithmetic and copies ran while one was open for 1% of the time, Pallas kernels for 28%

profile of v2, /device:TPU:0, one launch (start us, length us, event | category | flops | bytes accessed | tf_op | source)
XLA Modules:
  0.0 53.2 jit_solution(14621986447050201098)
XLA Ops:
  0.7 5.1 %y_modes.1 = bf16[16,128,128]{2,1,0:T(8,128)(2,1)} custom-call(s32[1]{0:T(128)S(6)} %copy.17.index, f32[16]{0:T(128)} %amplitude_ref.1, f32[32]{0:T(128)} %load_ref.1, bf16[32,256,128]{2,1,0:T(8,128)(2,1)} %bitcast.19, bf16[256,128]{1,0:T(8,128)(2,1)} %bitcast.21, bf16[128,512]{1,0:T(8,128)(2,1)} %constant.19.clone.table_hbm), custom_call_target="tpu_custom_call" | custom-call | flops 268435456 | bytes 4194304 | tf_op jit(solution)/shard_map/y_modes/pallas_call | solution.py:190
  5.8 8.3 %all-to-all-start = ((bf16[16,128,128]{2,1,0:T(8,128)(2,1)}), bf16[16,128,128]{2,1,0:T(8,128)(2,1)S(1)}, u32[]{:S(2)}, u32[]{:S(2)}) async-start(bf16[16,128,128]{2,1,0:T(8,128)(2,1)} %y_modes.1), calls=%async_computation | async-start | bytes 1048576 | tf_op jit(solution)/shard_map/all_to_all | solution.py:505
  14.8 4.3 %prepare.1 = (bf16[2,2,1024,128]{3,2,1,0:T(8,128)(2,1)S(1)}, bf16[2048,256]{1,0:T(8,128)(2,1)S(1)}, bf16[256,1024]{1,0:T(8,128)(2,1)S(1)}) custom-call(bf16[4,2,32,32,64]{4,3,2,1,0:T(8,128)(2,1)} %bitcast.18, bf16[2048,256]{1,0:T(8,128)(2,1)} %constant.20.clone.forward_ref, bf16[256,1024]{1,0:T(8,128)(2,1)} %constant.21.clone.inverse_ref), custom_call_target="tpu_custom_call" | custom-call | flops 2097152 | bytes 5242880 | tf_op jit(solution)/shard_map/prepare/pallas_call | solution.py:235
  19.0 10.2 %all-to-all-done.pencil_ref = bf16[16,128,128]{2,1,0:T(8,128)(2,1)S(1)} async-done(((bf16[16,128,128]{2,1,0:T(8,128)(2,1)}), bf16[16,128,128]{2,1,0:T(8,128)(2,1)S(1)}, u32[]{:S(2)}, u32[]{:S(2)}) %all-to-all-start) | async-done | bytes 524320 | tf_op jit(solution)/shard_map/all_to_all | solution.py:505
  29.3 0.0 copy-start.1
  29.3 0.0 copy-start.2
  29.3 0.0 copy-start.3
  29.3 0.0 copy-start.4
  29.3 2.5 %mix.1 = bf16[32,64,128]{2,1,0:T(8,128)(2,1)} custom-call(s32[1]{0:T(128)S(6)} %sub.7.limit_ref, bf16[16,128,128]{2,1,0:T(8,128)(2,1)S(1)} %all-to-all-done.pencil_ref, bf16[2048,256]{1,0:T(8,128)(2,1)S(1)} %get-tuple-element.8.forward_ref, bf16[2,2,1024,128]{3,2,1,0:T(8,128)(2,1)S(1)} %get-tuple-element.9.weight_ref, ...), custom_call_target="tpu_custom_call" | custom-call | flops 134217728 | bytes 4194304 | tf_op jit(solution)/shard_map/mix/pallas_call | solution.py:325
  31.8 2.9 %all-to-all-start.1 = ((bf16[32,64,128]{2,1,0:T(8,128)(2,1)}), bf16[32,64,128]{2,1,0:T(8,128)(2,1)S(1)}, u32[]{:S(2)}, u32[]{:S(2)}) async-start(bf16[32,64,128]{2,1,0:T(8,128)(2,1)} %mix.1), calls=%async_computation.1 | async-start | bytes 1048576 | tf_op jit(solution)/shard_map/all_to_all | solution.py:509
  34.7 0.3 collective-permute-start
  35.0 1.0 %collective-permute-done = s32[1]{0:T(128)} collective-permute-done((s32[1]{0:T(128)}, s32[1]{0:T(128)}, u32[]{:S(2)}, u32[]{:S(2)}) %collective-permute-start) | collective-permute-done | bytes 36 | tf_op jit(solution)/shard_map/ppermute | solution.py:499
  36.0 0.7 %pad_add_fusion.index_ref = s32[2]{0:T(128)S(1)} fusion(s32[1]{0:T(128)} %collective-permute-done, s32[1]{0:T(128)S(6)} %copy.17.index), kind=kLoop, calls=%fused_computation | loop fusion | flops 2 | bytes 16 | tf_op jit(solution)/shard_map/concatenate | solution.py:496
  36.7 0.0 copy-done.1
  36.7 0.0 copy-done.2
  36.7 0.0 copy-done.3
  36.7 0.0 copy-done.4
  36.7 0.0 copy-start
  36.7 10.9 %pointwise.1.points = bf16[2,2,8,256,128]{4,3,2,1,0:T(8,128)(2,1)S(1)} custom-call(s32[1]{0:T(128)} %bitcast.8.place_ref, s32[2]{0:T(128)S(1)} %pad_add_fusion.index_ref, f32[16]{0:T(128)S(1)} %copy-done.1, f32[32]{0:T(128)S(1)} %copy-done.2, f32[32]{0:T(128)S(1)} %copy-done.4, bf16[32,32]{1,0:T(8,128)(2,1)S(1)} %copy-done.3, ...), custom_call_target="tpu_custom_call" | custom-call | flops 2147483648 | bytes 8388608 | tf_op jit(solution)/shard_map/pointwise/pallas_call | solution.py:391
  47.6 2.7 %all-to-all-done.1.back_ref = bf16[32,64,128]{2,1,0:T(8,128)(2,1)S(1)} async-done(((bf16[32,64,128]{2,1,0:T(8,128)(2,1)}), bf16[32,64,128]{2,1,0:T(8,128)(2,1)S(1)}, u32[]{:S(2)}, u32[]{:S(2)}) %all-to-all-start.1) | async-done | bytes 524320 | tf_op jit(solution)/shard_map/all_to_all | solution.py:509
  50.2 0.0 copy-done
  50.2 3.0 %layer.1 = bf16[2,8,256,128]{3,2,1,0:T(8,128)(2,1)} custom-call(bf16[32,64,128]{2,1,0:T(8,128)(2,1)S(1)} %all-to-all-done.1.back_ref, bf16[128,512]{1,0:T(8,128)(2,1)S(1)} %copy-done, bf16[2,2,8,256,128]{4,3,2,1,0:T(8,128)(2,1)S(1)} %pointwise.1.points), custom_call_target="tpu_custom_call" | custom-call | flops 268435456 | bytes 5242880 | tf_op jit(solution)/shard_map/layer/pallas_call | solution.py:455
Async XLA Ops:
  5.8 23.5 %all-to-all-start = ((bf16[16,128,128]{2,1,0:T(8,128)(2,1)}), bf16[16,128,128]{2,1,0:T(8,128)(2,1)S(1)}, u32[]{:S(2)}, u32[]{:S(2)}) async-start(bf16[16,128,128]{2,1,0:T(8,128)(2,1)} %y_modes.1), calls=%async_computation | async-start | bytes 1048576 | tf_op jit(solution)/shard_map/all_to_all | solution.py:505
  29.3 7.4 %copy-start.1 = (f32[16]{0:T(128)S(1)}, f32[16]{0:T(128)}, u32[]{:S(2)}) copy-start(f32[16]{0:T(128)} %amplitude_ref.1) | copy-start | bytes 196
  29.3 7.4 %copy-start.2 = (f32[32]{0:T(128)S(1)}, f32[32]{0:T(128)}, u32[]{:S(2)}) copy-start(f32[32]{0:T(128)} %load_ref.1) | copy-start | bytes 388
  29.3 7.4 %copy-start.3 = (bf16[32,32]{1,0:T(8,128)(2,1)S(1)}, bf16[32,32]{1,0:T(8,128)(2,1)}, u32[]{:S(2)}) copy-start(bf16[32,32]{1,0:T(8,128)(2,1)} %weight_ref.1) | copy-start | bytes 6148
  29.3 7.4 %copy-start.4 = (f32[32]{0:T(128)S(1)}, f32[32]{0:T(128)}, u32[]{:S(2)}) copy-start(f32[32]{0:T(128)} %bias_ref.1) | copy-start | bytes 388
  31.8 18.4 %all-to-all-start.1 = ((bf16[32,64,128]{2,1,0:T(8,128)(2,1)}), bf16[32,64,128]{2,1,0:T(8,128)(2,1)S(1)}, u32[]{:S(2)}, u32[]{:S(2)}) async-start(bf16[32,64,128]{2,1,0:T(8,128)(2,1)} %mix.1), calls=%async_computation.1 | async-start | bytes 1048576 | tf_op jit(solution)/shard_map/all_to_all | solution.py:509
  34.7 1.3 %collective-permute-start = (s32[1]{0:T(128)}, s32[1]{0:T(128)}, u32[]{:S(2)}, u32[]{:S(2)}) collective-permute-start(s32[1]{0:T(128)} %param.17), channel_id=1, source_target_pairs={{0,16},{16,0},{1,17},{17,1},{2,18},{18,2},{3,19},{19,3},{4,20},{20... | collective-permute-start | bytes 20 | tf_op jit(solution)/shard_map/ppermute | solution.py:499
  36.7 13.5 %copy-start = (bf16[128,512]{1,0:T(8,128)(2,1)S(1)}, bf16[128,512]{1,0:T(8,128)(2,1)}, u32[]{:S(2)}) copy-start(bf16[128,512]{1,0:T(8,128)(2,1)} %constant.22.clone.table_ref) | copy-start | bytes 393220

commit v3 on v2

--- a/solution.py
+++ b/solution.py
@@ -11,6 +11,8 @@
 TWO_PI = 2.0 * math.pi
 LANES = 128
 SUBLANES = 8
+FORCING_ROWS = 64
+PART_ROWS = SUBLANES * SUBLANES // 2
 SMEM = pltpu.SMEM
 F32 = jnp.float32
 BF16 = jnp.bfloat16
@@ -30,9 +32,16 @@
     return jnp.asarray(table.astype(BF16))
 
 
-def forward_y_table(modes_y, length_y):
+def by_owner(table, slabs):
+    modes, length = table.shape
+    local = modes // slabs
+    return table.reshape(2, slabs // 2, local, length).transpose(1, 0, 2, 3)
+
+
+def forward_y_table(modes_y, length_y, slabs):
     cos, sin = host_phases(np.arange(modes_y), np.arange(length_y), length_y)
-    return as_bf16(2.0 * np.concatenate([cos, -sin], axis=0).astype(BF16).astype(np.float32))
+    table = np.stack([by_owner(cos, slabs), by_owner(-sin, slabs)], axis=0)
+    return as_bf16(2.0 * table.astype(BF16).astype(np.float32).reshape(2 * modes_y, length_y))
 
 
 def inverse_y_table(modes_y, length_y, length_x, slabs):
@@ -47,9 +56,9 @@
 def forward_x_table(modes_x, length_x, slabs, planes):
     cos, sin = host_phases(first_frequencies(modes_x, length_x), np.arange(length_x), length_x)
     whole = np.array([[cos, -sin], [sin, cos]])
-    whole = whole.reshape(2, 2, modes_x, slabs, length_x // slabs)
-    table = np.einsum("abqsx,zw->sazxwbq", whole, np.eye(planes, dtype=np.float32))
-    return as_bf16(table.reshape(2 * planes * length_x, planes * 2 * modes_x))
+    whole = whole.reshape(2, 2, modes_x, 2, slabs // 2, length_x // slabs)
+    table = np.einsum("abqhsx,zw->hsazxwbq", whole, np.eye(planes, dtype=np.float32))
+    return as_bf16(table.reshape(2, planes * length_x, planes * 2 * modes_x))
 
 
 def inverse_x_table(modes_x, length_x, slabs, planes):
@@ -90,13 +99,14 @@
 
 
 def y_modes_kernel(
-    index,
+    index_any,
     amplitude_hbm,
     load_hbm,
     cells_hbm,
     forcing_hbm,
     table_hbm,
     out_hbm,
+    index,
     amplitudes,
     load,
     cells,
@@ -116,12 +126,13 @@
     planes, y_blocks, slab_rows = cell_layout(cell_rows, table.shape[1])
     modes_y = table.shape[0] // 2
     span = planes * slab_rows
-    halves, slabs, half_rows, _ = packed.shape
-    half_channels = channels // halves
+    owners, block_rows, _ = out_hbm.shape
+    part_rows = block_rows // groups
     small = [
         pltpu.make_async_copy(source, target, arrived.at[n])
         for n, (source, target) in enumerate(
             [
+                (index_any, index),
                 (amplitude_hbm, amplitudes),
                 (load_hbm, load),
                 (forcing_hbm, forcing),
@@ -135,20 +146,27 @@
         )
         for g in range(groups)
     ]
-    for copy in small[:3] + large[:1] + small[3:] + large[1:]:
+    for copy in small[:4] + large[:1] + small[4:] + large[1:]:
         copy.start()
-    for copy in small[:3]:
+    for copy in small[:4]:
         copy.wait()
-    amplitude = amplitudes[index[0]]
+    amplitude = amplitudes[index[0, 0]]
     forcing_wide[...] = forcing[...].astype(F32)
-    small[3].wait()
-    leaving = []
+    small[4].wait()
+    leaving = [
+        pltpu.make_async_copy(packed.at[g], out_hbm.at[:, pl.ds(g * part_rows, part_rows), :], sent.at[g])
+        for g in range(groups)
+    ]
     for step in range(groups + 1):
         if step < groups:
             large[step].wait()
+            strengths = [amplitude * load[step * width + c] for c in range(width)]
+            for start in range(0, cell_rows, FORCING_ROWS):
+                some = pl.ds(start, FORCING_ROWS)
+                force = forcing_wide[some, :]
+                for c in range(width):
+                    field[step % 2, c, some, :] = half_field(cells[step * width + c, some, :], force, strengths[c])
             for c in range(width):
-                channel = step * width + c
-                field[step % 2, c] = half_field(cells[channel], forcing_wide[...], amplitude * load[channel])
                 for z in range(planes):
                     for j in range(y_blocks):
                         picked = field[step % 2, c, pl.ds(j * planes + z, slab_rows, stride=planes * y_blocks), :]
@@ -164,35 +182,31 @@
                 tile = slice(t * LANES, (t + 1) * LANES)
                 pair = pair_halves(result[:modes_y, tile], result[modes_y:, tile])
                 for n in range(2):
-                    half, c = divmod(g * width + 2 * t + n, half_channels)
-                    modes[half, pl.ds(c, modes_y, stride=half_channels), :] = pair[n]
-            if step * width % half_channels == 0:
-                half = g * width // half_channels
-                for d in range(slabs):
-                    packed[half, d] = modes[half, pl.ds(d * half_rows, half_rows), :].astype(BF16)
-                copy = pltpu.make_async_copy(
-                    packed.at[half], out_hbm.at[:, pl.ds(half * half_rows, half_rows), :], sent.at[half]
-                )
-                copy.start()
-                leaving.append(copy)
+                    modes[g % 2, pl.ds(2 * t + n, modes_y, stride=width), :] = pair[n]
+            for d in range(owners):
+                packed[g, d] = modes[g % 2, pl.ds(d * part_rows, part_rows), :].astype(BF16)
+            leaving[g].start()
     for copy in leaving:
         copy.wait()
 
 
 def y_modes(amp_index, amplitudes, load, cells, forcing, slabs, modes_y, length_y):
     channels, cell_rows, _ = cells.shape
-    width, halves = 4, 2
-    block_rows = modes_y // slabs * channels
-    table = forward_y_table(modes_y, length_y)
+    width = SUBLANES
+    parts = channels // width
+    owners = slabs // 2
+    block_rows = modes_y // owners * channels
+    table = forward_y_table(modes_y, length_y, slabs)
     planes, _, slab_rows = cell_layout(cell_rows, length_y)
     operands = in_hbm(amplitudes, load, cells, forcing, table)
     anywhere = pl.BlockSpec(memory_space=pl.ANY)
     return pl.pallas_call(
         y_modes_kernel,
-        in_specs=[pl.BlockSpec(memory_space=SMEM)] + [anywhere] * len(operands),
+        in_specs=[anywhere] * (1 + len(operands)),
         out_specs=anywhere,
-        out_shape=jax.ShapeDtypeStruct((slabs, block_rows, LANES), BF16),
+        out_shape=jax.ShapeDtypeStruct((owners, block_rows, LANES), BF16),
         scratch_shapes=[
+            SMEM(amp_index.shape, jnp.int32),
             SMEM(amplitudes.shape, F32),
             SMEM(load.shape, F32),
             pltpu.VMEM(cells.shape, BF16),
@@ -201,10 +215,10 @@
             pltpu.VMEM(table.shape, BF16),
             pltpu.VMEM((2, width, cell_rows, LANES), F32),
             pltpu.VMEM((2, width * planes * slab_rows, length_y), BF16),
-            pltpu.VMEM((halves, modes_y * channels // halves, LANES), F32),
-            pltpu.VMEM((halves, slabs, block_rows // halves, LANES), BF16),
-            pltpu.SemaphoreType.DMA((4 + channels // width,)),
-            pltpu.SemaphoreType.DMA((halves,)),
+            pltpu.VMEM((2, modes_y * width, LANES), F32),
+            pltpu.VMEM((parts, owners, block_rows // parts, LANES), BF16),
+            pltpu.SemaphoreType.DMA((5 + parts,)),
+            pltpu.SemaphoreType.DMA((parts,)),
         ],
         compiler_params=pltpu.CompilerParams(vmem_limit_bytes=12 * 1024 * 1024),
         cost_estimate=pl.CostEstimate(
@@ -214,9 +228,32 @@
     )(amp_index, *operands)
 
 
-def prepare_kernel(weight_ref, forward_ref, inverse_ref, weights, forward_out, inverse_out, wide):
-    forward_out[...] = forward_ref[...]
-    inverse_out[...] = inverse_ref[...]
+def prepare_kernel(
+    half_ref,
+    own_any,
+    other_any,
+    amplitude_ref,
+    load_ref,
+    weight_ref,
+    forward_hbm,
+    inverse_hbm,
+    strengths,
+    weights,
+    forward,
+    inverse,
+    wide,
+    indices,
+    arrived,
+):
+    half, me = half_ref[0], half_ref[1]
+    copies = [
+        pltpu.make_async_copy(forward_hbm.at[half], forward, arrived.at[0]),
+        pltpu.make_async_copy(inverse_hbm, inverse, arrived.at[1]),
+        pltpu.make_async_copy(own_any, indices.at[pl.ds(0, 1)], arrived.at[2]),
+        pltpu.make_async_copy(other_any, indices.at[pl.ds(1, 1)], arrived.at[3]),
+    ]
+    for copy in copies:
+        copy.start()
     local_modes, parts, channels, _, _ = weight_ref.shape
     for k in range(local_modes // 2):
         for r in range(parts):
@@ -224,55 +261,91 @@
                 pair = [weight_ref[2 * k + n, r, o].astype(F32) for n in range(2)]
                 wide[k, r, pl.ds(o, channels, stride=channels), :] = jnp.concatenate(pair, axis=1)
     weights[...] = wide[...].astype(BF16)
-
-
-def prepare(spectral_weight, length_x, slabs, planes):
+    for copy in copies:
+        copy.wait()
+    for m in range(2):
+        amplitude = amplitude_ref[indices[lax.rem(me + m, 2), 0]]
+        for c in range(channels):
+            strengths[m * channels + c] = amplitude * load_ref[c]
+
+
+def prepare(place, own, other, amplitudes, load, spectral_weight, length_x, slabs, planes):
     local_modes, parts, channels, _, modes_x = spectral_weight.shape
     forward = forward_x_table(modes_x, length_x, slabs, planes)
     inverse = inverse_x_table(modes_x, length_x, slabs, planes)
     wide = (local_modes // 2, parts, channels * channels, 2 * modes_x)
     vmem = pl.BlockSpec(memory_space=pltpu.VMEM)
+    smem = pl.BlockSpec(memory_space=SMEM)
+    anywhere = pl.BlockSpec(memory_space=pl.ANY)
     return pl.pallas_call(
         prepare_kernel,
-        in_specs=[vmem] * 3,
-        out_specs=[vmem] * 3,
+        in_specs=[smem] + [anywhere] * 2 + [smem] * 2 + [vmem] + [anywhere] * 2,
+        out_specs=[smem] + [vmem] * 3,
         out_shape=[
+            jax.ShapeDtypeStruct((2 * channels,), F32),
             pltpu.VMEM(wide, BF16),
-            pltpu.VMEM(forward.shape, BF16),
+            pltpu.VMEM(forward.shape[1:], BF16),
             pltpu.VMEM(inverse.shape, BF16),
         ],
-        scratch_shapes=[pltpu.VMEM(wide, F32)],
+        scratch_shapes=[pltpu.VMEM(wide, F32), SMEM((2, 1), jnp.int32), pltpu.SemaphoreType.DMA((4,))],
         compiler_params=pltpu.CompilerParams(vmem_limit_bytes=16 * 1024 * 1024),
         cost_estimate=pl.CostEstimate(
             flops=4 * spectral_weight.size, bytes_accessed=10 * spectral_weight.size, transcendentals=0
         ),
         name="prepare",
-    )(*in_hbm(spectral_weight, forward, inverse))
-
-
-def mix_kernel(limit_ref, pencil_ref, forward_ref, weight_ref, inverse_ref, out_ref, spectrum, mixed):
-    slabs, block_rows, _ = pencil_ref.shape
-    pairs, _, rows, width = weight_ref.shape
+    )(place, own, other, amplitudes, load, *in_hbm(spectral_weight, forward, inverse))
+
+
+def spectrum_kernel(half_ref, pencil_ref, forward_ref, out_ref):
+    sources, block_rows, _ = pencil_ref.shape
+    rows = out_ref.shape[0]
+    parts = rows // PART_ROWS
+    picked = []
+    for part in range(parts):
+        start = pl.multiple_of((2 * part + half_ref[0]) * PART_ROWS, PART_ROWS)
+        picked.append(
+            jnp.concatenate([pencil_ref[s, pl.ds(start, PART_ROWS), :] for s in range(sources)], axis=1)
+        )
+    result = jnp.dot(jnp.concatenate(picked, axis=0), forward_ref[...], preferred_element_type=F32)
+    out_ref[...] = result.astype(out_ref.dtype)
+
+
+def partial_spectrum(half, pencil, forward, dtype):
+    _, block_rows, _ = pencil.shape
+    vmem = pl.BlockSpec(memory_space=pltpu.VMEM)
+    return pl.pallas_call(
+        spectrum_kernel,
+        in_specs=[pl.BlockSpec(memory_space=SMEM), vmem, vmem],
+        out_specs=vmem,
+        out_shape=jax.ShapeDtypeStruct((block_rows // 2, forward.shape[1]), dtype),
+        compiler_params=pltpu.CompilerParams(vmem_limit_bytes=8 * 1024 * 1024),
+        cost_estimate=pl.CostEstimate(
+            flops=block_rows * forward.size, bytes_accessed=2 * pencil.size, transcendentals=0
+        ),
+        name="partial_spectrum",
+    )(half, pencil, forward)
+
+
+def mix_kernel(limit_ref, own_ref, other_ref, weight_ref, inverse_ref, out_hbm, spectrum, mixed, packed, sent):
+    block_rows, _ = own_ref.shape
+    pairs, _, _, width = weight_ref.shape
     local_modes = 2 * pairs
     channels = block_rows // local_modes
-    planes = forward_ref.shape[1] // width
+    planes = own_ref.shape[1] // width
     groups = channels // SUBLANES
-    half_channels = channels // 2
     block = SUBLANES * 2 * local_modes
-    pencil = jnp.concatenate([pencil_ref[s] for s in range(slabs)], axis=1)
-    result = jnp.dot(pencil, forward_ref[...], preferred_element_type=F32)
+    low = low_half((SUBLANES, width))
+    result = own_ref[...] + other_ref[...].astype(F32)
     for z in range(planes):
-        for half in range(2):
+        lanes = slice(z * width, (z + 1) * width)
+        for part in range(groups):
             for k in range(pairs):
-                start = (half * local_modes + 2 * k) * half_channels
-                both = [
-                    result[start + n * half_channels : start + (n + 1) * half_channels, z * width : (z + 1) * width]
-                    for n in range(2)
-                ]
-                parts = pair_halves(*both)
-                for r in range(2):
-                    spectrum[k, z, r, pl.ds(half * half_channels, half_channels), :] = parts[r]
-    low = low_half((SUBLANES, width))
+                start = (part * local_modes + 2 * k) * SUBLANES
+                real, imag = pair_halves(
+                    result[start : start + SUBLANES, lanes], result[start + SUBLANES : start + 2 * SUBLANES, lanes]
+                )
+                spectrum[k, z, 0, pl.ds(part * SUBLANES, SUBLANES), :] = real
+                spectrum[k, z, 1, pl.ds(part * SUBLANES, SUBLANES), :] = imag
     for k in range(pairs):
         keep = [jnp.where(limit_ref[0] > 2 * k + n, 1.0, 0.0).astype(F32) for n in range(2)]
         sums = [[[None, None] for _ in range(groups)] for _ in range(planes)]
@@ -304,51 +377,65 @@
                         low, swapped, -swapped
                     )
     left = jnp.concatenate([mixed[z].astype(BF16) for z in range(planes)], axis=1)
-    back = jnp.dot(left, inverse_ref[...], preferred_element_type=F32)
-    members = out_ref.shape[0] // slabs
-    for h in range(members):
-        for t in range(slabs // 2):
-            tile = slice(t * LANES, (t + 1) * LANES)
-            start = 2 * h * block
-            pair = pair_halves(back[start : start + block, tile], back[start + block : start + 2 * block, tile])
-            for n in range(2):
-                out_ref[(2 * t + n) * members + h] = pair[n].astype(BF16)
-
-
-def mix(limit, pencil, weights, forward, inverse, members):
-    slabs, block_rows, _ = pencil.shape
+    members = groups // 2
+    wide = 2 * LANES
+    leaving = []
+    for t in range(inverse_ref.shape[1] // wide):
+        back = jnp.dot(left, inverse_ref[:, t * wide : (t + 1) * wide], preferred_element_type=F32)
+        for u in range(2):
+            tile = slice(u * LANES, (u + 1) * LANES)
+            for h in range(members):
+                start = 2 * h * block
+                pair = pair_halves(back[start : start + block, tile], back[start + block : start + 2 * block, tile])
+                for n in range(2):
+                    packed[(4 * t + 2 * u + n) * members + h] = pair[n].astype(BF16)
+        blocks = pl.ds(4 * t * members, 4 * members)
+        copy = pltpu.make_async_copy(packed.at[blocks], out_hbm.at[blocks], sent.at[t])
+        copy.start()
+        leaving.append(copy)
+    for copy in leaving:
+        copy.wait()
+
+
+def mix(limit, own, other, weights, inverse, slabs, members):
+    block_rows, _ = own.shape
     pairs, _, _, width = weights.shape
     channels = block_rows // (2 * pairs)
-    planes = forward.shape[1] // width
+    planes = own.shape[1] // width
+    rows = channels * 4 * pairs
+    blocks = (slabs * members, SUBLANES * 4 * pairs, LANES)
     vmem = pl.BlockSpec(memory_space=pltpu.VMEM)
-    block = SUBLANES * 4 * pairs
     return pl.pallas_call(
         mix_kernel,
         in_specs=[pl.BlockSpec(memory_space=SMEM)] + [vmem] * 4,
-        out_specs=vmem,
-        out_shape=jax.ShapeDtypeStruct((members * slabs, block, LANES), BF16),
+        out_specs=pl.BlockSpec(memory_space=pl.ANY),
+        out_shape=jax.ShapeDtypeStruct(blocks, BF16),
         scratch_shapes=[
             pltpu.VMEM((pairs, planes, 2, channels, width), F32),
-            pltpu.VMEM((planes, channels // SUBLANES * block, width), F32),
+            pltpu.VMEM((planes, rows, width), F32),
+            pltpu.VMEM(blocks, BF16),
+            pltpu.SemaphoreType.DMA((slabs // 4,)),
         ],
-        compiler_params=pltpu.CompilerParams(vmem_limit_bytes=12 * 1024 * 1024),
+        compiler_params=pltpu.CompilerParams(vmem_limit_bytes=8 * 1024 * 1024),
         cost_estimate=pl.CostEstimate(
-            flops=2 * block_rows * forward.size, bytes_accessed=8 * weights.size, transcendentals=0
+            flops=2 * rows * inverse.size, bytes_accessed=4 * weights.size, transcendentals=0
         ),
         name="mix",
-    )(limit, pencil, forward, weights, inverse)
+    )(limit, own, other, weights, inverse)
 
 
 def pointwise_kernel(
-    place_ref, index_ref, amplitude_ref, load_ref, bias_ref, weight_ref, base_ref, forcing_ref, out_ref, spread
+    place_ref, strength_ref, bias_ref, weight_ref, base_ref, forcing_ref, out_ref, spread, native
 ):
-    channels, depth, _ = base_ref.shape
-    members = index_ref.shape[0]
+    members, inner, out_rows, length_y = out_ref.shape
+    channels, cell_rows, _ = base_ref.shape
+    outer = channels // (members * inner)
+    planes, y_blocks, slab_rows = cell_layout(cell_rows, length_y)
+    depth = 2 * SUBLANES
     out_channels = channels // members
-    me = place_ref[0]
-
-    @pl.when(pl.program_id(0) == 0)
-    def _():
+    me = place_ref[1]
+
+    def spread_weight():
         tall = (out_channels * depth, channels)
         wide = (channels, channels * depth)
         row_of = lax.broadcasted_iota(jnp.int32, tall, 0) // depth + me * out_channels
@@ -362,60 +449,78 @@
         )
         spread[...] = jnp.where(same, 2.0 * full, 0.0).astype(BF16)
 
-    forcing = forcing_ref[...].astype(F32)
-    fields = []
-    for m in range(members):
-        amplitude = amplitude_ref[index_ref[lax.rem(me - m + members, members)]]
-        parts = [half_field(base_ref[c], forcing, amplitude * load_ref[c]).astype(BF16) for c in range(channels)]
-        fields.append(jnp.concatenate(parts, axis=0))
-    result = jnp.dot(spread[...], jnp.concatenate(fields, axis=1), preferred_element_type=F32)
-    _, outer, inner, _, _ = out_ref.shape
-    start = pl.program_id(0) * depth
-    for a in range(outer):
-        for b in range(inner):
-            o = a * inner + b
-            bias = bias_ref[me * out_channels + o]
-            for m in range(members):
-                cells = result[o * depth : (o + 1) * depth, m * LANES : (m + 1) * LANES] + bias
-                out_ref[m, a, b, pl.ds(pl.multiple_of(start, depth), depth), :] = cells.astype(BF16)
-
-
-def pointwise(place, indices, amplitudes, load, bias, weight, cells, forcing):
+    spread_weight()
+
+    def body(step, carry):
+        rows = pl.ds(pl.multiple_of(step * depth, depth), depth)
+        forcing = forcing_ref[rows, :].astype(F32)
+        fields = []
+        for m in range(members):
+            parts = [
+                half_field(base_ref[c, rows, :], forcing, strength_ref[m * channels + c]).astype(BF16)
+                for c in range(channels)
+            ]
+            fields.append(jnp.concatenate(parts, axis=0))
+        result = jnp.dot(spread[...], jnp.concatenate(fields, axis=1), preferred_element_type=F32)
+        for a in range(outer):
+            for b in range(inner):
+                o = a * inner + b
+                bias = bias_ref[me * out_channels + o]
+                for m in range(members):
+                    cells = result[o * depth : (o + 1) * depth, m * LANES : (m + 1) * LANES] + bias
+                    native[m, a, b, rows, :] = cells
+        return carry
+
+    lax.fori_loop(0, cell_rows // depth, body, 0)
+
+    def arrange(b, carry):
+        for m in range(members):
+            for a in range(outer):
+                for z in range(planes):
+                    rows = pl.ds((a * planes + z) * slab_rows, slab_rows)
+                    for j in range(y_blocks):
+                        picked = native[m, a, b, pl.ds(j * planes + z, slab_rows, stride=planes * y_blocks), :]
+                        out_ref[m, b, rows, pl.ds(j * LANES, LANES)] = picked.astype(BF16)
+        return carry
+
+    lax.fori_loop(0, inner, arrange, 0)
+
+
+def pointwise(place, strengths, bias, weight, cells, forcing, length_y):
     channels, cell_rows, _ = cells.shape
-    members = indices.shape[0]
+    members = strengths.shape[0] // channels
     depth = 2 * SUBLANES
     inner = SUBLANES
     outer = channels // members // inner
     spread = (channels // members * depth, channels * depth)
     smem = pl.BlockSpec(memory_space=SMEM)
+    vmem = pl.BlockSpec(memory_space=pltpu.VMEM)
     return pl.pallas_call(
         pointwise_kernel,
-        grid=(cell_rows // depth,),
-        in_specs=[smem] * 5
-        + [
-            pl.BlockSpec(weight.shape, lambda r: (0, 0)),
-            pl.BlockSpec((channels, depth, LANES), lambda r: (0, r, 0)),
-            pl.BlockSpec((depth, LANES), lambda r: (r, 0)),
+        in_specs=[smem] * 3 + [vmem] * 3,
+        out_specs=vmem,
+        out_shape=pltpu.VMEM((members, inner, outer * cell_rows * LANES // length_y, length_y), BF16),
+        scratch_shapes=[
+            pltpu.VMEM(spread, BF16),
+            pltpu.VMEM((members, outer, inner, cell_rows, LANES), F32),
         ],
-        out_specs=pl.BlockSpec(memory_space=pltpu.VMEM),
-        out_shape=pltpu.VMEM((members, outer, inner, cell_rows, LANES), BF16),
-        scratch_shapes=[pltpu.VMEM(spread, BF16)],
-        compiler_params=pltpu.CompilerParams(vmem_limit_bytes=12 * 1024 * 1024),
+        compiler_params=pltpu.CompilerParams(vmem_limit_bytes=16 * 1024 * 1024),
         cost_estimate=pl.CostEstimate(
             flops=4 * spread[0] * spread[1] * members * cell_rows // depth * LANES,
             bytes_accessed=8 * cells.size,
             transcendentals=members * cells.size,
         ),
         name="pointwise",
-    )(place, indices, amplitudes, load, bias, weight, *in_hbm(cells, forcing))
-
-
-def layer_kernel(back_ref, table_ref, points, out_hbm, columns, spectral, result, sent):
-    members, outer, inner, cell_rows, _ = points.shape
+    )(place, strengths, bias, weight, *in_hbm(cells, forcing))
+
+
+def layer_kernel(back_ref, table_ref, point_ref, out_hbm, columns, native, result, sent):
+    members, inner, rows, length_y = point_ref.shape
+    _, outer, cell_rows, _ = native.shape
     sources, block_rows, _ = back_ref.shape
     slabs = sources // members
     depth = block_rows // inner
-    planes, y_blocks, slab_rows = cell_layout(cell_rows, table_ref.shape[1])
+    planes, y_blocks, slab_rows = cell_layout(cell_rows, length_y)
     leaving = [pltpu.make_async_copy(result.at[:, b], out_hbm.at[:, b], sent.at[b]) for b in range(inner)]
     for m in range(members):
         for s in range(slabs):
@@ -424,42 +529,41 @@
                 columns[b, m, pl.ds(s * depth, depth), :] = block[b * depth : (b + 1) * depth]
     for b in range(inner):
         turn = b % 2
+        total = None
         for m in range(members):
-            values = lax.dot_general(
+            spectral = lax.dot_general(
                 columns[b, m].astype(BF16), table_ref[...], (((0,), (0,)), ((), ())), preferred_element_type=F32
             )
-            for a in range(outer):
-                for z in range(planes):
-                    start = (a * planes + z) * slab_rows
-                    for j in range(y_blocks):
-                        spectral[
-                            turn, m, a, pl.ds(j * planes + z, slab_rows, stride=planes * y_blocks), :
-                        ] = values[start : start + slab_rows, j * LANES : (j + 1) * LANES]
+            value = jax.nn.gelu(point_ref[m, b].astype(F32) + spectral, approximate=True)
+            total = value if total is None else total + value
+        total = total * (1.0 / members)
         for a in range(outer):
-            total = None
-            for m in range(members):
-                value = jax.nn.gelu(points[m, a, b].astype(F32) + spectral[turn, m, a], approximate=True)
-                total = value if total is None else total + value
-            result[a, b] = (total * (1.0 / members)).astype(BF16)
+            for z in range(planes):
+                start = (a * planes + z) * slab_rows
+                for j in range(y_blocks):
+                    native[turn, a, pl.ds(j * planes + z, slab_rows, stride=planes * y_blocks), :] = total[
+                        start : start + slab_rows, j * LANES : (j + 1) * LANES
+                    ]
+        for a in range(outer):
+            result[a, b] = native[turn, a].astype(BF16)
         leaving[b].start()
     for copy in leaving:
         copy.wait()
 
 
-def layer(back, points, length_x, length_y, modes_y):
-    members, outer, inner, cell_rows, _ = points.shape
-    slabs = back.shape[0] // members
+def layer(back, points, outer, length_x, modes_y, slabs):
+    members, inner, rows, length_y = points.shape
+    cell_rows = rows * length_y // (outer * LANES)
     table = inverse_y_table(modes_y, length_y, length_x, slabs)
     vmem = pl.BlockSpec(memory_space=pltpu.VMEM)
-    anywhere = pl.BlockSpec(memory_space=pl.ANY)
     return pl.pallas_call(
         layer_kernel,
         in_specs=[vmem, vmem, vmem],
-        out_specs=anywhere,
+        out_specs=pl.BlockSpec(memory_space=pl.ANY),
         out_shape=pltpu.HBM((outer, inner, cell_rows, LANES), BF16),
         scratch_shapes=[
             pltpu.VMEM((inner, members, 2 * modes_y, LANES), F32),
-            pltpu.VMEM((2, members, outer, cell_rows, LANES), F32),
+            pltpu.VMEM((2, outer, cell_rows, LANES), F32),
             pltpu.VMEM((outer, inner, cell_rows, LANES), BF16),
             pltpu.SemaphoreType.DMA((inner,)),
         ],
@@ -492,23 +596,34 @@
     cells = cells.reshape(channels, slab_rows * SUBLANES, LANES)
     force = forcing.reshape(slab_rows, planes, y_blocks, LANES).transpose(0, 2, 1, 3)
     force = force.reshape(slab_rows * SUBLANES, LANES)
-    me = lax.axis_index("member")
-    indices = jnp.concatenate(
-        [amp_index]
-        + [
-            lax.ppermute(amp_index, "member", [(s, (s + r) % members) for s in range(members)])
-            for r in range(1, members)
-        ]
-    )
+    owners = slabs // 2
+    slab, me = lax.axis_index("slab"), lax.axis_index("member")
+    half = slab // owners
+    place = jnp.stack([half, me])
+    other_half = jnp.reshape(1 - half, (1,))
+    partners = [(n, (n + owners) % slabs) for n in range(slabs)]
+    index = amp_index.reshape(1, 1)
+    other_index = lax.ppermute(index, "member", [(n, 1 - n) for n in range(2)])
     out_channels = channels // members
-    packed = y_modes(amp_index, amplitudes, load, cells, force, slabs, modes_y, length_y)
-    pencil = lax.all_to_all(packed, "slab", split_axis=0, concat_axis=0, tiled=True)
-    weights, forward, inverse = prepare(spectral_weight.transpose(0, 2, 3, 4, 1), length_x, slabs, planes)
-    limit = mode_count - lax.axis_index("slab") * local_modes
-    back = mix(limit, pencil, weights, forward, inverse, members)
+    packed = y_modes(index, amplitudes, load, cells, force, slabs, modes_y, length_y)
+    pencil = lax.all_to_all(
+        packed,
+        "slab",
+        split_axis=0,
+        concat_axis=0,
+        tiled=True,
+        axis_index_groups=[list(range(h * owners, (h + 1) * owners)) for h in range(2)],
+    )
+    strengths, weights, forward, inverse = prepare(
+        place, index, other_index, amplitudes, load, spectral_weight.transpose(0, 2, 3, 4, 1), length_x, slabs, planes
+    )
+    leaving = partial_spectrum(other_half, pencil, forward, BF16)
+    other = lax.ppermute(leaving, "slab", partners)
+    own = partial_spectrum(place, pencil, forward, F32)
+    back = mix(mode_count - slab * local_modes, own, other, weights, inverse, slabs, members)
     back = lax.all_to_all(back, ("slab", "member"), split_axis=0, concat_axis=0, tiled=True)
-    points = pointwise(me.reshape(1), indices, amplitudes, load, point_bias, point_weight, cells, force)
-    result = layer(back, points, length_x, length_y, modes_y)
+    points = pointwise(place, strengths, point_bias, point_weight, cells, force, length_y)
+    result = layer(back, points, out_channels // SUBLANES, length_x, modes_y, slabs)
     result = result.reshape(out_channels, slab_rows, y_blocks, planes, LANES).transpose(0, 1, 3, 2, 4)
     return result.reshape(out_channels, slab_rows, planes, length_y)
 
@@ -522,7 +637,7 @@
         and planes * length_y == SUBLANES * LANES
         and 2 * local_modes == SUBLANES
         and 2 * SUBLANES * members == channels
-        and slabs % 2 == 0
+        and slabs % 4 == 0
     )
 
 

time: 53.7 us -> 51.3 us (0.955)
  Pallas kernels: 25.7 us -> 22.7 us
  starting transfers between devices: 11.5 us -> 13.8 us
  waiting for transfers between devices: 13.9 us -> 12.9 us
  other arithmetic: 0.69 us -> 0.08 us
    all_to_all x1, waiting for transfers between devices: 10.2 us -> 2.6 us  [fast_local(): lax.all_to_all(packed, 'slab', split_axis=0, concat_axis=0, tiled=True, a...]
    all_to_all x1, waiting for transfers between devices: 2.66 us -> 7.9 us  [fast_local(): lax.all_to_all(back, ('slab', 'member'), split_axis=0, concat_axis=0, til...]
    pallas_call x4 -> x6, Pallas kernels: 23.2 us -> 20.7 us  [the longest x1 7.6 us: pointwise(): pl.pallas_call(pointwise_kernel, in_specs=[smem] * 3 + [vmem] * 3, out_sp...]
    ppermute x1 -> x2, starting transfers between devices: 0.32 us -> 2.65 us  [the longest x1 2.65 us: fast_local(): other = lax.ppermute(leaving, 'slab', partners)]
    all_to_all x1, starting transfers between devices: 8.32 us -> 6.19 us  [fast_local(): lax.all_to_all(packed, 'slab', split_axis=0, concat_axis=0, tiled=True, a...]
    all_to_all x1, starting transfers between devices: 2.88 us -> 4.96 us  [fast_local(): lax.all_to_all(back, ('slab', 'member'), split_axis=0, concat_axis=0, til...]
    ppermute x1 -> x2, waiting for transfers between devices: 0.98 us -> 2.41 us  [the longest x1 1.28 us: fast_local(): other_index = lax.ppermute(index, 'member', [(n, 1 - n) for n in range(2)])]
    concatenate x1 -> x0, other arithmetic: 0.69 us -> none  [fast_local(): jnp.concatenate([amp_index] + [lax.ppermute(amp_index, 'member', [(s, (s...]
  transfers between devices with their start and end apart: 3 -> 4, of which waited for: 3 -> 4; matrix products, arithmetic and copies ran while one was open for 1% -> 0% of each run, Pallas kernels for 28% -> 26%
where the time goes in v3:
time: 51.3 us; the launch traced here: 51 us
  Pallas kernels  22.7 us (44%)
  starting transfers between devices  13.8 us (27%)
  waiting for transfers between devices  12.9 us (25%)
  between operations  1.46 us (3%)
    all_to_all x1, waiting for transfers between devices, fast_local(): lax.all_to_all(back, ('slab', 'member'), split_axis=0, concat_axis=0, til...  7.9 us
    pallas_call x1, Pallas kernels, pointwise(): pl.pallas_call(pointwise_kernel, in_specs=[smem] * 3 + [vmem] * 3, out_sp...  7.6 us
    all_to_all x1, starting transfers between devices, fast_local(): lax.all_to_all(packed, 'slab', split_axis=0, concat_axis=0, tiled=True, a...  6.19 us
    pallas_call x1, Pallas kernels, prepare(): pl.pallas_call(prepare_kernel, in_specs=[smem] + [anywhere] * 2 + [smem]...  5.12 us
    all_to_all x1, starting transfers between devices, fast_local(): lax.all_to_all(back, ('slab', 'member'), split_axis=0, concat_axis=0, til...  4.96 us
    pallas_call x1, Pallas kernels, y_modes(): pl.pallas_call(y_modes_kernel, in_specs=[anywhere] * (1 + len(operands)),...  4.13 us
    pallas_call x1, Pallas kernels, layer(): pl.pallas_call(layer_kernel, in_specs=[vmem, vmem, vmem], out_specs=pl.Bl...  2.81 us
    ppermute x1, starting transfers between devices, fast_local(): other = lax.ppermute(leaving, 'slab', partners)  2.65 us
  transfers between devices with their start and end apart: 4, of which 4 were waited for; matrix products, arithmetic and copies ran while one was open for 0% of the time, Pallas kernels for 26%

profile of v3, /device:TPU:0, one launch (start us, length us, event | category | flops | bytes accessed | tf_op | source)
XLA Modules:
  0.0 51.0 jit_solution(18371402487607624959)
XLA Ops:
  0.0 0.0 copy-start.1
  0.0 0.0 copy-start.2
  0.7 4.1 %y_modes.1 = bf16[8,256,128]{2,1,0:T(8,128)(2,1)} custom-call(s32[1,1]{1,0:T(1,128)} %bitcast.21.index_any, f32[16]{0:T(128)} %amplitude_ref.1, f32[32]{0:T(128)} %load_ref.1, bf16[32,256,128]{2,1,0:T(8,128)(2,1)} %bitcast.24, bf16[256,128]{1,0:T(8,128)(2,1)} %bitcast.26, bf16[128,512]{1,0:T(8,128)(2,1)} %constant.36.clone.table_hbm), custom_call_target="tpu_custom_call" | custom-call | flops 268435456 | bytes 4194304 | tf_op jit(solution)/shard_map/y_modes/pallas_call | solution.py:203
  4.8 6.2 %all-to-all-start = ((bf16[8,256,128]{2,1,0:T(8,128)(2,1)}), bf16[8,256,128]{2,1,0:T(8,128)(2,1)S(1)}, u32[]{:S(2)}, u32[]{:S(2)}) async-start(bf16[8,256,128]{2,1,0:T(8,128)(2,1)} %y_modes.1), calls=%async_computation | async-start | bytes 1048576 | tf_op jit(solution)/shard_map/all_to_all | solution.py:609
  11.0 0.0 collective-permute-start
  11.0 0.1 pad_add_fusion.half_ref.place_ref
  11.1 1.3 %collective-permute-done.other_any = s32[1,1]{1,0:T(1,128)} collective-permute-done((s32[1,1]{1,0:T(1,128)}, s32[1,1]{1,0:T(1,128)}, u32[]{:S(2)}, u32[]{:S(2)}) %collective-permute-start) | collective-permute-done | bytes 36 | tf_op jit(solution)/shard_map/ppermute | solution.py:606
  12.4 0.0 copy-done.1
  12.4 0.0 copy-done.2
  12.4 5.1 %prepare.1 = (f32[64]{0:T(128)S(1)}, bf16[2,2,1024,128]{3,2,1,0:T(8,128)(2,1)S(1)}, bf16[1024,256]{1,0:T(8,128)(2,1)S(1)}, bf16[256,1024]{1,0:T(8,128)(2,1)S(1)}) custom-call(s32[2]{0:T(128)S(1)} %pad_add_fusion.half_ref.place_ref, s32[1,1]{1,0:T(1,128)} %bitcast.22.own_any, s32[1,1]{1,0:T(1,128)} %collective-permute-done.other_any, f32[16]{0:T(128)S(1)} %copy-done.1, ...), custom_call_target="tpu_custom_call" | custom-call | flops 2097152 | bytes 5242880 | tf_op jit(solution)/shard_map/prepare/pallas_call | solution.py:280
  17.5 2.6 %all-to-all-done.pencil_ref = bf16[8,256,128]{2,1,0:T(8,128)(2,1)S(1)} async-done(((bf16[8,256,128]{2,1,0:T(8,128)(2,1)}), bf16[8,256,128]{2,1,0:T(8,128)(2,1)S(1)}, u32[]{:S(2)}, u32[]{:S(2)}) %all-to-all-start) | async-done | bytes 524320 | tf_op jit(solution)/shard_map/all_to_all | solution.py:609
  20.1 0.2 partial_spectrum.3
  20.4 2.6 %collective-permute-start.1 = (bf16[128,256]{1,0:T(8,128)(2,1)S(1)}, bf16[128,256]{1,0:T(8,128)(2,1)S(1)}, u32[]{:S(2)}, u32[]{:S(2)}) collective-permute-start(bf16[128,256]{1,0:T(8,128)(2,1)S(1)} %partial_spectrum.3), channel_id=1, source_target_pairs={{0,8},{1,9},{2,10},{3,11},{4,12},{5,13},{6,14},{7,15},{8,0},{9,1},... | collective-permute-start | bytes 196616 | tf_op jit(solution)/shard_map/ppermute | solution.py:621
  23.7 0.0 copy-start.3
  23.7 0.0 copy-start.4
  23.7 0.8 %partial_spectrum.2.own_ref = f32[128,256]{1,0:T(8,128)S(1)} custom-call(s32[2]{0:T(128)S(1)} %pad_add_fusion.half_ref.place_ref, bf16[8,256,128]{2,1,0:T(8,128)(2,1)S(1)} %all-to-all-done.pencil_ref, bf16[1024,256]{1,0:T(8,128)(2,1)S(1)} %get-tuple-element.9.forward_ref), custom_call_target="tpu_custom_call" | custom-call | flops 67108864 | bytes 524288 | tf_op jit(solution)/shard_map/partial_spectrum/pallas_call | solution.py:316
  24.5 1.1 %collective-permute-done.1.other_ref = bf16[128,256]{1,0:T(8,128)(2,1)S(1)} collective-permute-done((bf16[128,256]{1,0:T(8,128)(2,1)S(1)}, bf16[128,256]{1,0:T(8,128)(2,1)S(1)}, u32[]{:S(2)}, u32[]{:S(2)}) %collective-permute-start.1) | collective-permute-done | bytes 65568 | tf_op jit(solution)/shard_map/ppermute | solution.py:621
  25.6 2.0 %mix.1 = bf16[32,64,128]{2,1,0:T(8,128)(2,1)} custom-call(s32[1]{0:T(128)S(6)} %sub.14.limit_ref, f32[128,256]{1,0:T(8,128)S(1)} %partial_spectrum.2.own_ref, bf16[128,256]{1,0:T(8,128)(2,1)S(1)} %collective-permute-done.1.other_ref, bf16[2,2,1024,128]{3,2,1,0:T(8,128)(2,1)S(1)} %get-tuple-element.10.weight_ref, ...), custom_call_target="tpu_custom_call" | custom-call | flops 134217728 | bytes 2097152 | tf_op jit(solution)/shard_map/mix/pallas_call | solution.py:408
  27.6 5.0 %all-to-all-start.1 = ((bf16[32,64,128]{2,1,0:T(8,128)(2,1)}), bf16[32,64,128]{2,1,0:T(8,128)(2,1)S(1)}, u32[]{:S(2)}, u32[]{:S(2)}) async-start(bf16[32,64,128]{2,1,0:T(8,128)(2,1)} %mix.1), calls=%async_computation.1 | async-start | bytes 1048576 | tf_op jit(solution)/shard_map/all_to_all | solution.py:624
  32.6 0.0 copy-done.3
  32.6 0.0 copy-done.4
  32.6 0.0 copy-start
  32.6 7.6 %pointwise.1.point_ref = bf16[2,8,128,512]{3,2,1,0:T(8,128)(2,1)S(1)} custom-call(s32[2]{0:T(128)S(1)} %pad_add_fusion.half_ref.place_ref, f32[64]{0:T(128)S(1)} %get-tuple-element.12.strength_ref, f32[32]{0:T(128)S(1)} %copy-done.4, bf16[32,32]{1,0:T(8,128)(2,1)S(1)} %copy-done.3, bf16[32,256,128]{2,1,0:T(8,128)(2,1)} %bitcast.25, bf16[256,128]{1,0:T(8,128)(2,1)} %bitcast.27), custom_call_target="tpu_custom_call" | custom-call | flops 2147483648 | bytes 8388608 | tf_op jit(solution)/shard_map/pointwise/pallas_call | solution.py:498
  40.3 7.9 %all-to-all-done.1.back_ref = bf16[32,64,128]{2,1,0:T(8,128)(2,1)S(1)} async-done(((bf16[32,64,128]{2,1,0:T(8,128)(2,1)}), bf16[32,64,128]{2,1,0:T(8,128)(2,1)S(1)}, u32[]{:S(2)}, u32[]{:S(2)}) %all-to-all-start.1) | async-done | bytes 524320 | tf_op jit(solution)/shard_map/all_to_all | solution.py:624
  48.2 0.0 copy-done
  48.2 2.8 %layer.1 = bf16[2,8,256,128]{3,2,1,0:T(8,128)(2,1)} custom-call(bf16[32,64,128]{2,1,0:T(8,128)(2,1)S(1)} %all-to-all-done.1.back_ref, bf16[128,512]{1,0:T(8,128)(2,1)S(1)} %copy-done, bf16[2,8,128,512]{3,2,1,0:T(8,128)(2,1)S(1)} %pointwise.1.point_ref), custom_call_target="tpu_custom_call" | custom-call | flops 268435456 | bytes 5242880 | tf_op jit(solution)/shard_map/layer/pallas_call | solution.py:559
Async XLA Ops:
  0.0 12.4 %copy-start.1 = (f32[16]{0:T(128)S(1)}, f32[16]{0:T(128)}, u32[]{:S(2)}) copy-start(f32[16]{0:T(128)} %amplitude_ref.1) | copy-start | bytes 196
  0.0 12.4 %copy-start.2 = (f32[32]{0:T(128)S(1)}, f32[32]{0:T(128)}, u32[]{:S(2)}) copy-start(f32[32]{0:T(128)} %load_ref.1) | copy-start | bytes 388
  4.8 15.3 %all-to-all-start = ((bf16[8,256,128]{2,1,0:T(8,128)(2,1)}), bf16[8,256,128]{2,1,0:T(8,128)(2,1)S(1)}, u32[]{:S(2)}, u32[]{:S(2)}) async-start(bf16[8,256,128]{2,1,0:T(8,128)(2,1)} %y_modes.1), calls=%async_computation | async-start | bytes 1048576 | tf_op jit(solution)/shard_map/all_to_all | solution.py:609
  11.0 1.4 %collective-permute-start = (s32[1,1]{1,0:T(1,128)}, s32[1,1]{1,0:T(1,128)}, u32[]{:S(2)}, u32[]{:S(2)}) collective-permute-start(s32[1,1]{1,0:T(1,128)} %bitcast.3), channel_id=1, source_target_pairs={{0,16},{16,0},{1,17},{17,1},{2,18},{18,2},{3,19},{19,3},{4,20},{20... | collective-permute-start | bytes 20 | tf_op jit(solution)/shard_map/ppermute | solution.py:606
  20.4 5.2 %collective-permute-start.1 = (bf16[128,256]{1,0:T(8,128)(2,1)S(1)}, bf16[128,256]{1,0:T(8,128)(2,1)S(1)}, u32[]{:S(2)}, u32[]{:S(2)}) collective-permute-start(bf16[128,256]{1,0:T(8,128)(2,1)S(1)} %partial_spectrum.3), channel_id=1, source_target_pairs={{0,8},{1,9},{2,10},{3,11},{4,12},{5,13},{6,14},{7,15},{8,0},{9,1},... | collective-permute-start | bytes 196616 | tf_op jit(solution)/shard_map/ppermute | solution.py:621
  23.7 8.9 %copy-start.3 = (bf16[32,32]{1,0:T(8,128)(2,1)S(1)}, bf16[32,32]{1,0:T(8,128)(2,1)}, u32[]{:S(2)}) copy-start(bf16[32,32]{1,0:T(8,128)(2,1)} %weight_ref.1) | copy-start | bytes 6148
  23.7 8.9 %copy-start.4 = (f32[32]{0:T(128)S(1)}, f32[32]{0:T(128)}, u32[]{:S(2)}) copy-start(f32[32]{0:T(128)} %bias_ref.1) | copy-start | bytes 388
  27.6 20.5 %all-to-all-start.1 = ((bf16[32,64,128]{2,1,0:T(8,128)(2,1)}), bf16[32,64,128]{2,1,0:T(8,128)(2,1)S(1)}, u32[]{:S(2)}, u32[]{:S(2)}) async-start(bf16[32,64,128]{2,1,0:T(8,128)(2,1)} %mix.1), calls=%async_computation.1 | async-start | bytes 1048576 | tf_op jit(solution)/shard_map/all_to_all | solution.py:624
  32.6 15.5 %copy-start = (bf16[128,512]{1,0:T(8,128)(2,1)S(1)}, bf16[128,512]{1,0:T(8,128)(2,1)}, u32[]{:S(2)}) copy-start(bf16[128,512]{1,0:T(8,128)(2,1)} %constant.39.clone.table_ref) | copy-start | bytes 393220

commit v4 on v3

--- a/solution.py
+++ b/solution.py
@@ -86,6 +86,11 @@
 
 def half_field(base, forcing, strength):
     return jnp.tanh(0.5 * (base.astype(F32) + strength * forcing))
+
+
+def double_gelu(x):
+    scale = math.sqrt(2.0 / math.pi)
+    return x * (1.0 + jnp.tanh(x * (scale + (0.044715 * scale) * (x * x))))
 
 
 def cell_layout(cell_rows, length_y):
@@ -122,12 +127,12 @@
 ):
     channels, cell_rows, _ = cells.shape
     width = field.shape[1]
-    groups = channels // width
+    groups = [(c, width) for c in range(0, channels, width)]
     planes, y_blocks, slab_rows = cell_layout(cell_rows, table.shape[1])
     modes_y = table.shape[0] // 2
     span = planes * slab_rows
     owners, block_rows, _ = out_hbm.shape
-    part_rows = block_rows // groups
+    part_rows = block_rows // (channels // width)
     small = [
         pltpu.make_async_copy(source, target, arrived.at[n])
         for n, (source, target) in enumerate(
@@ -142,9 +147,9 @@
     ]
     large = [
         pltpu.make_async_copy(
-            cells_hbm.at[pl.ds(g * width, width)], cells.at[pl.ds(g * width, width)], arrived.at[len(small) + g]
+            cells_hbm.at[pl.ds(first, count)], cells.at[pl.ds(first, count)], arrived.at[len(small) + n]
         )
-        for g in range(groups)
+        for n, (first, count) in enumerate(groups)
     ]
     for copy in small[:4] + large[:1] + small[4:] + large[1:]:
         copy.start()
@@ -155,18 +160,19 @@
     small[4].wait()
     leaving = [
         pltpu.make_async_copy(packed.at[g], out_hbm.at[:, pl.ds(g * part_rows, part_rows), :], sent.at[g])
-        for g in range(groups)
+        for g in range(channels // width)
     ]
-    for step in range(groups + 1):
-        if step < groups:
+    for step in range(len(groups) + 1):
+        if step < len(groups):
+            first, count = groups[step]
             large[step].wait()
-            strengths = [amplitude * load[step * width + c] for c in range(width)]
+            strengths = [amplitude * load[first + c] for c in range(count)]
             for start in range(0, cell_rows, FORCING_ROWS):
                 some = pl.ds(start, FORCING_ROWS)
                 force = forcing_wide[some, :]
-                for c in range(width):
-                    field[step % 2, c, some, :] = half_field(cells[step * width + c, some, :], force, strengths[c])
-            for c in range(width):
+                for c in range(count):
+                    field[step % 2, c, some, :] = half_field(cells[first + c, some, :], force, strengths[c])
+            for c in range(count):
                 for z in range(planes):
                     for j in range(y_blocks):
                         picked = field[step % 2, c, pl.ds(j * planes + z, slab_rows, stride=planes * y_blocks), :]
@@ -174,18 +180,23 @@
                             step % 2, pl.ds(c * span + z * slab_rows, slab_rows), pl.ds(j * LANES, LANES)
                         ] = picked.astype(BF16)
         if step > 0:
-            g = step - 1
+            first, count = groups[step - 1]
             result = lax.dot_general(
-                table[...], rows[g % 2], (((1,), (1,)), ((), ())), preferred_element_type=F32
+                table[...],
+                rows[(step - 1) % 2, pl.ds(0, count * span), :],
+                (((1,), (1,)), ((), ())),
+                preferred_element_type=F32,
             )
-            for t in range(width // 2):
+            part, place = divmod(first, width)
+            for t in range(count // 2):
                 tile = slice(t * LANES, (t + 1) * LANES)
                 pair = pair_halves(result[:modes_y, tile], result[modes_y:, tile])
                 for n in range(2):
-                    modes[g % 2, pl.ds(2 * t + n, modes_y, stride=width), :] = pair[n]
-            for d in range(owners):
-                packed[g, d] = modes[g % 2, pl.ds(d * part_rows, part_rows), :].astype(BF16)
-            leaving[g].start()
+                    modes[part % 2, pl.ds(place + 2 * t + n, modes_y, stride=width), :] = pair[n]
+            if place + count == width:
+                for d in range(owners):
+                    packed[part, d] = modes[part % 2, pl.ds(d * part_rows, part_rows), :].astype(BF16)
+                leaving[part].start()
     for copy in leaving:
         copy.wait()
 
@@ -534,9 +545,9 @@
             spectral = lax.dot_general(
                 columns[b, m].astype(BF16), table_ref[...], (((0,), (0,)), ((), ())), preferred_element_type=F32
             )
-            value = jax.nn.gelu(point_ref[m, b].astype(F32) + spectral, approximate=True)
+            value = double_gelu(point_ref[m, b].astype(F32) + spectral)
             total = value if total is None else total + value
-        total = total * (1.0 / members)
+        total = total * (0.5 / members)
         for a in range(outer):
             for z in range(planes):
                 start = (a * planes + z) * slab_rows

time: 51.3 us -> 51.1 us (level)
  transfers between devices with their start and end apart: 4 -> 4, of which waited for: 4 -> 4; matrix products, arithmetic and copies ran while one was open for 0% -> 0% of each run, Pallas kernels for 26% -> 27%
where the time goes in v4:
time: 51.1 us; the launch traced here: 50.7 us
  Pallas kernels  22.4 us (44%)
  starting transfers between devices  13.8 us (27%)
  waiting for transfers between devices  12.9 us (25%)
  between operations  1.46 us (3%)
    all_to_all x1, waiting for transfers between devices, fast_local(): lax.all_to_all(back, ('slab', 'member'), split_axis=0, concat_axis=0, til...  7.9 us
    pallas_call x1, Pallas kernels, pointwise(): pl.pallas_call(pointwise_kernel, in_specs=[smem] * 3 + [vmem] * 3, out_sp...  7.6 us
    all_to_all x1, starting transfers between devices, fast_local(): lax.all_to_all(packed, 'slab', split_axis=0, concat_axis=0, tiled=True, a...  6.19 us
    pallas_call x1, Pallas kernels, prepare(): pl.pallas_call(prepare_kernel, in_specs=[smem] + [anywhere] * 2 + [smem]...  5.12 us
    all_to_all x1, starting transfers between devices, fast_local(): lax.all_to_all(back, ('slab', 'member'), split_axis=0, concat_axis=0, til...  4.96 us
    pallas_call x1, Pallas kernels, y_modes(): pl.pallas_call(y_modes_kernel, in_specs=[anywhere] * (1 + len(operands)),...  4.13 us
    ppermute x1, starting transfers between devices, fast_local(): other = lax.ppermute(leaving, 'slab', partners)  2.65 us
    all_to_all x1, waiting for transfers between devices, fast_local(): lax.all_to_all(packed, 'slab', split_axis=0, concat_axis=0, tiled=True, a...  2.6 us
  transfers between devices with their start and end apart: 4, of which 4 were waited for; matrix products, arithmetic and copies ran while one was open for 0% of the time, Pallas kernels for 27%

profile of v4, /device:TPU:0, one launch (start us, length us, event | category | flops | bytes accessed | tf_op | source)
XLA Modules:
  0.0 50.7 jit_solution(9752296910822973051)
XLA Ops:
  0.0 0.0 copy-start.1
  0.0 0.0 copy-start.2
  0.7 4.1 %y_modes.1 = bf16[8,256,128]{2,1,0:T(8,128)(2,1)} custom-call(s32[1,1]{1,0:T(1,128)} %bitcast.21.index_any, f32[16]{0:T(128)} %amplitude_ref.1, f32[32]{0:T(128)} %load_ref.1, bf16[32,256,128]{2,1,0:T(8,128)(2,1)} %bitcast.24, bf16[256,128]{1,0:T(8,128)(2,1)} %bitcast.26, bf16[128,512]{1,0:T(8,128)(2,1)} %constant.36.clone.table_hbm), custom_call_target="tpu_custom_call" | custom-call | flops 268435456 | bytes 4194304 | tf_op jit(solution)/shard_map/y_modes/pallas_call | solution.py:214
  4.8 6.2 %all-to-all-start = ((bf16[8,256,128]{2,1,0:T(8,128)(2,1)}), bf16[8,256,128]{2,1,0:T(8,128)(2,1)S(1)}, u32[]{:S(2)}, u32[]{:S(2)}) async-start(bf16[8,256,128]{2,1,0:T(8,128)(2,1)} %y_modes.1), calls=%async_computation | async-start | bytes 1048576 | tf_op jit(solution)/shard_map/all_to_all | solution.py:620
  11.0 0.0 collective-permute-start
  11.0 0.1 pad_add_fusion.half_ref.place_ref
  11.1 1.3 %collective-permute-done.other_any = s32[1,1]{1,0:T(1,128)} collective-permute-done((s32[1,1]{1,0:T(1,128)}, s32[1,1]{1,0:T(1,128)}, u32[]{:S(2)}, u32[]{:S(2)}) %collective-permute-start) | collective-permute-done | bytes 36 | tf_op jit(solution)/shard_map/ppermute | solution.py:617
  12.4 0.0 copy-done.1
  12.4 0.0 copy-done.2
  12.4 5.1 %prepare.1 = (f32[64]{0:T(128)S(1)}, bf16[2,2,1024,128]{3,2,1,0:T(8,128)(2,1)S(1)}, bf16[1024,256]{1,0:T(8,128)(2,1)S(1)}, bf16[256,1024]{1,0:T(8,128)(2,1)S(1)}) custom-call(s32[2]{0:T(128)S(1)} %pad_add_fusion.half_ref.place_ref, s32[1,1]{1,0:T(1,128)} %bitcast.22.own_any, s32[1,1]{1,0:T(1,128)} %collective-permute-done.other_any, f32[16]{0:T(128)S(1)} %copy-done.1, ...), custom_call_target="tpu_custom_call" | custom-call | flops 2097152 | bytes 5242880 | tf_op jit(solution)/shard_map/prepare/pallas_call | solution.py:291
  17.5 2.6 %all-to-all-done.pencil_ref = bf16[8,256,128]{2,1,0:T(8,128)(2,1)S(1)} async-done(((bf16[8,256,128]{2,1,0:T(8,128)(2,1)}), bf16[8,256,128]{2,1,0:T(8,128)(2,1)S(1)}, u32[]{:S(2)}, u32[]{:S(2)}) %all-to-all-start) | async-done | bytes 524320 | tf_op jit(solution)/shard_map/all_to_all | solution.py:620
  20.1 0.2 partial_spectrum.3
  20.4 2.6 %collective-permute-start.1 = (bf16[128,256]{1,0:T(8,128)(2,1)S(1)}, bf16[128,256]{1,0:T(8,128)(2,1)S(1)}, u32[]{:S(2)}, u32[]{:S(2)}) collective-permute-start(bf16[128,256]{1,0:T(8,128)(2,1)S(1)} %partial_spectrum.3), channel_id=1, source_target_pairs={{0,8},{1,9},{2,10},{3,11},{4,12},{5,13},{6,14},{7,15},{8,0},{9,1},... | collective-permute-start | bytes 196616 | tf_op jit(solution)/shard_map/ppermute | solution.py:632
  23.7 0.0 copy-start.3
  23.7 0.0 copy-start.4
  23.7 0.8 %partial_spectrum.2.own_ref = f32[128,256]{1,0:T(8,128)S(1)} custom-call(s32[2]{0:T(128)S(1)} %pad_add_fusion.half_ref.place_ref, bf16[8,256,128]{2,1,0:T(8,128)(2,1)S(1)} %all-to-all-done.pencil_ref, bf16[1024,256]{1,0:T(8,128)(2,1)S(1)} %get-tuple-element.9.forward_ref), custom_call_target="tpu_custom_call" | custom-call | flops 67108864 | bytes 524288 | tf_op jit(solution)/shard_map/partial_spectrum/pallas_call | solution.py:327
  24.5 1.1 %collective-permute-done.1.other_ref = bf16[128,256]{1,0:T(8,128)(2,1)S(1)} collective-permute-done((bf16[128,256]{1,0:T(8,128)(2,1)S(1)}, bf16[128,256]{1,0:T(8,128)(2,1)S(1)}, u32[]{:S(2)}, u32[]{:S(2)}) %collective-permute-start.1) | collective-permute-done | bytes 65568 | tf_op jit(solution)/shard_map/ppermute | solution.py:632
  25.6 2.0 %mix.1 = bf16[32,64,128]{2,1,0:T(8,128)(2,1)} custom-call(s32[1]{0:T(128)S(6)} %sub.14.limit_ref, f32[128,256]{1,0:T(8,128)S(1)} %partial_spectrum.2.own_ref, bf16[128,256]{1,0:T(8,128)(2,1)S(1)} %collective-permute-done.1.other_ref, bf16[2,2,1024,128]{3,2,1,0:T(8,128)(2,1)S(1)} %get-tuple-element.10.weight_ref, ...), custom_call_target="tpu_custom_call" | custom-call | flops 134217728 | bytes 2097152 | tf_op jit(solution)/shard_map/mix/pallas_call | solution.py:419
  27.6 5.0 %all-to-all-start.1 = ((bf16[32,64,128]{2,1,0:T(8,128)(2,1)}), bf16[32,64,128]{2,1,0:T(8,128)(2,1)S(1)}, u32[]{:S(2)}, u32[]{:S(2)}) async-start(bf16[32,64,128]{2,1,0:T(8,128)(2,1)} %mix.1), calls=%async_computation.1 | async-start | bytes 1048576 | tf_op jit(solution)/shard_map/all_to_all | solution.py:635
  32.6 0.0 copy-done.3
  32.6 0.0 copy-done.4
  32.6 0.0 copy-start
  32.6 7.6 %pointwise.1.point_ref = bf16[2,8,128,512]{3,2,1,0:T(8,128)(2,1)S(1)} custom-call(s32[2]{0:T(128)S(1)} %pad_add_fusion.half_ref.place_ref, f32[64]{0:T(128)S(1)} %get-tuple-element.12.strength_ref, f32[32]{0:T(128)S(1)} %copy-done.4, bf16[32,32]{1,0:T(8,128)(2,1)S(1)} %copy-done.3, bf16[32,256,128]{2,1,0:T(8,128)(2,1)} %bitcast.25, bf16[256,128]{1,0:T(8,128)(2,1)} %bitcast.27), custom_call_target="tpu_custom_call" | custom-call | flops 2147483648 | bytes 8388608 | tf_op jit(solution)/shard_map/pointwise/pallas_call | solution.py:509
  40.3 7.9 %all-to-all-done.1.back_ref = bf16[32,64,128]{2,1,0:T(8,128)(2,1)S(1)} async-done(((bf16[32,64,128]{2,1,0:T(8,128)(2,1)}), bf16[32,64,128]{2,1,0:T(8,128)(2,1)S(1)}, u32[]{:S(2)}, u32[]{:S(2)}) %all-to-all-start.1) | async-done | bytes 524320 | tf_op jit(solution)/shard_map/all_to_all | solution.py:635
  48.2 0.0 copy-done
  48.2 2.6 %layer.1 = bf16[2,8,256,128]{3,2,1,0:T(8,128)(2,1)} custom-call(bf16[32,64,128]{2,1,0:T(8,128)(2,1)S(1)} %all-to-all-done.1.back_ref, bf16[128,512]{1,0:T(8,128)(2,1)S(1)} %copy-done, bf16[2,8,128,512]{3,2,1,0:T(8,128)(2,1)S(1)} %pointwise.1.point_ref), custom_call_target="tpu_custom_call" | custom-call | flops 268435456 | bytes 5242880 | tf_op jit(solution)/shard_map/layer/pallas_call | solution.py:570
Async XLA Ops:
  0.0 12.4 %copy-start.1 = (f32[16]{0:T(128)S(1)}, f32[16]{0:T(128)}, u32[]{:S(2)}) copy-start(f32[16]{0:T(128)} %amplitude_ref.1) | copy-start | bytes 196
  0.0 12.4 %copy-start.2 = (f32[32]{0:T(128)S(1)}, f32[32]{0:T(128)}, u32[]{:S(2)}) copy-start(f32[32]{0:T(128)} %load_ref.1) | copy-start | bytes 388
  4.8 15.3 %all-to-all-start = ((bf16[8,256,128]{2,1,0:T(8,128)(2,1)}), bf16[8,256,128]{2,1,0:T(8,128)(2,1)S(1)}, u32[]{:S(2)}, u32[]{:S(2)}) async-start(bf16[8,256,128]{2,1,0:T(8,128)(2,1)} %y_modes.1), calls=%async_computation | async-start | bytes 1048576 | tf_op jit(solution)/shard_map/all_to_all | solution.py:620
  11.0 1.4 %collective-permute-start = (s32[1,1]{1,0:T(1,128)}, s32[1,1]{1,0:T(1,128)}, u32[]{:S(2)}, u32[]{:S(2)}) collective-permute-start(s32[1,1]{1,0:T(1,128)} %bitcast.3), channel_id=1, source_target_pairs={{0,16},{16,0},{1,17},{17,1},{2,18},{18,2},{3,19},{19,3},{4,20},{20... | collective-permute-start | bytes 20 | tf_op jit(solution)/shard_map/ppermute | solution.py:617
  20.4 5.2 %collective-permute-start.1 = (bf16[128,256]{1,0:T(8,128)(2,1)S(1)}, bf16[128,256]{1,0:T(8,128)(2,1)S(1)}, u32[]{:S(2)}, u32[]{:S(2)}) collective-permute-start(bf16[128,256]{1,0:T(8,128)(2,1)S(1)} %partial_spectrum.3), channel_id=1, source_target_pairs={{0,8},{1,9},{2,10},{3,11},{4,12},{5,13},{6,14},{7,15},{8,0},{9,1},... | collective-permute-start | bytes 196616 | tf_op jit(solution)/shard_map/ppermute | solution.py:632
  23.7 8.9 %copy-start.3 = (bf16[32,32]{1,0:T(8,128)(2,1)S(1)}, bf16[32,32]{1,0:T(8,128)(2,1)}, u32[]{:S(2)}) copy-start(bf16[32,32]{1,0:T(8,128)(2,1)} %weight_ref.1) | copy-start | bytes 6148
  23.7 8.9 %copy-start.4 = (f32[32]{0:T(128)S(1)}, f32[32]{0:T(128)}, u32[]{:S(2)}) copy-start(f32[32]{0:T(128)} %bias_ref.1) | copy-start | bytes 388
  27.6 20.5 %all-to-all-start.1 = ((bf16[32,64,128]{2,1,0:T(8,128)(2,1)}), bf16[32,64,128]{2,1,0:T(8,128)(2,1)S(1)}, u32[]{:S(2)}, u32[]{:S(2)}) async-start(bf16[32,64,128]{2,1,0:T(8,128)(2,1)} %mix.1), calls=%async_computation.1 | async-start | bytes 1048576 | tf_op jit(solution)/shard_map/all_to_all | solution.py:635
  32.6 15.5 %copy-start = (bf16[128,512]{1,0:T(8,128)(2,1)S(1)}, bf16[128,512]{1,0:T(8,128)(2,1)}, u32[]{:S(2)}) copy-start(bf16[128,512]{1,0:T(8,128)(2,1)} %constant.39.clone.table_ref) | copy-start | bytes 393220

commit v5 on v4

--- a/solution.py
+++ b/solution.py
@@ -1,4 +1,5 @@
 import math
+import random
 
 import jax
 import jax.numpy as jnp
@@ -32,10 +33,16 @@
     return jnp.asarray(table.astype(BF16))
 
 
+def half_order(owners):
+    order = list(range(owners))
+    random.Random(4).shuffle(order)
+    return order
+
+
 def by_owner(table, slabs):
     modes, length = table.shape
     local = modes // slabs
-    return table.reshape(2, slabs // 2, local, length).transpose(1, 0, 2, 3)
+    return table.reshape(2, slabs // 2, local, length).transpose(1, 0, 2, 3)[half_order(slabs // 2)]
 
 
 def forward_y_table(modes_y, length_y, slabs):
@@ -56,7 +63,7 @@
 def forward_x_table(modes_x, length_x, slabs, planes):
     cos, sin = host_phases(first_frequencies(modes_x, length_x), np.arange(length_x), length_x)
     whole = np.array([[cos, -sin], [sin, cos]])
-    whole = whole.reshape(2, 2, modes_x, 2, slabs // 2, length_x // slabs)
+    whole = whole.reshape(2, 2, modes_x, 2, slabs // 2, length_x // slabs)[:, :, :, :, half_order(slabs // 2)]
     table = np.einsum("abqhsx,zw->hsazxwbq", whole, np.eye(planes, dtype=np.float32))
     return as_bf16(table.reshape(2, planes * length_x, planes * 2 * modes_x))
 
@@ -623,7 +630,7 @@
         split_axis=0,
         concat_axis=0,
         tiled=True,
-        axis_index_groups=[list(range(h * owners, (h + 1) * owners)) for h in range(2)],
+        axis_index_groups=[[h * owners + n for n in half_order(owners)] for h in range(2)],
     )
     strengths, weights, forward, inverse = prepare(
         place, index, other_index, amplitudes, load, spectral_weight.transpose(0, 2, 3, 4, 1), length_x, slabs, planes

time: 51.1 us -> 50.4 us (0.986)
  starting transfers between devices: 13.8 us -> 13.2 us
    all_to_all x1, starting transfers between devices: 4.96 us -> 3.8 us  [fast_local(): lax.all_to_all(back, ('slab', 'member'), split_axis=0, concat_axis=0, til...]
    all_to_all x1, waiting for transfers between devices: 2.6 us -> 1.84 us  [fast_local(): lax.all_to_all(packed, 'slab', split_axis=0, concat_axis=0, tiled=True, a...]
    ppermute x1, waiting for transfers between devices: 1.13 us -> 1.83 us  [fast_local(): other = lax.ppermute(leaving, 'slab', partners)]
    all_to_all x1, starting transfers between devices: 6.19 us -> 6.76 us  [fast_local(): lax.all_to_all(packed, 'slab', split_axis=0, concat_axis=0, tiled=True, a...]
where the time goes in v5:
time: 50.4 us; the launch traced here: 50 us
  Pallas kernels  22.4 us (44%)
  starting transfers between devices  13.2 us (26%)
  waiting for transfers between devices  12.9 us (26%)
  between operations  1.43 us (3%)
    all_to_all x1, waiting for transfers between devices, fast_local(): lax.all_to_all(back, ('slab', 'member'), split_axis=0, concat_axis=0, til...  7.9 us
    pallas_call x1, Pallas kernels, pointwise(): pl.pallas_call(pointwise_kernel, in_specs=[smem] * 3 + [vmem] * 3, out_sp...  7.61 us
    all_to_all x1, starting transfers between devices, fast_local(): lax.all_to_all(packed, 'slab', split_axis=0, concat_axis=0, tiled=True, a...  6.76 us
    pallas_call x1, Pallas kernels, prepare(): pl.pallas_call(prepare_kernel, in_specs=[smem] + [anywhere] * 2 + [smem]...  5.12 us
    pallas_call x1, Pallas kernels, y_modes(): pl.pallas_call(y_modes_kernel, in_specs=[anywhere] * (1 + len(operands)),...  4.13 us
    all_to_all x1, starting transfers between devices, fast_local(): lax.all_to_all(back, ('slab', 'member'), split_axis=0, concat_axis=0, til...  3.8 us
    ppermute x1, starting transfers between devices, fast_local(): other = lax.ppermute(leaving, 'slab', partners)  2.65 us
    pallas_call x1, Pallas kernels, layer(): pl.pallas_call(layer_kernel, in_specs=[vmem, vmem, vmem], out_specs=pl.Bl...  2.54 us
  transfers between devices with their start and end apart: 4, of which 4 were waited for; matrix products, arithmetic and copies ran while one was open for 0% of the time, Pallas kernels for 27%

profile of v5, /device:TPU:0, one launch (start us, length us, event | category | flops | bytes accessed | tf_op | source)
XLA Modules:
  0.0 50.0 jit_solution(7302757964639440737)
XLA Ops:
  0.0 0.0 copy-start.1
  0.0 0.0 copy-start.2
  0.7 4.1 %y_modes.1 = bf16[8,256,128]{2,1,0:T(8,128)(2,1)} custom-call(s32[1,1]{1,0:T(1,128)} %bitcast.21.index_any, f32[16]{0:T(128)} %amplitude_ref.1, f32[32]{0:T(128)} %load_ref.1, bf16[32,256,128]{2,1,0:T(8,128)(2,1)} %bitcast.24, bf16[256,128]{1,0:T(8,128)(2,1)} %bitcast.26, bf16[128,512]{1,0:T(8,128)(2,1)} %constant.36.clone.table_hbm), custom_call_target="tpu_custom_call" | custom-call | flops 268435456 | bytes 4194304 | tf_op jit(solution)/shard_map/y_modes/pallas_call | solution.py:221
  4.8 6.8 %all-to-all-start = ((bf16[8,256,128]{2,1,0:T(8,128)(2,1)}), bf16[8,256,128]{2,1,0:T(8,128)(2,1)S(1)}, u32[]{:S(2)}, u32[]{:S(2)}) async-start(bf16[8,256,128]{2,1,0:T(8,128)(2,1)} %y_modes.1), calls=%async_computation | async-start | bytes 1048576 | tf_op jit(solution)/shard_map/all_to_all | solution.py:627
  11.6 0.0 collective-permute-start
  11.6 0.1 pad_add_fusion.half_ref.place_ref
  11.7 1.3 %collective-permute-done.other_any = s32[1,1]{1,0:T(1,128)} collective-permute-done((s32[1,1]{1,0:T(1,128)}, s32[1,1]{1,0:T(1,128)}, u32[]{:S(2)}, u32[]{:S(2)}) %collective-permute-start) | collective-permute-done | bytes 36 | tf_op jit(solution)/shard_map/ppermute | solution.py:624
  13.0 0.0 copy-done.1
  13.0 0.0 copy-done.2
  13.0 5.1 %prepare.1 = (f32[64]{0:T(128)S(1)}, bf16[2,2,1024,128]{3,2,1,0:T(8,128)(2,1)S(1)}, bf16[1024,256]{1,0:T(8,128)(2,1)S(1)}, bf16[256,1024]{1,0:T(8,128)(2,1)S(1)}) custom-call(s32[2]{0:T(128)S(1)} %pad_add_fusion.half_ref.place_ref, s32[1,1]{1,0:T(1,128)} %bitcast.22.own_any, s32[1,1]{1,0:T(1,128)} %collective-permute-done.other_any, f32[16]{0:T(128)S(1)} %copy-done.1, ...), custom_call_target="tpu_custom_call" | custom-call | flops 2097152 | bytes 5242880 | tf_op jit(solution)/shard_map/prepare/pallas_call | solution.py:298
  18.1 1.8 %all-to-all-done.pencil_ref = bf16[8,256,128]{2,1,0:T(8,128)(2,1)S(1)} async-done(((bf16[8,256,128]{2,1,0:T(8,128)(2,1)}), bf16[8,256,128]{2,1,0:T(8,128)(2,1)S(1)}, u32[]{:S(2)}, u32[]{:S(2)}) %all-to-all-start) | async-done | bytes 524320 | tf_op jit(solution)/shard_map/all_to_all | solution.py:627
  19.9 0.2 partial_spectrum.3
  20.2 2.6 %collective-permute-start.1 = (bf16[128,256]{1,0:T(8,128)(2,1)S(1)}, bf16[128,256]{1,0:T(8,128)(2,1)S(1)}, u32[]{:S(2)}, u32[]{:S(2)}) collective-permute-start(bf16[128,256]{1,0:T(8,128)(2,1)S(1)} %partial_spectrum.3), channel_id=1, source_target_pairs={{0,8},{1,9},{2,10},{3,11},{4,12},{5,13},{6,14},{7,15},{8,0},{9,1},... | collective-permute-start | bytes 196616 | tf_op jit(solution)/shard_map/ppermute | solution.py:639
  23.5 0.0 copy-start.3
  23.5 0.0 copy-start.4
  23.5 0.8 %partial_spectrum.2.own_ref = f32[128,256]{1,0:T(8,128)S(1)} custom-call(s32[2]{0:T(128)S(1)} %pad_add_fusion.half_ref.place_ref, bf16[8,256,128]{2,1,0:T(8,128)(2,1)S(1)} %all-to-all-done.pencil_ref, bf16[1024,256]{1,0:T(8,128)(2,1)S(1)} %get-tuple-element.9.forward_ref), custom_call_target="tpu_custom_call" | custom-call | flops 67108864 | bytes 524288 | tf_op jit(solution)/shard_map/partial_spectrum/pallas_call | solution.py:334
  24.3 1.8 %collective-permute-done.1.other_ref = bf16[128,256]{1,0:T(8,128)(2,1)S(1)} collective-permute-done((bf16[128,256]{1,0:T(8,128)(2,1)S(1)}, bf16[128,256]{1,0:T(8,128)(2,1)S(1)}, u32[]{:S(2)}, u32[]{:S(2)}) %collective-permute-start.1) | collective-permute-done | bytes 65568 | tf_op jit(solution)/shard_map/ppermute | solution.py:639
  26.1 2.0 %mix.1 = bf16[32,64,128]{2,1,0:T(8,128)(2,1)} custom-call(s32[1]{0:T(128)S(6)} %sub.14.limit_ref, f32[128,256]{1,0:T(8,128)S(1)} %partial_spectrum.2.own_ref, bf16[128,256]{1,0:T(8,128)(2,1)S(1)} %collective-permute-done.1.other_ref, bf16[2,2,1024,128]{3,2,1,0:T(8,128)(2,1)S(1)} %get-tuple-element.10.weight_ref, ...), custom_call_target="tpu_custom_call" | custom-call | flops 134217728 | bytes 2097152 | tf_op jit(solution)/shard_map/mix/pallas_call | solution.py:426
  28.1 3.8 %all-to-all-start.1 = ((bf16[32,64,128]{2,1,0:T(8,128)(2,1)}), bf16[32,64,128]{2,1,0:T(8,128)(2,1)S(1)}, u32[]{:S(2)}, u32[]{:S(2)}) async-start(bf16[32,64,128]{2,1,0:T(8,128)(2,1)} %mix.1), calls=%async_computation.1 | async-start | bytes 1048576 | tf_op jit(solution)/shard_map/all_to_all | solution.py:642
  31.9 0.0 copy-done.3
  32.0 0.0 copy-done.4
  32.0 0.0 copy-start
  32.0 7.6 %pointwise.1.point_ref = bf16[2,8,128,512]{3,2,1,0:T(8,128)(2,1)S(1)} custom-call(s32[2]{0:T(128)S(1)} %pad_add_fusion.half_ref.place_ref, f32[64]{0:T(128)S(1)} %get-tuple-element.12.strength_ref, f32[32]{0:T(128)S(1)} %copy-done.4, bf16[32,32]{1,0:T(8,128)(2,1)S(1)} %copy-done.3, bf16[32,256,128]{2,1,0:T(8,128)(2,1)} %bitcast.25, bf16[256,128]{1,0:T(8,128)(2,1)} %bitcast.27), custom_call_target="tpu_custom_call" | custom-call | flops 2147483648 | bytes 8388608 | tf_op jit(solution)/shard_map/pointwise/pallas_call | solution.py:516
  39.6 7.9 %all-to-all-done.1.back_ref = bf16[32,64,128]{2,1,0:T(8,128)(2,1)S(1)} async-done(((bf16[32,64,128]{2,1,0:T(8,128)(2,1)}), bf16[32,64,128]{2,1,0:T(8,128)(2,1)S(1)}, u32[]{:S(2)}, u32[]{:S(2)}) %all-to-all-start.1) | async-done | bytes 524320 | tf_op jit(solution)/shard_map/all_to_all | solution.py:642
  47.5 0.0 copy-done
  47.5 2.5 %layer.1 = bf16[2,8,256,128]{3,2,1,0:T(8,128)(2,1)} custom-call(bf16[32,64,128]{2,1,0:T(8,128)(2,1)S(1)} %all-to-all-done.1.back_ref, bf16[128,512]{1,0:T(8,128)(2,1)S(1)} %copy-done, bf16[2,8,128,512]{3,2,1,0:T(8,128)(2,1)S(1)} %pointwise.1.point_ref), custom_call_target="tpu_custom_call" | custom-call | flops 268435456 | bytes 5242880 | tf_op jit(solution)/shard_map/layer/pallas_call | solution.py:577
Async XLA Ops:
  0.0 13.0 %copy-start.1 = (f32[16]{0:T(128)S(1)}, f32[16]{0:T(128)}, u32[]{:S(2)}) copy-start(f32[16]{0:T(128)} %amplitude_ref.1) | copy-start | bytes 196
  0.0 13.0 %copy-start.2 = (f32[32]{0:T(128)S(1)}, f32[32]{0:T(128)}, u32[]{:S(2)}) copy-start(f32[32]{0:T(128)} %load_ref.1) | copy-start | bytes 388
  4.8 15.1 %all-to-all-start = ((bf16[8,256,128]{2,1,0:T(8,128)(2,1)}), bf16[8,256,128]{2,1,0:T(8,128)(2,1)S(1)}, u32[]{:S(2)}, u32[]{:S(2)}) async-start(bf16[8,256,128]{2,1,0:T(8,128)(2,1)} %y_modes.1), calls=%async_computation | async-start | bytes 1048576 | tf_op jit(solution)/shard_map/all_to_all | solution.py:627
  11.6 1.4 %collective-permute-start = (s32[1,1]{1,0:T(1,128)}, s32[1,1]{1,0:T(1,128)}, u32[]{:S(2)}, u32[]{:S(2)}) collective-permute-start(s32[1,1]{1,0:T(1,128)} %bitcast.3), channel_id=1, source_target_pairs={{0,16},{16,0},{1,17},{17,1},{2,18},{18,2},{3,19},{19,3},{4,20},{20... | collective-permute-start | bytes 20 | tf_op jit(solution)/shard_map/ppermute | solution.py:624
  20.2 5.9 %collective-permute-start.1 = (bf16[128,256]{1,0:T(8,128)(2,1)S(1)}, bf16[128,256]{1,0:T(8,128)(2,1)S(1)}, u32[]{:S(2)}, u32[]{:S(2)}) collective-permute-start(bf16[128,256]{1,0:T(8,128)(2,1)S(1)} %partial_spectrum.3), channel_id=1, source_target_pairs={{0,8},{1,9},{2,10},{3,11},{4,12},{5,13},{6,14},{7,15},{8,0},{9,1},... | collective-permute-start | bytes 196616 | tf_op jit(solution)/shard_map/ppermute | solution.py:639
  23.5 8.5 %copy-start.3 = (bf16[32,32]{1,0:T(8,128)(2,1)S(1)}, bf16[32,32]{1,0:T(8,128)(2,1)}, u32[]{:S(2)}) copy-start(bf16[32,32]{1,0:T(8,128)(2,1)} %weight_ref.1) | copy-start | bytes 6148
  23.5 8.5 %copy-start.4 = (f32[32]{0:T(128)S(1)}, f32[32]{0:T(128)}, u32[]{:S(2)}) copy-start(f32[32]{0:T(128)} %bias_ref.1) | copy-start | bytes 388
  28.1 19.4 %all-to-all-start.1 = ((bf16[32,64,128]{2,1,0:T(8,128)(2,1)}), bf16[32,64,128]{2,1,0:T(8,128)(2,1)S(1)}, u32[]{:S(2)}, u32[]{:S(2)}) async-start(bf16[32,64,128]{2,1,0:T(8,128)(2,1)} %mix.1), calls=%async_computation.1 | async-start | bytes 1048576 | tf_op jit(solution)/shard_map/all_to_all | solution.py:642
  32.0 15.5 %copy-start = (bf16[128,512]{1,0:T(8,128)(2,1)S(1)}, bf16[128,512]{1,0:T(8,128)(2,1)}, u32[]{:S(2)}) copy-start(bf16[128,512]{1,0:T(8,128)(2,1)} %constant.39.clone.table_ref) | copy-start | bytes 393220

commit v6 on v5

--- a/solution.py
+++ b/solution.py
@@ -396,18 +396,18 @@
                     )
     left = jnp.concatenate([mixed[z].astype(BF16) for z in range(planes)], axis=1)
     members = groups // 2
-    wide = 2 * LANES
     leaving = []
-    for t in range(inverse_ref.shape[1] // wide):
-        back = jnp.dot(left, inverse_ref[:, t * wide : (t + 1) * wide], preferred_element_type=F32)
-        for u in range(2):
-            tile = slice(u * LANES, (u + 1) * LANES)
-            for h in range(members):
-                start = 2 * h * block
-                pair = pair_halves(back[start : start + block, tile], back[start + block : start + 2 * block, tile])
-                for n in range(2):
-                    packed[(4 * t + 2 * u + n) * members + h] = pair[n].astype(BF16)
-        blocks = pl.ds(4 * t * members, 4 * members)
+    for t in range(inverse_ref.shape[1] // LANES):
+        if t % 2 == 0:
+            pair_of = slice(t * LANES, (t + 2) * LANES)
+            wide = jnp.dot(left, inverse_ref[:, pair_of], preferred_element_type=F32)
+        back = wide[:, (t % 2) * LANES : (t % 2 + 1) * LANES]
+        for h in range(members):
+            start = 2 * h * block
+            pair = pair_halves(back[start : start + block], back[start + block : start + 2 * block])
+            for n in range(2):
+                packed[(2 * t + n) * members + h] = pair[n].astype(BF16)
+        blocks = pl.ds(2 * t * members, 2 * members)
         copy = pltpu.make_async_copy(packed.at[blocks], out_hbm.at[blocks], sent.at[t])
         copy.start()
         leaving.append(copy)
@@ -432,7 +432,7 @@
             pltpu.VMEM((pairs, planes, 2, channels, width), F32),
             pltpu.VMEM((planes, rows, width), F32),
             pltpu.VMEM(blocks, BF16),
-            pltpu.SemaphoreType.DMA((slabs // 4,)),
+            pltpu.SemaphoreType.DMA((slabs // 2,)),
         ],
         compiler_params=pltpu.CompilerParams(vmem_limit_bytes=8 * 1024 * 1024),
         cost_estimate=pl.CostEstimate(

time: 50.4 us -> 50.4 us (level)
  no operation moved by 1% of the time
where the time goes in v6:
time: 50.4 us; the launch traced here: 50 us
  Pallas kernels  22.4 us (44%)
  starting transfers between devices  13.2 us (26%)
  waiting for transfers between devices  12.9 us (26%)
  between operations  1.43 us (3%)
    all_to_all x1, waiting for transfers between devices, fast_local(): lax.all_to_all(back, ('slab', 'member'), split_axis=0, concat_axis=0, til...  7.9 us
    pallas_call x1, Pallas kernels, pointwise(): pl.pallas_call(pointwise_kernel, in_specs=[smem] * 3 + [vmem] * 3, out_sp...  7.61 us
    all_to_all x1, starting transfers between devices, fast_local(): lax.all_to_all(packed, 'slab', split_axis=0, concat_axis=0, tiled=True, a...  6.76 us
    pallas_call x1, Pallas kernels, prepare(): pl.pallas_call(prepare_kernel, in_specs=[smem] + [anywhere] * 2 + [smem]...  5.12 us
    pallas_call x1, Pallas kernels, y_modes(): pl.pallas_call(y_modes_kernel, in_specs=[anywhere] * (1 + len(operands)),...  4.13 us
    all_to_all x1, starting transfers between devices, fast_local(): lax.all_to_all(back, ('slab', 'member'), split_axis=0, concat_axis=0, til...  3.81 us
    ppermute x1, starting transfers between devices, fast_local(): other = lax.ppermute(leaving, 'slab', partners)  2.65 us
    pallas_call x1, Pallas kernels, layer(): pl.pallas_call(layer_kernel, in_specs=[vmem, vmem, vmem], out_specs=pl.Bl...  2.54 us
  transfers between devices with their start and end apart: 4, of which 4 were waited for; matrix products, arithmetic and copies ran while one was open for 0% of the time, Pallas kernels for 27%

profile of v6, /device:TPU:0, one launch (start us, length us, event | category | flops | bytes accessed | tf_op | source)
XLA Modules:
  0.0 50.0 jit_solution(14417537604673086116)
XLA Ops:
  0.0 0.0 copy-start.1
  0.0 0.0 copy-start.2
  0.7 4.1 %y_modes.1 = bf16[8,256,128]{2,1,0:T(8,128)(2,1)} custom-call(s32[1,1]{1,0:T(1,128)} %bitcast.21.index_any, f32[16]{0:T(128)} %amplitude_ref.1, f32[32]{0:T(128)} %load_ref.1, bf16[32,256,128]{2,1,0:T(8,128)(2,1)} %bitcast.24, bf16[256,128]{1,0:T(8,128)(2,1)} %bitcast.26, bf16[128,512]{1,0:T(8,128)(2,1)} %constant.36.clone.table_hbm), custom_call_target="tpu_custom_call" | custom-call | flops 268435456 | bytes 4194304 | tf_op jit(solution)/shard_map/y_modes/pallas_call | solution.py:221
  4.8 6.8 %all-to-all-start = ((bf16[8,256,128]{2,1,0:T(8,128)(2,1)}), bf16[8,256,128]{2,1,0:T(8,128)(2,1)S(1)}, u32[]{:S(2)}, u32[]{:S(2)}) async-start(bf16[8,256,128]{2,1,0:T(8,128)(2,1)} %y_modes.1), calls=%async_computation | async-start | bytes 1048576 | tf_op jit(solution)/shard_map/all_to_all | solution.py:627
  11.6 0.0 collective-permute-start
  11.6 0.1 pad_add_fusion.half_ref.place_ref
  11.7 1.3 %collective-permute-done.other_any = s32[1,1]{1,0:T(1,128)} collective-permute-done((s32[1,1]{1,0:T(1,128)}, s32[1,1]{1,0:T(1,128)}, u32[]{:S(2)}, u32[]{:S(2)}) %collective-permute-start) | collective-permute-done | bytes 36 | tf_op jit(solution)/shard_map/ppermute | solution.py:624
  13.0 0.0 copy-done.1
  13.0 0.0 copy-done.2
  13.0 5.1 %prepare.1 = (f32[64]{0:T(128)S(1)}, bf16[2,2,1024,128]{3,2,1,0:T(8,128)(2,1)S(1)}, bf16[1024,256]{1,0:T(8,128)(2,1)S(1)}, bf16[256,1024]{1,0:T(8,128)(2,1)S(1)}) custom-call(s32[2]{0:T(128)S(1)} %pad_add_fusion.half_ref.place_ref, s32[1,1]{1,0:T(1,128)} %bitcast.22.own_any, s32[1,1]{1,0:T(1,128)} %collective-permute-done.other_any, f32[16]{0:T(128)S(1)} %copy-done.1, ...), custom_call_target="tpu_custom_call" | custom-call | flops 2097152 | bytes 5242880 | tf_op jit(solution)/shard_map/prepare/pallas_call | solution.py:298
  18.1 1.8 %all-to-all-done.pencil_ref = bf16[8,256,128]{2,1,0:T(8,128)(2,1)S(1)} async-done(((bf16[8,256,128]{2,1,0:T(8,128)(2,1)}), bf16[8,256,128]{2,1,0:T(8,128)(2,1)S(1)}, u32[]{:S(2)}, u32[]{:S(2)}) %all-to-all-start) | async-done | bytes 524320 | tf_op jit(solution)/shard_map/all_to_all | solution.py:627
  19.9 0.2 partial_spectrum.3
  20.2 2.6 %collective-permute-start.1 = (bf16[128,256]{1,0:T(8,128)(2,1)S(1)}, bf16[128,256]{1,0:T(8,128)(2,1)S(1)}, u32[]{:S(2)}, u32[]{:S(2)}) collective-permute-start(bf16[128,256]{1,0:T(8,128)(2,1)S(1)} %partial_spectrum.3), channel_id=1, source_target_pairs={{0,8},{1,9},{2,10},{3,11},{4,12},{5,13},{6,14},{7,15},{8,0},{9,1},... | collective-permute-start | bytes 196616 | tf_op jit(solution)/shard_map/ppermute | solution.py:639
  23.5 0.0 copy-start.3
  23.5 0.0 copy-start.4
  23.5 0.8 %partial_spectrum.2.own_ref = f32[128,256]{1,0:T(8,128)S(1)} custom-call(s32[2]{0:T(128)S(1)} %pad_add_fusion.half_ref.place_ref, bf16[8,256,128]{2,1,0:T(8,128)(2,1)S(1)} %all-to-all-done.pencil_ref, bf16[1024,256]{1,0:T(8,128)(2,1)S(1)} %get-tuple-element.9.forward_ref), custom_call_target="tpu_custom_call" | custom-call | flops 67108864 | bytes 524288 | tf_op jit(solution)/shard_map/partial_spectrum/pallas_call | solution.py:334
  24.3 1.8 %collective-permute-done.1.other_ref = bf16[128,256]{1,0:T(8,128)(2,1)S(1)} collective-permute-done((bf16[128,256]{1,0:T(8,128)(2,1)S(1)}, bf16[128,256]{1,0:T(8,128)(2,1)S(1)}, u32[]{:S(2)}, u32[]{:S(2)}) %collective-permute-start.1) | collective-permute-done | bytes 65568 | tf_op jit(solution)/shard_map/ppermute | solution.py:639
  26.1 2.0 %mix.1 = bf16[32,64,128]{2,1,0:T(8,128)(2,1)} custom-call(s32[1]{0:T(128)S(6)} %sub.14.limit_ref, f32[128,256]{1,0:T(8,128)S(1)} %partial_spectrum.2.own_ref, bf16[128,256]{1,0:T(8,128)(2,1)S(1)} %collective-permute-done.1.other_ref, bf16[2,2,1024,128]{3,2,1,0:T(8,128)(2,1)S(1)} %get-tuple-element.10.weight_ref, ...), custom_call_target="tpu_custom_call" | custom-call | flops 134217728 | bytes 2097152 | tf_op jit(solution)/shard_map/mix/pallas_call | solution.py:426
  28.1 3.8 %all-to-all-start.1 = ((bf16[32,64,128]{2,1,0:T(8,128)(2,1)}), bf16[32,64,128]{2,1,0:T(8,128)(2,1)S(1)}, u32[]{:S(2)}, u32[]{:S(2)}) async-start(bf16[32,64,128]{2,1,0:T(8,128)(2,1)} %mix.1), calls=%async_computation.1 | async-start | bytes 1048576 | tf_op jit(solution)/shard_map/all_to_all | solution.py:642
  32.0 0.0 copy-done.3
  32.0 0.0 copy-done.4
  32.0 0.0 copy-start
  32.0 7.6 %pointwise.1.point_ref = bf16[2,8,128,512]{3,2,1,0:T(8,128)(2,1)S(1)} custom-call(s32[2]{0:T(128)S(1)} %pad_add_fusion.half_ref.place_ref, f32[64]{0:T(128)S(1)} %get-tuple-element.12.strength_ref, f32[32]{0:T(128)S(1)} %copy-done.4, bf16[32,32]{1,0:T(8,128)(2,1)S(1)} %copy-done.3, bf16[32,256,128]{2,1,0:T(8,128)(2,1)} %bitcast.25, bf16[256,128]{1,0:T(8,128)(2,1)} %bitcast.27), custom_call_target="tpu_custom_call" | custom-call | flops 2147483648 | bytes 8388608 | tf_op jit(solution)/shard_map/pointwise/pallas_call | solution.py:516
  39.6 7.9 %all-to-all-done.1.back_ref = bf16[32,64,128]{2,1,0:T(8,128)(2,1)S(1)} async-done(((bf16[32,64,128]{2,1,0:T(8,128)(2,1)}), bf16[32,64,128]{2,1,0:T(8,128)(2,1)S(1)}, u32[]{:S(2)}, u32[]{:S(2)}) %all-to-all-start.1) | async-done | bytes 524320 | tf_op jit(solution)/shard_map/all_to_all | solution.py:642
  47.5 0.0 copy-done
  47.5 2.5 %layer.1 = bf16[2,8,256,128]{3,2,1,0:T(8,128)(2,1)} custom-call(bf16[32,64,128]{2,1,0:T(8,128)(2,1)S(1)} %all-to-all-done.1.back_ref, bf16[128,512]{1,0:T(8,128)(2,1)S(1)} %copy-done, bf16[2,8,128,512]{3,2,1,0:T(8,128)(2,1)S(1)} %pointwise.1.point_ref), custom_call_target="tpu_custom_call" | custom-call | flops 268435456 | bytes 5242880 | tf_op jit(solution)/shard_map/layer/pallas_call | solution.py:577
Async XLA Ops:
  0.0 13.0 %copy-start.1 = (f32[16]{0:T(128)S(1)}, f32[16]{0:T(128)}, u32[]{:S(2)}) copy-start(f32[16]{0:T(128)} %amplitude_ref.1) | copy-start | bytes 196
  0.0 13.0 %copy-start.2 = (f32[32]{0:T(128)S(1)}, f32[32]{0:T(128)}, u32[]{:S(2)}) copy-start(f32[32]{0:T(128)} %load_ref.1) | copy-start | bytes 388
  4.8 15.1 %all-to-all-start = ((bf16[8,256,128]{2,1,0:T(8,128)(2,1)}), bf16[8,256,128]{2,1,0:T(8,128)(2,1)S(1)}, u32[]{:S(2)}, u32[]{:S(2)}) async-start(bf16[8,256,128]{2,1,0:T(8,128)(2,1)} %y_modes.1), calls=%async_computation | async-start | bytes 1048576 | tf_op jit(solution)/shard_map/all_to_all | solution.py:627
  11.6 1.4 %collective-permute-start = (s32[1,1]{1,0:T(1,128)}, s32[1,1]{1,0:T(1,128)}, u32[]{:S(2)}, u32[]{:S(2)}) collective-permute-start(s32[1,1]{1,0:T(1,128)} %bitcast.3), channel_id=1, source_target_pairs={{0,16},{16,0},{1,17},{17,1},{2,18},{18,2},{3,19},{19,3},{4,20},{20... | collective-permute-start | bytes 20 | tf_op jit(solution)/shard_map/ppermute | solution.py:624
  20.2 5.9 %collective-permute-start.1 = (bf16[128,256]{1,0:T(8,128)(2,1)S(1)}, bf16[128,256]{1,0:T(8,128)(2,1)S(1)}, u32[]{:S(2)}, u32[]{:S(2)}) collective-permute-start(bf16[128,256]{1,0:T(8,128)(2,1)S(1)} %partial_spectrum.3), channel_id=1, source_target_pairs={{0,8},{1,9},{2,10},{3,11},{4,12},{5,13},{6,14},{7,15},{8,0},{9,1},... | collective-permute-start | bytes 196616 | tf_op jit(solution)/shard_map/ppermute | solution.py:639
  23.5 8.5 %copy-start.3 = (bf16[32,32]{1,0:T(8,128)(2,1)S(1)}, bf16[32,32]{1,0:T(8,128)(2,1)}, u32[]{:S(2)}) copy-start(bf16[32,32]{1,0:T(8,128)(2,1)} %weight_ref.1) | copy-start | bytes 6148
  23.5 8.5 %copy-start.4 = (f32[32]{0:T(128)S(1)}, f32[32]{0:T(128)}, u32[]{:S(2)}) copy-start(f32[32]{0:T(128)} %bias_ref.1) | copy-start | bytes 388
  28.1 19.4 %all-to-all-start.1 = ((bf16[32,64,128]{2,1,0:T(8,128)(2,1)}), bf16[32,64,128]{2,1,0:T(8,128)(2,1)S(1)}, u32[]{:S(2)}, u32[]{:S(2)}) async-start(bf16[32,64,128]{2,1,0:T(8,128)(2,1)} %mix.1), calls=%async_computation.1 | async-start | bytes 1048576 | tf_op jit(solution)/shard_map/all_to_all | solution.py:642
  32.0 15.5 %copy-start = (bf16[128,512]{1,0:T(8,128)(2,1)S(1)}, bf16[128,512]{1,0:T(8,128)(2,1)}, u32[]{:S(2)}) copy-start(bf16[128,512]{1,0:T(8,128)(2,1)} %constant.39.clone.table_ref) | copy-start | bytes 393220
